TPU v7x, 32 devices: a whole 2x2x4 slice. The times are simulated.
32 devices in a mesh: groups: 2 (over x), row: 16 (over z, y, core).
Axes of the slice: x: 2, y: 2, z: 4, core: 2. Of those that a mesh axis runs over, the one named last changes fastest.
Arguments:
- density: bfloat16 [512, 7, 128, 128], P(('groups', 'row')), parts along dimension 0, may hold values from -0.625 to 0.625
- block_cols: int32 [512, 7], P(('groups', 'row')), parts along dimension 0, may hold values from -1 to 255, as said below
Outputs:
- transposed: bfloat16 [512, 7, 128, 128], P(('groups', 'row')), parts along dimension 0
There are 2 independent parts, one for each index of `groups`. A program takes and returns all parts, laid end to end along the dimension named above; each array names one. Nothing has to cross between parts.
Inputs may be any that keep to these rules, and one draw needn't show every extreme that they name: `block_cols`: block row i stands for the block at (i % 8, (i // 8) % 8, i // 64) of a grid of blocks. Its slots list, in this order, the columns i - 64, i - 8, i - 1, i, i + 1, i + 8, i + 64; slot 3 always holds i, and a neighbour slot holds -1 where that neighbour lies outside the grid or its pair is not kept. The pattern is symmetric: j is listed in row i exactly when i is listed in row j. Some row uses all 7 slots.
All inputs are finite; a program needn't handle non-finite values.
Results may differ from a plain program's by a relative error of at most 0.0051.
Values may be sent and summed in bfloat16 or wider, within the bound.
No kernel may reach another device: no remote copies, remote signals or barrier semaphores. Data moves between devices by JAX's collectives and lax.ppermute only.
A program may use at most 128 MiB of HBM per device.

v0:
```python
import jax
import jax.numpy as jnp
from jax import lax
from jax.sharding import PartitionSpec as P

K = 7
GX = 8
PLANE = 64


def shifted(value, axis, steps):
    count = lax.axis_size(axis)
    leading, last = (max(0, -steps), min(count, count - steps))
    return lax.ppermute(value, axis, [(source, source + steps) for source in range(leading, last)])


def stencil_offsets():
    return [-PLANE, -GX, -1, 0, 1, GX, PLANE]


def slot_triples():
    offsets = stencil_offsets()
    triples = []
    for left_slot in range(K):
        for out_slot in range(K):
            step = offsets[out_slot] - offsets[left_slot]
            if step in offsets:
                triples.append((left_slot, out_slot, offsets.index(step)))
    return triples


def neighbour_views(blocks, cols):
    row_count = blocks.shape[0]
    layer_dist = PLANE // row_count
    low_b, low_c = shifted((blocks, cols), "row", 1)
    high_b, high_c = shifted((blocks, cols), "row", -1)
    far_low_b, far_low_c = shifted((blocks, cols), "row", layer_dist)
    far_high_b, far_high_c = shifted((blocks, cols), "row", -layer_dist)
    near_blocks = jnp.concatenate([low_b, blocks, high_b], axis=0)
    near_cols = jnp.concatenate([low_c, cols, high_c], axis=0)
    views = {}
    for offset in stencil_offsets():
        if offset == PLANE:
            views[offset] = (far_high_b, far_high_c)
        elif offset == -PLANE:
            views[offset] = (far_low_b, far_low_c)
        else:
            start = row_count + offset
            views[offset] = (
                near_blocks[start : start + row_count],
                near_cols[start : start + row_count],
            )
    return views


def block_product(left_blocks, cols, views):
    offsets = stencil_offsets()
    in_use = cols >= 0
    totals = [None] * K
    for left_slot, out_slot, right_slot in slot_triples():
        view_b, view_c = views[offsets[left_slot]]
        keep = (
            in_use[:, left_slot]
            & in_use[:, out_slot]
            & (view_c[:, right_slot] == cols[:, out_slot])
        )
        product = jnp.einsum(
            "imr,irn->imn",
            left_blocks[:, left_slot],
            view_b[:, right_slot],
            preferred_element_type=jnp.float32,
        )
        term = jnp.where(keep[:, None, None], product, jnp.zeros_like(product))
        totals[out_slot] = term if totals[out_slot] is None else totals[out_slot] + term
    return jnp.stack(totals, axis=1)


def on_device(density, block_cols):
    row_count = density.shape[0]
    first_row = lax.axis_index("row") * row_count
    views = neighbour_views(density, block_cols)
    square = block_product(density, block_cols, views).astype(jnp.bfloat16)
    cube_part = block_product(square, block_cols, views)
    purified = (3.0 * square.astype(jnp.float32) - 2.0 * cube_part).astype(jnp.bfloat16)
    new_views = neighbour_views(purified, block_cols)
    column_ids = first_row + jnp.arange(row_count, dtype=jnp.int32)
    offsets = stencil_offsets()
    pieces = []
    for slot in range(K):
        view_b, view_c = new_views[offsets[slot]]
        keep = (block_cols[:, slot] >= 0) & (view_c[:, K - 1 - slot] == column_ids)
        flipped_one = jnp.swapaxes(view_b[:, K - 1 - slot], 1, 2)
        pieces.append(jnp.where(keep[:, None, None], flipped_one, jnp.zeros_like(flipped_one)))
    return jnp.stack(pieces, axis=1)


def solution(mesh):
    placed = (P(("groups", "row"), None, None, None), P(("groups", "row"), None))
    return jax.shard_map(
        on_device,
        mesh=mesh,
        in_specs=placed,
        out_specs=P(("groups", "row"), None, None, None),
        check_vma=False,
    )
```

profile of v0, /device:TPU:0, one launch (start us, length us, event | category | flops | bytes accessed | tf_op | source)
XLA Modules:
  0.0 384.0 jit_solution(13013065933677431279)
XLA Ops:
  0.0 6.1 %copy.6 = bf16[16,7,128,128]{2,3,0,1:T(8,128)(2,1)} copy(bf16[16,7,128,128]{3,2,1,0:T(8,128)(2,1)} %param.2) | data formatting | bytes 7340032 | tf_op args[0]
  6.1 4.2 %collective-permute-start.3 = (bf16[16,7,128,128]{2,3,0,1:T(8,128)(2,1)}, bf16[16,7,128,128]{2,3,0,1:T(8,128)(2,1)}, u32[]{:S(2)}, u32[]{:S(2)}) collective-permute-start(bf16[16,7,128,128]{2,3,0,1:T(8,128)(2,1)} %copy.6), channel_id=1, source_target_pairs={{0,1},{1,2},{2,3},{3,4},{4,5},{5,6},{6,7},{7,8},{8,9},{9,10},{10,1... | collective-permute-start | bytes 11010056 | tf_op jit(solution)/shard_map/ppermute | solution.py:14
  11.5 3.4 collective-permute-start.2
  16.2 4.3 %copy.3 = bf16[16,7,128,128]{3,2,0,1:T(8,128)(2,1)} copy(bf16[16,7,128,128]{3,2,1,0:T(8,128)(2,1)} %param.2) | data formatting | bytes 7340032 | tf_op args[0]
  20.5 9.6 %collective-permute-start.1 = (bf16[16,7,128,128]{3,2,0,1:T(8,128)(2,1)}, bf16[16,7,128,128]{3,2,0,1:T(8,128)(2,1)}, u32[]{:S(2)}, u32[]{:S(2)}) collective-permute-start(bf16[16,7,128,128]{3,2,0,1:T(8,128)(2,1)} %copy.3), channel_id=1, source_target_pairs={{0,4},{1,5},{2,6},{3,7},{4,8},{5,9},{6,10},{7,11},{8,12},{9,13},{1... | collective-permute-start | bytes 11010056 | tf_op jit(solution)/shard_map/ppermute | solution.py:14
  30.2 49.4 %collective-permute-start = (s32[16,7]{0,1:T(8,128)S(1)}, s32[16,7]{0,1:T(8,128)S(1)}, u32[]{:S(2)}, u32[]{:S(2)}) collective-permute-start(s32[16,7]{0,1:T(8,128)S(1)} %copy-done.23), channel_id=1, source_target_pairs={{0,4},{1,5},{2,6},{3,7},{4,8},{5,9},{6,10},{7,11},{8,12},{9,13},{1... | collective-permute-start | bytes 1352 | tf_op jit(solution)/shard_map/ppermute | solution.py:14
  81.0 24.5 %collective-permute-done = s32[16,7]{0,1:T(8,128)S(1)} collective-permute-done((s32[16,7]{0,1:T(8,128)S(1)}, s32[16,7]{0,1:T(8,128)S(1)}, u32[]{:S(2)}, u32[]{:S(2)}) %collective-permute-start) | collective-permute-done | bytes 480 | tf_op jit(solution)/shard_map/ppermute | solution.py:14
  108.5 2.5 convolution_select_fusion.34
  111.0 2.7 convolution_select_fusion.32
  113.7 2.7 convolution_select_fusion.30
  116.4 2.6 convolution_select_fusion.23
  119.0 2.5 convolution_select_fusion.21
  121.5 2.5 convolution_select_fusion.19
  124.0 2.7 maximum_bitcast_fusion.2
  130.1 2.5 fusion.13
  132.5 2.6 copy.21
  138.2 48.7 %collective-permute-done.7 = bf16[16,7,128,128]{3,2,0,1:T(8,128)(2,1)} collective-permute-done((bf16[16,7,128,128]{3,2,0,1:T(8,128)(2,1)}, bf16[16,7,128,128]{3,2,0,1:T(8,128)(2,1)}, u32[]{:S(2)}, u32[]{:S(2)}) %collective-permute-start.7) | collective-permute-done | bytes 3670048 | tf_op jit(solution)/shard_map/ppermute | solution.py:14
  188.6 2.4 convolution_select_fusion.16
  191.0 2.4 convolution_select_fusion.14
  193.4 2.4 convolution_select_fusion.12
  195.8 2.5 convolution_select_fusion.7
  198.3 2.5 convolution_select_fusion.5
  210.9 2.6 bitcast_dynamic-update-slice_fusion.3
  215.9 2.5 copy.47
  218.4 2.8 add_add_fusion
  221.2 2.6 copy.53
  229.4 2.4 bitcast_dynamic-update-slice_fusion.2
  231.8 2.5 bitcast_dynamic-update-slice_fusion.1
  246.6 3.9 %collective-permute-start.8 = (bf16[16,7,128,128]{3,2,0,1:T(8,128)(2,1)S(1)}, bf16[16,7,128,128]{3,2,0,1:T(8,128)(2,1)S(1)}, u32[]{:S(2)}, u32[]{:S(2)}) collective-permute-start(bf16[16,7,128,128]{3,2,0,1:T(8,128)(2,1)S(1)} %subtract_convert_fusion), channel_id=1, source_target_pairs={{0,4},{1,5},{2,6},{3,7},{4,8},{5,9},{6,10},{7,11},{8,12},{9,13},{1... | collective-permute-start | bytes 11010056 | tf_op jit(solution)/shard_map/ppermute | solution.py:14
  254.7 70.6 %collective-permute-done.8 = bf16[16,7,128,128]{3,2,0,1:T(8,128)(2,1)S(1)} collective-permute-done((bf16[16,7,128,128]{3,2,0,1:T(8,128)(2,1)S(1)}, bf16[16,7,128,128]{3,2,0,1:T(8,128)(2,1)S(1)}, u32[]{:S(2)}, u32[]{:S(2)}) %collective-permute-start.8) | collective-permute-done | bytes 3670048 | tf_op jit(solution)/shard_map/ppermute | solution.py:14
  331.2 45.7 %collective-permute-done.11 = bf16[16,7,128,128]{3,2,0,1:T(8,128)(2,1)S(1)} collective-permute-done((bf16[16,7,128,128]{3,2,0,1:T(8,128)(2,1)S(1)}, bf16[16,7,128,128]{3,2,0,1:T(8,128)(2,1)S(1)}, u32[]{:S(2)}, u32[]{:S(2)}) %collective-permute-start.11) | collective-permute-done | bytes 3670048 | tf_op jit(solution)/shard_map/ppermute | solution.py:14
  377.9 6.0 %copy.64 = bf16[16,7,128,128]{3,2,1,0:T(8,128)(2,1)} copy(bf16[16,7,128,128]{2,3,0,1:T(8,128)(2,1)} %fusion.49) | data formatting | bytes 7340032 | tf_op jit(solution)/shard_map/stack | solution.py:94
  (105 shorter events, 56.4 us)
Async XLA Ops:
  0.0 11.5 %copy-start.23 = (s32[16,7]{0,1:T(8,128)S(1)}, s32[16,7]{0,1:T(8,128)}, u32[]{:S(2)}) copy-start(s32[16,7]{0,1:T(8,128)} %param.3) | copy-start | bytes 1348
  6.1 117.9 %collective-permute-start.3 = (bf16[16,7,128,128]{2,3,0,1:T(8,128)(2,1)}, bf16[16,7,128,128]{2,3,0,1:T(8,128)(2,1)}, u32[]{:S(2)}, u32[]{:S(2)}) collective-permute-start(bf16[16,7,128,128]{2,3,0,1:T(8,128)(2,1)} %copy.6), channel_id=1, source_target_pairs={{0,1},{1,2},{2,3},{3,4},{4,5},{5,6},{6,7},{7,8},{8,9},{9,10},{10,1... | collective-permute-start | bytes 11010056 | tf_op jit(solution)/shard_map/ppermute | solution.py:14
  10.2 113.7 %collective-permute-start.5 = (bf16[16,7,128,128]{2,3,0,1:T(8,128)(2,1)}, bf16[16,7,128,128]{2,3,0,1:T(8,128)(2,1)}, u32[]{:S(2)}, u32[]{:S(2)}) collective-permute-start(bf16[16,7,128,128]{2,3,0,1:T(8,128)(2,1)} %copy.6), channel_id=1, source_target_pairs={{1,0},{2,1},{3,2},{4,3},{5,4},{6,5},{7,6},{8,7},{9,8},{10,9},{11,1... | collective-permute-start | bytes 11010056 | tf_op jit(solution)/shard_map/ppermute | solution.py:14
  11.5 18.7 %collective-permute-start.2 = (s32[16,7]{0,1:T(8,128)S(1)}, s32[16,7]{0,1:T(8,128)S(1)}, u32[]{:S(2)}, u32[]{:S(2)}) collective-permute-start(s32[16,7]{0,1:T(8,128)S(1)} %copy-done.23), channel_id=1, source_target_pairs={{0,1},{1,2},{2,3},{3,4},{4,5},{5,6},{6,7},{7,8},{8,9},{9,10},{10,1... | collective-permute-start | bytes 1352 | tf_op jit(solution)/shard_map/ppermute | solution.py:14
  14.9 64.7 %collective-permute-start.4 = (s32[16,7]{0,1:T(8,128)S(1)}, s32[16,7]{0,1:T(8,128)S(1)}, u32[]{:S(2)}, u32[]{:S(2)}) collective-permute-start(s32[16,7]{0,1:T(8,128)S(1)} %copy-done.23), channel_id=1, source_target_pairs={{1,0},{2,1},{3,2},{4,3},{5,4},{6,5},{7,6},{8,7},{9,8},{10,9},{11,1... | collective-permute-start | bytes 1352 | tf_op jit(solution)/shard_map/ppermute | solution.py:14
  20.5 109.5 %collective-permute-start.1 = (bf16[16,7,128,128]{3,2,0,1:T(8,128)(2,1)}, bf16[16,7,128,128]{3,2,0,1:T(8,128)(2,1)}, u32[]{:S(2)}, u32[]{:S(2)}) collective-permute-start(bf16[16,7,128,128]{3,2,0,1:T(8,128)(2,1)} %copy.3), channel_id=1, source_target_pairs={{0,4},{1,5},{2,6},{3,7},{4,8},{5,9},{6,10},{7,11},{8,12},{9,13},{1... | collective-permute-start | bytes 11010056 | tf_op jit(solution)/shard_map/ppermute | solution.py:14
  30.2 75.3 %collective-permute-start = (s32[16,7]{0,1:T(8,128)S(1)}, s32[16,7]{0,1:T(8,128)S(1)}, u32[]{:S(2)}, u32[]{:S(2)}) collective-permute-start(s32[16,7]{0,1:T(8,128)S(1)} %copy-done.23), channel_id=1, source_target_pairs={{0,4},{1,5},{2,6},{3,7},{4,8},{5,9},{6,10},{7,11},{8,12},{9,13},{1... | collective-permute-start | bytes 1352 | tf_op jit(solution)/shard_map/ppermute | solution.py:14
  79.6 27.2 %collective-permute-start.6 = (s32[16,7]{0,1:T(8,128)S(1)}, s32[16,7]{0,1:T(8,128)S(1)}, u32[]{:S(2)}, u32[]{:S(2)}) collective-permute-start(s32[16,7]{0,1:T(8,128)S(1)} %copy-done.23), channel_id=1, source_target_pairs={{4,0},{5,1},{6,2},{7,3},{8,4},{9,5},{10,6},{11,7},{12,8},{13,9},{1... | collective-permute-start | bytes 1352 | tf_op jit(solution)/shard_map/ppermute | solution.py:14
  105.5 81.4 %collective-permute-start.7 = (bf16[16,7,128,128]{3,2,0,1:T(8,128)(2,1)}, bf16[16,7,128,128]{3,2,0,1:T(8,128)(2,1)}, u32[]{:S(2)}, u32[]{:S(2)}) collective-permute-start(bf16[16,7,128,128]{3,2,0,1:T(8,128)(2,1)} %copy.3), channel_id=1, source_target_pairs={{4,0},{5,1},{6,2},{7,3},{8,4},{9,5},{10,6},{11,7},{12,8},{13,9},{1... | collective-permute-start | bytes 11010056 | tf_op jit(solution)/shard_map/ppermute | solution.py:14
  116.4 7.6 %copy-start = (bf16[16,7,128,128]{2,3,0,1:T(8,128)(2,1)S(1)}, bf16[16,7,128,128]{2,3,0,1:T(8,128)(2,1)}, u32[]{:S(2)}) copy-start(bf16[16,7,128,128]{2,3,0,1:T(8,128)(2,1)} %copy.6) | copy-start | bytes 11010052
  126.6 10.1 %copy-start.4 = (bf16[16,128,128]{1,2,0:T(8,128)(2,1)}, bf16[16,128,128]{1,2,0:T(8,128)(2,1)S(1)}, u32[]{:S(2)}) copy-start(bf16[16,128,128]{1,2,0:T(8,128)(2,1)S(1)} %get-tuple-element.19) | copy-start | bytes 1572868
  126.6 80.3 %copy-start.6 = (bf16[16,128,128]{1,2,0:T(8,128)(2,1)}, bf16[16,128,128]{1,2,0:T(8,128)(2,1)S(1)}, u32[]{:S(2)}) copy-start(bf16[16,128,128]{1,2,0:T(8,128)(2,1)S(1)} %get-tuple-element.28) | copy-start | bytes 1572868
  135.1 51.8 %copy-start.10 = (f32[16,128,128]{1,2,0:T(8,128)S(1)}, f32[16,128,128]{1,2,0:T(8,128)}, u32[]{:S(2)}) copy-start(f32[16,128,128]{1,2,0:T(8,128)} %copy.21) | copy-start | bytes 3145732
  195.8 7.3 %copy-start.8 = (bf16[16,128,128]{1,2,0:T(8,128)(2,1)S(1)}, bf16[16,128,128]{1,2,0:T(8,128)(2,1)}, u32[]{:S(2)}) copy-start(bf16[16,128,128]{1,2,0:T(8,128)(2,1)} %get-tuple-element.25) | copy-start | bytes 1572868
  195.8 7.3 %copy-start.20 = (f32[16,128,128]{1,2,0:T(8,128)S(1)}, f32[16,128,128]{1,2,0:T(8,128)}, u32[]{:S(2)}) copy-start(f32[16,128,128]{1,2,0:T(8,128)} %convolution_select_fusion.32) | copy-start | bytes 3145732
  223.8 3.9 %copy-start.22 = (bf16[16,1,128,128]{3,2,0,1:T(8,128)(2,1)S(1)}, bf16[16,1,128,128]{3,2,0,1:T(8,128)(2,1)}, u32[]{:S(2)}) copy-start(bf16[16,1,128,128]{3,2,0,1:T(8,128)(2,1)} %copy.32) | copy-start | bytes 1572868
  223.8 4.8 %copy-start.21 = (bf16[16,1,128,128]{3,2,0,1:T(8,128)(2,1)S(1)}, bf16[16,1,128,128]{3,2,0,1:T(8,128)(2,1)}, u32[]{:S(2)}) copy-start(bf16[16,1,128,128]{3,2,0,1:T(8,128)(2,1)} %copy.33) | copy-start | bytes 1572868
  223.8 5.6 %copy-start.3 = (bf16[16,128,128]{1,2,0:T(8,128)(2,1)S(1)}, bf16[16,128,128]{1,2,0:T(8,128)(2,1)}, u32[]{:S(2)}) copy-start(bf16[16,128,128]{1,2,0:T(8,128)(2,1)} %get-tuple-element.17) | copy-start | bytes 1572868
  223.8 5.6 %copy-start.16 = (f32[16,128,128]{2,1,0:T(8,128)S(1)}, f32[16,128,128]{2,1,0:T(8,128)}, u32[]{:S(2)}) copy-start(f32[16,128,128]{2,1,0:T(8,128)} %convolution_select_fusion.23) | copy-start | bytes 3145732
  225.7 6.1 %copy-start.2 = (bf16[16,128,128]{1,2,0:T(8,128)(2,1)S(1)}, bf16[16,128,128]{1,2,0:T(8,128)(2,1)}, u32[]{:S(2)}) copy-start(bf16[16,128,128]{1,2,0:T(8,128)(2,1)} %get-tuple-element.20) | copy-start | bytes 1572868
  225.7 6.1 %copy-start.14 = (f32[16,128,128]{2,1,0:T(8,128)S(1)}, f32[16,128,128]{2,1,0:T(8,128)}, u32[]{:S(2)}) copy-start(f32[16,128,128]{2,1,0:T(8,128)} %convolution_select_fusion.21) | copy-start | bytes 3145732
  229.4 5.4 %copy-start.19 = (f32[16,128,128]{2,1,0:T(8,128)S(1)}, f32[16,128,128]{2,1,0:T(8,128)}, u32[]{:S(2)}) copy-start(f32[16,128,128]{2,1,0:T(8,128)} %convolution_select_fusion.16) | copy-start | bytes 3145732
  231.8 4.5 %copy-start.9 = (bf16[16,128,128]{1,2,0:T(8,128)(2,1)S(1)}, bf16[16,128,128]{1,2,0:T(8,128)(2,1)}, u32[]{:S(2)}) copy-start(bf16[16,128,128]{1,2,0:T(8,128)(2,1)} %get-tuple-element.25) | copy-start | bytes 1572868
  231.8 4.5 %copy-start.18 = (f32[16,128,128]{2,1,0:T(8,128)S(1)}, f32[16,128,128]{2,1,0:T(8,128)}, u32[]{:S(2)}) copy-start(f32[16,128,128]{2,1,0:T(8,128)} %convolution_select_fusion.14) | copy-start | bytes 3145732
  234.8 2.2 copy-start.7
  234.8 2.2 copy-start.17
  236.3 2.3 copy-start.11
  237.0 4.7 %copy-start.5 = (bf16[16,128,128]{1,2,0:T(8,128)(2,1)S(1)}, bf16[16,128,128]{1,2,0:T(8,128)(2,1)}, u32[]{:S(2)}) copy-start(bf16[16,128,128]{1,2,0:T(8,128)(2,1)} %copy-done.4) | copy-start | bytes 1572868
  246.6 78.7 %collective-permute-start.8 = (bf16[16,7,128,128]{3,2,0,1:T(8,128)(2,1)S(1)}, bf16[16,7,128,128]{3,2,0,1:T(8,128)(2,1)S(1)}, u32[]{:S(2)}, u32[]{:S(2)}) collective-permute-start(bf16[16,7,128,128]{3,2,0,1:T(8,128)(2,1)S(1)} %subtract_convert_fusion), channel_id=1, source_target_pairs={{0,4},{1,5},{2,6},{3,7},{4,8},{5,9},{6,10},{7,11},{8,12},{9,13},{1... | collective-permute-start | bytes 11010056 | tf_op jit(solution)/shard_map/ppermute | solution.py:14
  250.5 75.8 %collective-permute-start.9 = (bf16[16,7,128,128]{3,2,0,1:T(8,128)(2,1)S(1)}, bf16[16,7,128,128]{3,2,0,1:T(8,128)(2,1)S(1)}, u32[]{:S(2)}, u32[]{:S(2)}) collective-permute-start(bf16[16,7,128,128]{3,2,0,1:T(8,128)(2,1)S(1)} %subtract_convert_fusion), channel_id=1, source_target_pairs={{0,1},{1,2},{2,3},{3,4},{4,5},{5,6},{6,7},{7,8},{8,9},{9,10},{10,1... | collective-permute-start | bytes 11010056 | tf_op jit(solution)/shard_map/ppermute | solution.py:14
  252.0 77.2 %collective-permute-start.10 = (bf16[16,7,128,128]{3,2,0,1:T(8,128)(2,1)S(1)}, bf16[16,7,128,128]{3,2,0,1:T(8,128)(2,1)S(1)}, u32[]{:S(2)}, u32[]{:S(2)}) collective-permute-start(bf16[16,7,128,128]{3,2,0,1:T(8,128)(2,1)S(1)} %subtract_convert_fusion), channel_id=1, source_target_pairs={{1,0},{2,1},{3,2},{4,3},{5,4},{6,5},{7,6},{8,7},{9,8},{10,9},{11,1... | collective-permute-start | bytes 11010056 | tf_op jit(solution)/shard_map/ppermute | solution.py:14
  253.3 123.6 %collective-permute-start.11 = (bf16[16,7,128,128]{3,2,0,1:T(8,128)(2,1)S(1)}, bf16[16,7,128,128]{3,2,0,1:T(8,128)(2,1)S(1)}, u32[]{:S(2)}, u32[]{:S(2)}) collective-permute-start(bf16[16,7,128,128]{3,2,0,1:T(8,128)(2,1)S(1)} %subtract_convert_fusion), channel_id=1, source_target_pairs={{4,0},{5,1},{6,2},{7,3},{8,4},{9,5},{10,6},{11,7},{12,8},{13,9},{1... | collective-permute-start | bytes 11010056 | tf_op jit(solution)/shard_map/ppermute | solution.py:14
  (4 other events, 6.5 us)
where the time goes:
time: 386 us; the launch traced here: 384 us
  waiting for transfers between devices  190 us (49%)
  starting transfers between devices  79.7 us (21%)
  matrix products  70.3 us (18%)
  local copies, waits for them, and re-layouts  32.4 us (8%)
  other arithmetic  11.6 us (3%)
    ppermute x12, waiting for transfers between devices, shifted(): lax.ppermute(value, axis, [(source, source + steps) for source in range(l...  190 us
    ppermute x12, starting transfers between devices, shifted(): lax.ppermute(value, axis, [(source, source + steps) for source in range(l...  79.7 us
    dot_general x38, matrix products, block_product(): jnp.einsum('imr,irn->imn', left_blocks[:, left_slot], view_b[:, right_slo...  70.3 us
    unnamed x53, local copies, waits for them, and re-layouts  15.6 us
  transfers between devices with their start and end apart: 12, of which 4 were waited for; matrix products, arithmetic and copies ran while one was open for 11% of the time, Pallas kernels for 0%

commit v1 on v0

v1 whole, which is shorter than its diff:
```python
import jax
import jax.numpy as jnp
from jax import lax
from jax.experimental import pallas as pl
from jax.experimental.pallas import tpu as pltpu
from jax.sharding import PartitionSpec as P

K = 7
GX = 8
PLANE = 64
CENTER = 3
BF16 = jnp.bfloat16
F32 = jnp.float32
VMEM_LIMIT = 48 * 1024 * 1024


def matching(value, parity, distance, period):
    count = lax.axis_size("row")
    pairs = []
    for source in range(count):
        place = source % period // distance
        step = distance if place % 2 == parity else -distance
        target = source + step
        if 0 <= target < count and target // period == source // period:
            pairs.append((source, target))
    return lax.ppermute(value, "row", pairs)


def dot(a, b):
    return jnp.dot(a, b, preferred_element_type=F32)


def masked(flag, block):
    return jnp.where(flag, block, jnp.zeros_like(block))


def rows_of(block_count, body, unroll=1):
    def step(i, carry):
        body(i)
        return carry

    lax.fori_loop(0, block_count, step, 0, unroll=unroll)


def local_edges(rows):
    edges = [(2, 1, 0, rows, -1), (4, 2, 0, rows, 1)]
    if rows > GX:
        edges += [(1, 0, GX, rows - GX, -GX), (5, 3, 0, rows - GX, GX)]
    return edges


def flip_diag_kernel(blocks, flipped):
    rows_of(flipped.shape[0], lambda j: flipped.__setitem__(j, blocks[j, CENTER].T), unroll=2)


def local_kernel(cols, blocks, diag_t, left_t, square_t, cube_t):
    rows = blocks.shape[0]
    for slot, place, first, count, step in local_edges(rows):

        def one(e, slot=slot, place=place, first=first, step=step):
            j = first + e
            k = jnp.clip(j + step, 0, rows - 1)
            x_t = masked(cols[j, slot] >= 0, blocks[k, K - 1 - slot]).T
            left_t[j, place] = x_t
            lhs = jnp.concatenate([diag_t[j], x_t], axis=1)
            rhs = jnp.concatenate([x_t, diag_t[k]], axis=0)
            square_t[j, place] = dot(lhs, rhs).astype(BF16)

        rows_of(count, one, unroll=2)
    lines = rows // GX
    for line in range(lines):

        def diag(x, line=line):
            j = line * GX + x
            lhs, rhs = [], []
            for slot, place, first, count, step in local_edges(rows):
                if first <= line * GX < first + count:
                    k = jnp.clip(j + step, 0, rows - 1)
                    lhs.append(left_t[j, place])
                    rhs.append(square_t[k, 3 - place])
            cube_t[j] = dot(jnp.concatenate(lhs, axis=1), jnp.concatenate(rhs, axis=0))

        rows_of(GX, diag, unroll=2)


def diag_square_kernel(cols, where, blocks, far_a, far_b, near_a, near_b, square_t, total):
    rows = blocks.shape[0]
    lines = rows // GX
    for line in range(lines):

        def local(x, line=line):
            j = line * GX + x
            lhs, rhs = [blocks[j, CENTER]], [blocks[j, CENTER]]
            for slot, place, first, count, step in local_edges(rows):
                if first <= line * GX < first + count:
                    k = jnp.clip(j + step, 0, rows - 1)
                    lhs.append(masked(cols[j, slot] >= 0, blocks[j, slot]))
                    rhs.append(blocks[k, K - 1 - slot])
            for far, at in ((far_a, 0), (far_b, 1)):
                lhs.append(masked(cols[j, where[at]] >= 0, blocks[j, where[at]]))
                rhs.append(far[j])
            total[j] = dot(jnp.concatenate(lhs, axis=1), jnp.concatenate(rhs, axis=0))

        rows_of(GX, local, unroll=2)
    for near, at in ((near_a, 2), (near_b, 4)):

        def edge(e, near=near, at=at):
            j = where[at + 1] + e
            left = masked(cols[j, where[at]] >= 0, blocks[j, where[at]])
            total[j] += dot(left, near[e])

        rows_of(GX, edge, unroll=2)
    rows_of(rows, lambda j: square_t.__setitem__(j, total[j].astype(BF16).T), unroll=2)


def remote_edge(flag, own, other, diag_own, diag_other):
    x_t = masked(flag, other).T
    y_t = masked(flag, own).T
    to_own = dot(jnp.concatenate([diag_own, x_t], axis=1), jnp.concatenate([x_t, diag_other], axis=0)).astype(BF16)
    to_other = dot(jnp.concatenate([diag_other, y_t], axis=1), jnp.concatenate([y_t, diag_own], axis=0)).astype(BF16)
    return x_t, to_own, dot(x_t, to_other)


def finish(diag_own, x_t, square, diag_square_other):
    cube = dot(jnp.concatenate([diag_own, x_t], axis=1), jnp.concatenate([square, diag_square_other], axis=0))
    return (3.0 * square.astype(F32) - 2.0 * cube).astype(BF16)


def near_kernel(
    cols, where, blocks, diag_t, left_t, square_t, cube_in, diag_square_t, near_a, near_b,
    out, near_left, near_square, cube_t, local_out, sem,
):
    rows = blocks.shape[0]
    for slot, place, first, count, step in local_edges(rows):

        def one(e, place=place, first=first, step=step):
            j = first + e
            k = jnp.clip(j + step, 0, rows - 1)
            local_out[place, j] = finish(diag_t[j], left_t[j, place], square_t[j, place], diag_square_t[k])

        rows_of(count, one, unroll=2)
        pltpu.make_async_copy(
            local_out.at[place, pl.ds(first, count)], out.at[pl.ds(first, count), slot], sem.at[place]
        ).start()
    rows_of(rows, lambda j: cube_t.__setitem__(j, cube_in[j]), unroll=2)
    for near, at, side in ((near_a, 2, 0), (near_b, 4, 1)):

        def edge(e, near=near, at=at, side=side):
            j = where[at + 1] + e
            x_t, square, cube = remote_edge(
                cols[j, where[at]] >= 0, blocks[j, where[at]], near[e], diag_t[j], near[GX + e]
            )
            near_left[side, e] = x_t
            near_square[side, e] = square
            cube_t[j] += cube

        rows_of(GX, edge, unroll=2)
    for slot, place, first, count, step in local_edges(rows):
        pltpu.make_async_copy(
            local_out.at[place, pl.ds(first, count)], out.at[pl.ds(first, count), slot], sem.at[place]
        ).wait()


def far_kernel(
    cols, where, blocks, diag_t, cube_t, diag_square_t, off_a, off_b, diag_a, diag_b, old,
    out, far_left, far_square, diag_out, sem,
):
    rows = blocks.shape[0]

    def one(j):
        total = cube_t[j] + dot(diag_t[j], diag_square_t[j])
        for off, diag, at in ((off_a, diag_a, 0), (off_b, diag_b, 1)):
            x_t, square, cube = remote_edge(
                cols[j, where[at]] >= 0, blocks[j, where[at]], off[j], diag_t[j], diag[j]
            )
            far_left[at, j] = x_t
            far_square[at, j] = square
            total += cube
        diag_out[j] = (3.0 * diag_square_t[j].astype(F32) - 2.0 * total).astype(BF16)

    rows_of(rows, one, unroll=2)
    copy = pltpu.make_async_copy(diag_out, out.at[:, CENTER], sem)
    copy.start()
    copy.wait()


def last_kernel(
    where, diag_t, far_left, far_square, far_a, far_b, near_left, near_square, near_a, near_b, old,
    out, far_out, near_out, sem,
):
    rows = diag_t.shape[0]
    copies = []
    for near, at, side in ((near_a, 2, 0), (near_b, 4, 1)):
        base = where[at + 1]

        def edge(e, near=near, base=base, side=side):
            near_out[side, e] = finish(diag_t[base + e], near_left[side, e], near_square[side, e], near[e])

        rows_of(GX, edge, unroll=2)
        copies.append(
            pltpu.make_async_copy(near_out.at[side], out.at[pl.ds(base, GX), where[at]], sem.at[2 + side])
        )
        copies[-1].start()
    for far, side in ((far_a, 0), (far_b, 1)):

        def edge(j, far=far, side=side):
            far_out[side, j] = finish(diag_t[j], far_left[side, j], far_square[side, j], far[j])

        rows_of(rows, edge, unroll=2)
        copies.append(pltpu.make_async_copy(far_out.at[side], out.at[:, where[side]], sem.at[side]))
        copies[-1].start()
    for copy in copies:
        copy.wait()


def on_device(density, block_cols):
    rows, _, size, _ = density.shape
    layer_dist = PLANE // rows
    row_id = lax.axis_index("row")
    layer_odd = row_id // layer_dist % 2
    strip_odd = row_id % layer_dist % 2
    slot_fa = jnp.where(layer_odd == 0, 6, 0)
    slot_na = jnp.where(strip_odd == 0, 5, 1)
    base_na = jnp.where(strip_odd == 0, rows - GX, 0)
    where = jnp.stack([slot_fa, 6 - slot_fa, slot_na, base_na, 6 - slot_na, rows - GX - base_na]).astype(jnp.int32)

    def block(*dims):
        return jax.ShapeDtypeStruct((*dims, size, size), BF16)

    def total(*dims):
        return jax.ShapeDtypeStruct((*dims, size, size), F32)

    smem = pl.BlockSpec(memory_space=pltpu.SMEM)
    vmem = pl.BlockSpec(memory_space=pltpu.VMEM)
    hbm = pl.BlockSpec(memory_space=pl.ANY)

    def call(kernel, ins, outs, out_specs, scratch, products, args, aliases=None):
        return pl.pallas_call(
            kernel,
            in_specs=ins,
            out_specs=out_specs,
            out_shape=outs,
            scratch_shapes=scratch,
            input_output_aliases=aliases or {},
            compiler_params=pltpu.CompilerParams(vmem_limit_bytes=VMEM_LIMIT),
            cost_estimate=pl.CostEstimate(
                flops=products * 2 * size**3, bytes_accessed=4 * rows * size * size * 2, transcendentals=0
            ),
        )(*args)

    def far(value, pairing):
        return matching(value, pairing, layer_dist, lax.axis_size("row"))

    def near(value, pairing):
        return matching(value, pairing, 1, layer_dist)

    def slot_of(slot):
        return lax.dynamic_index_in_dim(density, slot, 1, keepdims=False)

    def strip_of(value, base):
        return lax.dynamic_slice_in_dim(value, base, GX, 0)

    off_b = far(slot_of(6 - slot_fa), 1)
    off_a = far(slot_of(slot_fa), 0)

    diag_t = call(flip_diag_kernel, [vmem], block(rows), vmem, [], rows, [density])
    diag_b = far(diag_t, 1)
    diag_a = far(diag_t, 0)
    strips = []
    for slot, base in ((slot_na, base_na), (6 - slot_na, rows - GX - base_na)):
        strips.append(jnp.concatenate([strip_of(slot_of(slot), base), strip_of(diag_t, base)], axis=0))
    near_b = near(strips[1], 1)
    near_a = near(strips[0], 0)

    left_t, square_t, cube_t = call(
        local_kernel,
        [smem, vmem, vmem],
        [block(rows, 4), block(rows, 4), total(rows)],
        [vmem] * 3,
        [],
        12 * rows,
        [block_cols, density, diag_t],
    )
    diag_square_t = call(
        diag_square_kernel,
        [smem, smem] + [vmem] * 5,
        block(rows),
        vmem,
        [pltpu.VMEM((rows, size, size), F32)],
        7 * rows,
        [block_cols, where, density, off_a, off_b, near_a, near_b],
    )
    far_square_b = far(diag_square_t, 1)
    far_square_a = far(diag_square_t, 0)
    near_square_b = near(strip_of(diag_square_t, rows - GX - base_na), 1)
    near_square_a = near(strip_of(diag_square_t, base_na), 0)

    out, near_left, near_square, cube_t = call(
        near_kernel,
        [smem, smem] + [vmem] * 8,
        [block(rows, K), block(2, GX), block(2, GX), total(rows)],
        [hbm] + [vmem] * 3,
        [pltpu.VMEM((4, rows, size, size), BF16), pltpu.SemaphoreType.DMA((4,))],
        12 * rows,
        [block_cols, where, density, diag_t, left_t, square_t, cube_t, diag_square_t, near_a, near_b],
    )
    out, far_left, far_square = call(
        far_kernel,
        [smem, smem] + [vmem] * 8 + [hbm],
        [block(rows, K), block(2, rows), block(2, rows)],
        [hbm] + [vmem] * 2,
        [pltpu.VMEM((rows, size, size), BF16), pltpu.SemaphoreType.DMA],
        12 * rows,
        [block_cols, where, density, diag_t, cube_t, diag_square_t, off_a, off_b, diag_a, diag_b, out],
        {10: 0},
    )
    return call(
        last_kernel,
        [smem] + [vmem] * 9 + [hbm],
        block(rows, K),
        hbm,
        [
            pltpu.VMEM((2, rows, size, size), BF16),
            pltpu.VMEM((2, GX, size, size), BF16),
            pltpu.SemaphoreType.DMA((4,)),
        ],
        6 * rows,
        [
            where, diag_t, far_left, far_square, far_square_a, far_square_b,
            near_left, near_square, near_square_a, near_square_b, out,
        ],
        {10: 0},
    )


def solution(mesh):
    placed = (P(("groups", "row"), None, None, None), P(("groups", "row"), None))
    return jax.shard_map(
        on_device,
        mesh=mesh,
        in_specs=placed,
        out_specs=P(("groups", "row"), None, None, None),
        check_vma=False,
    )
```

time: 386 us -> 83 us (0.22)
  the two profiles are of different devices: /device:TPU:0 before, /device:TPU:11 now
where the time goes in v1:
time: 83 us; the launch traced here: 82.7 us
  Pallas kernels  43.2 us (52%)
  starting transfers between devices  17.5 us (21%)
  waiting for transfers between devices  10.7 us (13%)
  local copies, waits for them, and re-layouts  9.28 us (11%)
  other arithmetic  1.7 us (2%)
    pallas_call x6, Pallas kernels, call(): pl.pallas_call(kernel, in_specs=ins, out_specs=out_specs, out_shape=outs,...  43.2 us
    ppermute x10, starting transfers between devices, matching(): return lax.ppermute(value, 'row', pairs)  17.5 us
    ppermute x10, waiting for transfers between devices, matching(): return lax.ppermute(value, 'row', pairs)  10.7 us
    unnamed x11, local copies, waits for them, and re-layouts  5.74 us
    squeeze x1, local copies, waits for them, and re-layouts, slot_of(): return lax.dynamic_index_in_dim(density, slot, 1, keepdims=False)  2.29 us
    concatenate x2, other arithmetic, on_device(): jnp.concatenate([strip_of(slot_of(slot), base), strip_of(diag_t, base)],...  1.7 us
  transfers between devices with their start and end apart: 10, of which 2 were waited for; matrix products, arithmetic and copies ran while one was open for 4% of the time, Pallas kernels for 45%

profile of v1, /device:TPU:11, one launch (start us, length us, event | category | flops | bytes accessed | tf_op | source)
XLA Modules:
  0.0 82.7 jit_solution(12224969170740569317)
XLA Ops:
  0.0 2.0 %copy-done = bf16[16,7,128,128]{3,2,1,0:T(8,128)(2,1)S(1)} copy-done((bf16[16,7,128,128]{3,2,1,0:T(8,128)(2,1)S(1)}, bf16[16,7,128,128]{3,2,1,0:T(8,128)(2,1)}, u32[]{:S(2)}) %copy-start) | copy-done | bytes 3670040
  2.0 0.6 shard_map.28.diag_t
  2.6 0.0 copy-start.4
  2.7 1.1 %dynamic-slice_bitcast_fusion.2 = (bf16[8,128,128]{2,1,0:T(8,128)(2,1)S(1)}, bf16[8,128,128]{2,1,0:T(8,128)(2,1)S(1)}) fusion(bf16[16,7,128,128]{3,2,1,0:T(8,128)(2,1)} %blocks.9, s32[]{:T(128)S(6)} %select_n.65, s32[]{:T(128)S(6)} %select_n.67, s32[]{:T(128)S(6)} %select_n.62, s32[]{:T(128)S(6)} %select_n.63), kind=kLoop, calls=%fused_computation.4 | loop fusion | bytes 1048592 | tf_op jit(solution)/shard_map/dynamic_slice | solution.py:261
  3.8 0.8 %pad_maximum_fusion = bf16[16,128,128]{2,1,0:T(8,128)(2,1)} fusion(bf16[8,128,128]{2,1,0:T(8,128)(2,1)S(1)} %get-tuple-element.32, bf16[8,128,128]{2,1,0:T(8,128)(2,1)S(1)} %get-tuple-element.26), kind=kLoop, calls=%fused_computation | loop fusion | flops 262144 | bytes 1048576 | tf_op jit(solution)/shard_map/concatenate | solution.py:271
  4.6 0.7 collective-permute-start.2
  5.3 0.9 %pad_maximum_fusion.1 = bf16[16,128,128]{2,1,0:T(8,128)(2,1)} fusion(bf16[8,128,128]{2,1,0:T(8,128)(2,1)S(1)} %get-tuple-element.31, bf16[8,128,128]{2,1,0:T(8,128)(2,1)S(1)} %get-tuple-element.25), kind=kLoop, calls=%fused_computation.1 | loop fusion | flops 262144 | bytes 1048576 | tf_op jit(solution)/shard_map/concatenate | solution.py:271
  6.2 3.0 %collective-permute-start.3 = (bf16[16,128,128]{2,1,0:T(8,128)(2,1)}, bf16[16,128,128]{2,1,0:T(8,128)(2,1)S(1)}, u32[]{:S(2)}, u32[]{:S(2)}) collective-permute-start(bf16[16,128,128]{2,1,0:T(8,128)(2,1)} %pad_maximum_fusion.1), channel_id=1, source_target_pairs={{1,2},{2,1},{5,6},{6,5},{9,10},{10,9},{13,14},{14,13},{17,18},{18,... | collective-permute-start | bytes 1572872 | tf_op jit(solution)/shard_map/ppermute | solution.py:26
  9.2 2.3 %dynamic-slice_bitcast_fusion = (bf16[16,128,128]{2,1,0:T(8,128)(2,1)}, bf16[16,128,128]{2,1,0:T(8,128)(2,1)}) fusion(bf16[16,7,128,128]{3,2,1,0:T(8,128)(2,1)} %blocks.9, s32[]{:T(128)S(6)} %select_n.61, s32[]{:T(128)} %select_n.56), kind=kLoop, calls=%fused_computation.2 | loop fusion | bytes 2097160 | tf_op jit(solution)/shard_map/jit(dynamic_index_in_dim)/squeeze | solution.py:258
  11.5 0.2 collective-permute-start
  11.7 4.3 %collective-permute-start.1 = (bf16[16,128,128]{2,1,0:T(8,128)(2,1)}, bf16[16,128,128]{2,1,0:T(8,128)(2,1)S(1)}, u32[]{:S(2)}, u32[]{:S(2)}) collective-permute-start(bf16[16,128,128]{2,1,0:T(8,128)(2,1)} %get-tuple-element.27), channel_id=1, source_target_pairs={{4,8},{5,9},{6,10},{7,11},{8,4},{9,5},{10,6},{11,7},{20,24},{21,25... | collective-permute-start | bytes 1572872 | tf_op jit(solution)/shard_map/ppermute | solution.py:26
  16.0 0.1 collective-permute-start.4
  16.1 0.0 collective-permute-done.2.near_a
  16.1 1.9 %collective-permute-start.5 = (bf16[16,128,128]{2,1,0:T(8,128)(2,1)S(1)}, bf16[16,128,128]{2,1,0:T(8,128)(2,1)}, u32[]{:S(2)}, u32[]{:S(2)}) collective-permute-start(bf16[16,128,128]{2,1,0:T(8,128)(2,1)S(1)} %shard_map.28.diag_t), channel_id=1, source_target_pairs={{4,8},{5,9},{6,10},{7,11},{8,4},{9,5},{10,6},{11,7},{20,24},{21,25... | collective-permute-start | bytes 1572872 | tf_op jit(solution)/shard_map/ppermute | solution.py:26
  18.0 0.1 copy.8.cols
  18.1 0.1 stack.27.where
  18.2 0.0 collective-permute-done.3.near_b
  18.2 7.6 %collective-permute-done.far_a.off_a = bf16[16,128,128]{2,1,0:T(8,128)(2,1)S(1)} collective-permute-done((bf16[16,128,128]{2,1,0:T(8,128)(2,1)}, bf16[16,128,128]{2,1,0:T(8,128)(2,1)S(1)}, u32[]{:S(2)}, u32[]{:S(2)}) %collective-permute-start) | collective-permute-done | bytes 524320 | tf_op jit(solution)/shard_map/ppermute | solution.py:26
  25.8 3.0 %collective-permute-done.1.far_b.off_b = bf16[16,128,128]{2,1,0:T(8,128)(2,1)S(1)} collective-permute-done((bf16[16,128,128]{2,1,0:T(8,128)(2,1)}, bf16[16,128,128]{2,1,0:T(8,128)(2,1)S(1)}, u32[]{:S(2)}, u32[]{:S(2)}) %collective-permute-start.1) | collective-permute-done | bytes 524320 | tf_op jit(solution)/shard_map/ppermute | solution.py:26
  28.9 6.0 %shard_map.30.diag_square_t = bf16[16,128,128]{2,1,0:T(8,128)(2,1)S(1)} custom-call(s32[16,7]{1,0:T(8,128)S(1)} %copy.8.cols, s32[6]{0:T(128)S(1)} %stack.27.where, bf16[16,7,128,128]{3,2,1,0:T(8,128)(2,1)} %blocks.9, bf16[16,128,128]{2,1,0:T(8,128)(2,1)S(1)} %collective-permute-done.far_a.off_a, ...), custom_call_target="tpu_custom_call" | custom-call | flops 469762048 | bytes 2097152 | tf_op jit(solution)/shard_map/pallas_call | solution.py:238
  34.8 0.1 collective-permute-start.6
  34.9 3.4 %collective-permute-start.7 = (bf16[16,128,128]{2,1,0:T(8,128)(2,1)S(1)}, bf16[16,128,128]{2,1,0:T(8,128)(2,1)S(1)}, u32[]{:S(2)}, u32[]{:S(2)}) collective-permute-start(bf16[16,128,128]{2,1,0:T(8,128)(2,1)S(1)} %shard_map.30.diag_square_t), channel_id=1, source_target_pairs={{4,8},{5,9},{6,10},{7,11},{8,4},{9,5},{10,6},{11,7},{20,24},{21,25... | collective-permute-start | bytes 1572872 | tf_op jit(solution)/shard_map/ppermute | solution.py:26
  38.3 0.1 collective-permute-start.8
  38.4 3.8 %collective-permute-start.9 = (bf16[8,128,128]{2,1,0:T(8,128)(2,1)S(1)}, bf16[8,128,128]{2,1,0:T(8,128)(2,1)S(1)}, u32[]{:S(2)}, u32[]{:S(2)}) collective-permute-start(bf16[8,128,128]{2,1,0:T(8,128)(2,1)S(1)} %get-tuple-element.29), channel_id=1, source_target_pairs={{1,2},{2,1},{5,6},{6,5},{9,10},{10,9},{13,14},{14,13},{17,18},{18,... | collective-permute-start | bytes 786440 | tf_op jit(solution)/shard_map/ppermute | solution.py:26
  42.3 9.3 %shard_map.29 = (bf16[16,4,128,128]{3,2,1,0:T(8,128)(2,1)S(1)}, bf16[16,4,128,128]{3,2,1,0:T(8,128)(2,1)S(1)}, f32[16,128,128]{2,1,0:T(8,128)S(1)}) custom-call(s32[16,7]{1,0:T(8,128)S(1)} %copy.8.cols, bf16[16,7,128,128]{3,2,1,0:T(8,128)(2,1)} %blocks.9, bf16[16,128,128]{2,1,0:T(8,128)(2,1)S(1)} %shard_map.28.diag_t), custom_call_target="tpu_custom_call" | custom-call | flops 805306368 | bytes 2097152 | tf_op jit(solution)/shard_map/pallas_call | solution.py:238
  51.6 1.3 %copy-done.1 = bf16[16,4,128,128]{3,2,1,0:T(8,128)(2,1)} copy-done((bf16[16,4,128,128]{3,2,1,0:T(8,128)(2,1)}, bf16[16,4,128,128]{3,2,1,0:T(8,128)(2,1)S(1)}, u32[]{:S(2)}) %copy-start.1) | copy-done | bytes 2097176
  53.0 1.3 %copy-done.2 = bf16[16,4,128,128]{3,2,1,0:T(8,128)(2,1)} copy-done((bf16[16,4,128,128]{3,2,1,0:T(8,128)(2,1)}, bf16[16,4,128,128]{3,2,1,0:T(8,128)(2,1)S(1)}, u32[]{:S(2)}) %copy-start.2) | copy-done | bytes 2097176
  54.3 12.2 %shard_map.31 = (bf16[16,7,128,128]{3,2,1,0:T(8,128)(2,1)}, bf16[2,8,128,128]{3,2,1,0:T(8,128)(2,1)S(1)}, bf16[2,8,128,128]{3,2,1,0:T(8,128)(2,1)S(1)}, f32[16,128,128]{2,1,0:T(8,128)S(1)}) custom-call(s32[16,7]{1,0:T(8,128)S(1)} %copy.8.cols, s32[6]{0:T(128)S(1)} %stack.27.where, bf16[16,7,128,128]{3,2,1,0:T(8,128)(2,1)} %blocks.9, ...), custom_call_target="tpu_custom_call" | custom-call | flops 805306368 | bytes 2097152 | tf_op jit(solution)/shard_map/pallas_call | solution.py:238
  66.5 1.0 %copy-done.3 = f32[16,128,128]{2,1,0:T(8,128)} copy-done((f32[16,128,128]{2,1,0:T(8,128)}, f32[16,128,128]{2,1,0:T(8,128)S(1)}, u32[]{:S(2)}) %copy-start.3) | copy-done | bytes 1048600
  67.5 0.0 collective-permute-done.5.diag_b
  67.5 9.5 %shard_map.32 = (bf16[16,7,128,128]{3,2,1,0:T(8,128)(2,1)}, bf16[2,16,128,128]{3,2,1,0:T(8,128)(2,1)S(1)}, bf16[2,16,128,128]{3,2,1,0:T(8,128)(2,1)S(1)}) custom-call(s32[16,7]{1,0:T(8,128)S(1)} %copy.8.cols, s32[6]{0:T(128)S(1)} %stack.27.where, bf16[16,7,128,128]{3,2,1,0:T(8,128)(2,1)} %blocks.9, ...), custom_call_target="tpu_custom_call", output_to_operand_aliasing={{0}: (10, {})} | custom-call | flops 805306368 | bytes 2097152 | tf_op jit(solution)/shard_map/pallas_call | solution.py:238
  77.0 5.6 %shard_map.33 = bf16[16,7,128,128]{3,2,1,0:T(8,128)(2,1)} custom-call(s32[6]{0:T(128)S(1)} %stack.27.where, bf16[16,128,128]{2,1,0:T(8,128)(2,1)S(1)} %shard_map.28.diag_t, bf16[2,16,128,128]{3,2,1,0:T(8,128)(2,1)S(1)} %get-tuple-element.20.far_left, bf16[2,16,128,128]{3,2,1,0:T(8,128)(2,1)S(1)} %get-tuple-element.21.far_square, ...), custom_call_target="tpu_custom_call", output_to_operand_aliasing={{}: (10, {})} | custom-call | flops 402653184 | bytes 2097152 | tf_op jit(solution)/shard_map/pallas_call | solution.py:238
  (12 shorter events, 0.1 us)
Async XLA Ops:
  0.0 2.0 %copy-start = (bf16[16,7,128,128]{3,2,1,0:T(8,128)(2,1)S(1)}, bf16[16,7,128,128]{3,2,1,0:T(8,128)(2,1)}, u32[]{:S(2)}) copy-start(bf16[16,7,128,128]{3,2,1,0:T(8,128)(2,1)} %blocks.9) | copy-start | bytes 11010052
  2.6 15.4 %copy-start.4 = (s32[16,7]{0,1:T(8,128)S(1)}, s32[16,7]{0,1:T(8,128)}, u32[]{:S(2)}) copy-start(s32[16,7]{0,1:T(8,128)} %param.3) | copy-start | bytes 1348
  4.6 11.5 %collective-permute-start.2 = (bf16[16,128,128]{2,1,0:T(8,128)(2,1)}, bf16[16,128,128]{2,1,0:T(8,128)(2,1)S(1)}, u32[]{:S(2)}, u32[]{:S(2)}) collective-permute-start(bf16[16,128,128]{2,1,0:T(8,128)(2,1)} %pad_maximum_fusion), channel_id=1, source_target_pairs={{0,1},{1,0},{2,3},{3,2},{4,5},{5,4},{6,7},{7,6},{8,9},{9,8},{10,11... | collective-permute-start | bytes 1572872 | tf_op jit(solution)/shard_map/ppermute | solution.py:26
  6.2 12.0 %collective-permute-start.3 = (bf16[16,128,128]{2,1,0:T(8,128)(2,1)}, bf16[16,128,128]{2,1,0:T(8,128)(2,1)S(1)}, u32[]{:S(2)}, u32[]{:S(2)}) collective-permute-start(bf16[16,128,128]{2,1,0:T(8,128)(2,1)} %pad_maximum_fusion.1), channel_id=1, source_target_pairs={{1,2},{2,1},{5,6},{6,5},{9,10},{10,9},{13,14},{14,13},{17,18},{18,... | collective-permute-start | bytes 1572872 | tf_op jit(solution)/shard_map/ppermute | solution.py:26
  11.5 14.3 %collective-permute-start = (bf16[16,128,128]{2,1,0:T(8,128)(2,1)}, bf16[16,128,128]{2,1,0:T(8,128)(2,1)S(1)}, u32[]{:S(2)}, u32[]{:S(2)}) collective-permute-start(bf16[16,128,128]{2,1,0:T(8,128)(2,1)} %get-tuple-element.28), channel_id=1, source_target_pairs={{0,4},{1,5},{2,6},{3,7},{4,0},{5,1},{6,2},{7,3},{8,12},{9,13},{10,... | collective-permute-start | bytes 1572872 | tf_op jit(solution)/shard_map/ppermute | solution.py:26
  11.7 17.2 %collective-permute-start.1 = (bf16[16,128,128]{2,1,0:T(8,128)(2,1)}, bf16[16,128,128]{2,1,0:T(8,128)(2,1)S(1)}, u32[]{:S(2)}, u32[]{:S(2)}) collective-permute-start(bf16[16,128,128]{2,1,0:T(8,128)(2,1)} %get-tuple-element.27), channel_id=1, source_target_pairs={{4,8},{5,9},{6,10},{7,11},{8,4},{9,5},{10,6},{11,7},{20,24},{21,25... | collective-permute-start | bytes 1572872 | tf_op jit(solution)/shard_map/ppermute | solution.py:26
  16.0 22.4 %collective-permute-start.4 = (bf16[16,128,128]{2,1,0:T(8,128)(2,1)S(1)}, bf16[16,128,128]{2,1,0:T(8,128)(2,1)S(1)}, u32[]{:S(2)}, u32[]{:S(2)}) collective-permute-start(bf16[16,128,128]{2,1,0:T(8,128)(2,1)S(1)} %shard_map.28.diag_t), channel_id=1, source_target_pairs={{0,4},{1,5},{2,6},{3,7},{4,0},{5,1},{6,2},{7,3},{8,12},{9,13},{10,... | collective-permute-start | bytes 1572872 | tf_op jit(solution)/shard_map/ppermute | solution.py:26
  16.1 51.4 %collective-permute-start.5 = (bf16[16,128,128]{2,1,0:T(8,128)(2,1)S(1)}, bf16[16,128,128]{2,1,0:T(8,128)(2,1)}, u32[]{:S(2)}, u32[]{:S(2)}) collective-permute-start(bf16[16,128,128]{2,1,0:T(8,128)(2,1)S(1)} %shard_map.28.diag_t), channel_id=1, source_target_pairs={{4,8},{5,9},{6,10},{7,11},{8,4},{9,5},{10,6},{11,7},{20,24},{21,25... | collective-permute-start | bytes 1572872 | tf_op jit(solution)/shard_map/ppermute | solution.py:26
  34.8 42.2 %collective-permute-start.6 = (bf16[16,128,128]{2,1,0:T(8,128)(2,1)S(1)}, bf16[16,128,128]{2,1,0:T(8,128)(2,1)S(1)}, u32[]{:S(2)}, u32[]{:S(2)}) collective-permute-start(bf16[16,128,128]{2,1,0:T(8,128)(2,1)S(1)} %shard_map.30.diag_square_t), channel_id=1, source_target_pairs={{0,4},{1,5},{2,6},{3,7},{4,0},{5,1},{6,2},{7,3},{8,12},{9,13},{10,... | collective-permute-start | bytes 1572872 | tf_op jit(solution)/shard_map/ppermute | solution.py:26
  34.9 42.1 %collective-permute-start.7 = (bf16[16,128,128]{2,1,0:T(8,128)(2,1)S(1)}, bf16[16,128,128]{2,1,0:T(8,128)(2,1)S(1)}, u32[]{:S(2)}, u32[]{:S(2)}) collective-permute-start(bf16[16,128,128]{2,1,0:T(8,128)(2,1)S(1)} %shard_map.30.diag_square_t), channel_id=1, source_target_pairs={{4,8},{5,9},{6,10},{7,11},{8,4},{9,5},{10,6},{11,7},{20,24},{21,25... | collective-permute-start | bytes 1572872 | tf_op jit(solution)/shard_map/ppermute | solution.py:26
  38.3 38.7 %collective-permute-start.8 = (bf16[8,128,128]{2,1,0:T(8,128)(2,1)S(1)}, bf16[8,128,128]{2,1,0:T(8,128)(2,1)S(1)}, u32[]{:S(2)}, u32[]{:S(2)}) collective-permute-start(bf16[8,128,128]{2,1,0:T(8,128)(2,1)S(1)} %get-tuple-element.30), channel_id=1, source_target_pairs={{0,1},{1,0},{2,3},{3,2},{4,5},{5,4},{6,7},{7,6},{8,9},{9,8},{10,11... | collective-permute-start | bytes 786440 | tf_op jit(solution)/shard_map/ppermute | solution.py:26
  38.4 38.6 %collective-permute-start.9 = (bf16[8,128,128]{2,1,0:T(8,128)(2,1)S(1)}, bf16[8,128,128]{2,1,0:T(8,128)(2,1)S(1)}, u32[]{:S(2)}, u32[]{:S(2)}) collective-permute-start(bf16[8,128,128]{2,1,0:T(8,128)(2,1)S(1)} %get-tuple-element.29), channel_id=1, source_target_pairs={{1,2},{2,1},{5,6},{6,5},{9,10},{10,9},{13,14},{14,13},{17,18},{18,... | collective-permute-start | bytes 786440 | tf_op jit(solution)/shard_map/ppermute | solution.py:26
  51.6 1.3 %copy-start.1 = (bf16[16,4,128,128]{3,2,1,0:T(8,128)(2,1)}, bf16[16,4,128,128]{3,2,1,0:T(8,128)(2,1)S(1)}, u32[]{:S(2)}) copy-start(bf16[16,4,128,128]{3,2,1,0:T(8,128)(2,1)S(1)} %get-tuple-element.15.left_t) | copy-start | bytes 6291460
  53.0 1.3 %copy-start.2 = (bf16[16,4,128,128]{3,2,1,0:T(8,128)(2,1)}, bf16[16,4,128,128]{3,2,1,0:T(8,128)(2,1)S(1)}, u32[]{:S(2)}) copy-start(bf16[16,4,128,128]{3,2,1,0:T(8,128)(2,1)S(1)} %get-tuple-element.16.square_t) | copy-start | bytes 6291460
  66.5 1.0 %copy-start.3 = (f32[16,128,128]{2,1,0:T(8,128)}, f32[16,128,128]{2,1,0:T(8,128)S(1)}, u32[]{:S(2)}) copy-start(f32[16,128,128]{2,1,0:T(8,128)S(1)} %get-tuple-element.18.cube_t) | copy-start | bytes 3145732

commit v2 on v0

v2 whole, which is shorter than its diff:
```python
import jax
import jax.numpy as jnp
from jax import lax
from jax.experimental import pallas as pl
from jax.experimental.pallas import tpu as pltpu
from jax.sharding import PartitionSpec as P

K = 7
GX = 8
PLANE = 64
CENTER = 3
BF16 = jnp.bfloat16
F32 = jnp.float32
VMEM_LIMIT = 12 * 1024 * 1024
KERNEL_COST = 1000
STAGE_LIMIT = 58 * 1024 * 1024


def matching(value, parity, distance, period):
    count = lax.axis_size("row")
    pairs = []
    for source in range(count):
        place = source % period // distance
        step = distance if place % 2 == parity else -distance
        target = source + step
        if 0 <= target < count and target // period == source // period:
            pairs.append((source, target))
    return lax.ppermute(value, "row", pairs)


def dot(a, b):
    return jnp.dot(a, b, preferred_element_type=F32)


def masked(flag, block):
    return jnp.where(flag, block, jnp.zeros_like(block))


def in_groups(items, load, compute, store, group=16):
    for start in range(0, len(items), group):
        chunk = items[start : start + group]
        loaded = [load(item) for item in chunk]
        results = [compute(*values) for values in loaded]
        for item, result in zip(chunk, results):
            store(item, result)


def local_edges(rows):
    edges = []
    for slot, place, step in ((2, 1, -1), (4, 2, 1), (1, 0, -GX), (5, 3, GX)):
        for j in range(rows):
            k = j + step
            if 0 <= k < rows and (abs(step) == GX or k // GX == j // GX):
                edges.append((j, slot, place, k))
    return edges


def places(rows):
    row_id = lax.axis_index("row")
    layer_dist = PLANE // rows
    far_slot = jnp.where(row_id // layer_dist % 2 == 0, K - 1, 0)
    even = row_id % layer_dist % 2 == 0
    near_slot = jnp.where(even, CENTER + 2, CENTER - 2)
    near_base = jnp.where(even, rows - GX, 0)
    return (far_slot, K - 1 - far_slot), (near_slot, K - 1 - near_slot), (near_base, rows - GX - near_base)


def stage_kernel(blocks, diag_t, send_a, send_b, strip_a, strip_b, diag, sem):
    rows = blocks.shape[0]
    far_slots, near_slots, bases = places(rows)
    copies = [pltpu.make_async_copy(blocks.at[:, CENTER], diag, sem.at[0])]
    for at, send in ((1, send_b), (0, send_a)):
        copies.append(pltpu.make_async_copy(blocks.at[:, far_slots[at]], send, sem.at[1 + at]))
    for at, strip in ((1, strip_b), (0, strip_a)):
        source = blocks.at[pl.ds(bases[at], GX), near_slots[at]]
        copies.append(pltpu.make_async_copy(source, strip.at[pl.ds(0, GX)], sem.at[3 + at]))
    for copy in copies:
        copy.start()
    copies[0].wait()
    in_groups(list(range(rows)), lambda j: (diag[j],), lambda x: x.T, diag_t.__setitem__)
    for at, strip in ((1, strip_b), (0, strip_a)):
        for e in range(GX):
            strip[GX + e] = diag_t[bases[at] + e]
    for copy in copies[1:]:
        copy.wait()


def local_kernel(
    cols, blocks, diag_t, near_a, near_b,
    left_t, square_t, cube_t, near_left, near_square, total, near_right, near_other,
):
    rows = blocks.shape[0]
    edges = local_edges(rows)
    _, near_slots, bases = places(rows)
    strip = list(range(GX))

    def load(edge):
        j, slot, place, k = edge
        return cols[j, slot] >= 0, blocks[k, K - 1 - slot], diag_t[j], diag_t[k]

    def compute(flag, x, diag_own, diag_other):
        x_t = flipped(flag, x)
        return x_t, one_square(diag_own, x_t, diag_other)

    def store(edge, result):
        j, slot, place, k = edge
        left_t[place, j], square_t[place, j] = result

    in_groups(edges, load, compute, store)
    if rows != 2 * GX:
        total[...] = jnp.zeros_like(total)
        cube_t[...] = jnp.zeros_like(cube_t)
    for side, near in enumerate((near_a, near_b)):
        slot, base = near_slots[side], bases[side]

        def load_left(e):
            return cols[base + e, slot] >= 0, near[e]

        def load_right(e):
            return cols[base + e, slot] >= 0, blocks[base + e, slot]

        in_groups(strip, load_left, flipped, lambda e, value: near_left.__setitem__((side, e), value))
        in_groups(strip, load_right, flipped, lambda e, value: near_right.__setitem__((side, e), value))
        in_groups(
            strip,
            lambda e: (diag_t[base + e], near_left[side, e], near[GX + e]),
            one_square,
            lambda e, value: near_square.__setitem__((side, e), value),
        )
        in_groups(
            strip,
            lambda e: (near[GX + e], near_right[side, e], diag_t[base + e]),
            one_square,
            lambda e, value: near_other.__setitem__((side, e), value),
        )

        def load_near(e):
            j = base + e
            return near_left[side, e], near_other[side, e], near_right[side, e]

        def near_terms(x_t, square, y_t):
            return dot(x_t, square), dot(x_t, y_t)

        def store_near(e, result):
            j = base + e
            for ref, value in zip((cube_t, total), result):
                ref[j] = value if rows == 2 * GX else ref[j] + value

        in_groups(strip, load_near, near_terms, store_near)

    def load_row(j):
        own = [edge for edge in edges if edge[0] == j]
        lhs = [left_t[place, j] for _, _, place, _ in own]
        squares = [square_t[3 - place, k] for _, _, place, k in own]
        others = [left_t[3 - place, k] for _, _, place, k in own]
        return (
            jnp.concatenate(lhs, axis=1),
            jnp.concatenate(squares, axis=0),
            jnp.concatenate(lhs + [diag_t[j]], axis=1),
            jnp.concatenate(others + [diag_t[j]], axis=0),
            cube_t[j],
            total[j],
        )

    def row_terms(lhs, squares, lhs_all, others, cube, square):
        return dot(lhs, squares) + cube, dot(lhs_all, others) + square

    def store_row(j, result):
        cube_t[j], total[j] = result

    in_groups(list(range(rows)), load_row, row_terms, store_row)


def diag_square_kernel(cols, blocks, total, far_a, far_b, square_t):
    rows = blocks.shape[0]
    far_slots, _, _ = places(rows)

    def load(j):
        own = [masked(cols[j, slot] >= 0, blocks[j, slot]) for slot in far_slots]
        return jnp.concatenate(own, axis=1), jnp.concatenate([far_a[j], far_b[j]], axis=0), total[j]

    in_groups(
        list(range(rows)),
        load,
        lambda lhs, rhs, extra_t: (dot(lhs, rhs).T + extra_t).astype(BF16),
        square_t.__setitem__,
    )


def one_square(diag_own, x_t, diag_other):
    lhs = jnp.concatenate([diag_own, x_t], axis=1)
    rhs = jnp.concatenate([x_t, diag_other], axis=0)
    return dot(lhs, rhs).astype(BF16)


def finish(diag_own, x_t, square, diag_square_other):
    cube = dot(jnp.concatenate([diag_own, x_t], axis=1), jnp.concatenate([square, diag_square_other], axis=0))
    return (3.0 * square.astype(F32) - 2.0 * cube).astype(BF16)


def flipped(flag, block):
    return masked(flag, block).T


def inside_kernel(
    cols, blocks, diag_t, left_t, square_t, diag_square_t, off_a, off_b,
    out, send_a, send_b, far_left, far_right, local_out, sem,
):
    rows = blocks.shape[0]
    edges = local_edges(rows)
    far_slots, _, bases = places(rows)
    for at, send in ((1, send_b), (0, send_a)):
        for e in range(GX):
            send[e] = diag_square_t[bases[at] + e]
    copies = []
    for slot, place in ((2, 1), (4, 2), (1, 0), (5, 3)):
        own = [edge for edge in edges if edge[2] == place]
        first, last = (0, rows - 1) if abs(slot - CENTER) == 1 else (own[0][0], own[-1][0])

        def load(edge):
            j, _, _, k = edge
            return diag_t[j], left_t[place, j], square_t[place, j], diag_square_t[k]

        in_groups(own, load, finish, lambda edge, value: local_out.__setitem__((place, edge[0]), value))
        inside = [edge[0] for edge in own]
        for j in range(first, last + 1):
            if j not in inside:
                local_out[place, j] = jnp.zeros_like(diag_t[j])
        at = pl.ds(first, last + 1 - first)
        copies.append(pltpu.make_async_copy(local_out.at[place, at], out.at[at, slot], sem.at[place]))
        copies[-1].start()
    for at, off in enumerate((off_a, off_b)):
        slot = far_slots[at]
        in_groups(
            list(range(rows)),
            lambda j: (cols[j, slot] >= 0, off[j]),
            flipped,
            lambda j, value: far_left.__setitem__((at, j), value),
        )
        in_groups(
            list(range(rows)),
            lambda j: (cols[j, slot] >= 0, blocks[j, slot]),
            flipped,
            lambda j, value: far_right.__setitem__((at, j), value),
        )
    for copy in copies:
        copy.wait()


def far_kernel(
    diag_t, cube_t, diag_square_t, far_left, far_right, diag_a, diag_b, old,
    out, far_square, far_other, diag_out, sem,
):
    rows = diag_t.shape[0]
    for diag, at in ((diag_a, 0), (diag_b, 1)):
        in_groups(
            list(range(rows)),
            lambda j: (diag_t[j], far_left[at, j], diag[j]),
            one_square,
            lambda j, value: far_square.__setitem__((at, j), value),
        )
        in_groups(
            list(range(rows)),
            lambda j: (diag[j], far_right[at, j], diag_t[j]),
            one_square,
            lambda j, value: far_other.__setitem__((at, j), value),
        )

    def load(j):
        lhs = jnp.concatenate([diag_t[j], far_left[0, j], far_left[1, j]], axis=1)
        rhs = jnp.concatenate([diag_square_t[j], far_other[0, j], far_other[1, j]], axis=0)
        return lhs, rhs, cube_t[j], diag_square_t[j]

    def last(lhs, rhs, extra, square):
        return (3.0 * square.astype(F32) - 2.0 * (dot(lhs, rhs) + extra)).astype(BF16)

    in_groups(list(range(rows)), load, last, diag_out.__setitem__)
    copy = pltpu.make_async_copy(diag_out, out.at[:, CENTER], sem)
    copy.start()
    copy.wait()


def near_last_kernel(diag_t, near_left, near_square, near_a, near_b, old, out, near_out, sem):
    _, near_slots, bases = places(diag_t.shape[0])
    copies = []
    for side, near in enumerate((near_a, near_b)):
        base = bases[side]
        in_groups(
            list(range(GX)),
            lambda e: (diag_t[base + e], near_left[side, e], near_square[side, e], near[e]),
            finish,
            lambda e, value: near_out.__setitem__((side, e), value),
        )
        target = out.at[pl.ds(base, GX), near_slots[side]]
        copies.append(pltpu.make_async_copy(near_out.at[side], target, sem.at[side]))
        copies[-1].start()
    for copy in copies:
        copy.wait()


def far_last_kernel(diag_t, far_left, far_square, far_a, far_b, old, out, far_out, sem):
    rows = diag_t.shape[0]
    far_slots, _, _ = places(rows)
    copies = []
    for side, far in enumerate((far_a, far_b)):
        in_groups(
            list(range(rows)),
            lambda j: (diag_t[j], far_left[side, j], far_square[side, j], far[j]),
            finish,
            lambda j, value: far_out.__setitem__((side, j), value),
        )
        copies.append(pltpu.make_async_copy(far_out.at[side], out.at[:, far_slots[side]], sem.at[side]))
        copies[-1].start()
    for copy in copies:
        copy.wait()


def on_device(density, block_cols):
    rows, _, size, _ = density.shape
    layer_dist = PLANE // rows
    count = lax.axis_size("row")

    def block(*dims):
        return jax.ShapeDtypeStruct((*dims, size, size), BF16)

    def wide(*dims):
        return jax.ShapeDtypeStruct((*dims, size, size), F32)

    def scratch(*dims):
        return pltpu.VMEM((*dims, size, size), BF16)

    dma = pltpu.SemaphoreType.DMA
    smem = pl.BlockSpec(memory_space=pltpu.SMEM)
    vmem = pl.BlockSpec(memory_space=pltpu.VMEM)
    hbm = pl.BlockSpec(memory_space=pltpu.HBM)

    def call(kernel, in_specs, args, outs, out_specs, scratch_shapes, alias=None, vmem_limit=VMEM_LIMIT):
        return pl.pallas_call(
            kernel,
            in_specs=in_specs,
            out_specs=out_specs,
            out_shape=outs,
            scratch_shapes=scratch_shapes,
            input_output_aliases={} if alias is None else {alias: 0},
            compiler_params=pltpu.CompilerParams(vmem_limit_bytes=vmem_limit),
            cost_estimate=pl.CostEstimate(flops=0, bytes_accessed=KERNEL_COST, transcendentals=0),
        )(*args)

    def far(value, pairing):
        return matching(value, pairing, layer_dist, count)

    def near(value, pairing):
        return matching(value, pairing, 1, layer_dist)

    diag_t, send_a, send_b, strip_a, strip_b = call(
        stage_kernel,
        [hbm],
        [density],
        [block(rows), block(rows), block(rows), block(2 * GX), block(2 * GX)],
        [vmem] * 5,
        [scratch(rows), dma((5,))],
        vmem_limit=STAGE_LIMIT,
    )
    off_b = far(send_b, 1)
    off_a = far(send_a, 0)
    diag_b = far(diag_t, 1)
    diag_a = far(diag_t, 0)
    near_b = near(strip_b, 1)
    near_a = near(strip_a, 0)
    left_t, square_t, cube_t, near_left, near_square, total = call(
        local_kernel,
        [smem] + [vmem] * 4,
        [block_cols, density, diag_t, near_a, near_b],
        [block(4, rows), block(4, rows), wide(rows), block(2, GX), block(2, GX), wide(rows)],
        [vmem] * 6,
        [scratch(2, GX), scratch(2, GX)],
    )
    diag_square_t = call(
        diag_square_kernel,
        [smem] + [vmem] * 4,
        [block_cols, density, total, off_a, off_b],
        block(rows),
        vmem,
        [],
    )
    far_square_b = far(diag_square_t, 1)
    far_square_a = far(diag_square_t, 0)
    out, square_a, square_b, far_left, far_right = call(
        inside_kernel,
        [smem] + [vmem] * 7,
        [block_cols, density, diag_t, left_t, square_t, diag_square_t, off_a, off_b],
        [block(rows, K), block(GX), block(GX), block(2, rows), block(2, rows)],
        [hbm] + [vmem] * 4,
        [scratch(4, rows), dma((4,))],
    )
    near_square_b = near(square_b, 1)
    near_square_a = near(square_a, 0)
    out, far_square = call(
        far_kernel,
        [vmem] * 7 + [hbm],
        [diag_t, cube_t, diag_square_t, far_left, far_right, diag_a, diag_b, out],
        [block(rows, K), block(2, rows)],
        [hbm, vmem],
        [scratch(2, rows), scratch(rows), dma],
        alias=7,
    )
    out = call(
        near_last_kernel,
        [vmem] * 5 + [hbm],
        [diag_t, near_left, near_square, near_square_a, near_square_b, out],
        block(rows, K),
        hbm,
        [scratch(2, GX), dma((2,))],
        alias=5,
    )
    return call(
        far_last_kernel,
        [vmem] * 5 + [hbm],
        [diag_t, far_left, far_square, far_square_a, far_square_b, out],
        block(rows, K),
        hbm,
        [scratch(2, rows), dma((2,))],
        alias=5,
    )


def solution(mesh):
    placed = (P(("groups", "row"), None, None, None), P(("groups", "row"), None))
    return jax.shard_map(
        on_device,
        mesh=mesh,
        in_specs=placed,
        out_specs=P(("groups", "row"), None, None, None),
        check_vma=False,
    )
```

time: 386 us -> 46.7 us (0.12)
  the two profiles are of different devices: /device:TPU:0 before, /device:TPU:11 now
where the time goes in v2:
time: 46.7 us; the launch traced here: 45.9 us
  starting transfers between devices  17.2 us (37%)
  Pallas kernels  15.5 us (33%)
  waiting for transfers between devices  9.91 us (21%)
  local copies, waits for them, and re-layouts  3.17 us (7%)
    ppermute x10, starting transfers between devices, matching(): return lax.ppermute(value, 'row', pairs)  17.2 us
    pallas_call x7, Pallas kernels, call(): pl.pallas_call(kernel, in_specs=in_specs, out_specs=out_specs, out_shape=...  15.5 us
    ppermute x10, waiting for transfers between devices, matching(): return lax.ppermute(value, 'row', pairs)  9.91 us
    unnamed x9, local copies, waits for them, and re-layouts  3.17 us
  transfers between devices with their start and end apart: 10, of which 6 were waited for; matrix products, arithmetic and copies ran while one was open for 0% of the time, Pallas kernels for 24%

profile of v2, /device:TPU:11, one launch (start us, length us, event | category | flops | bytes accessed | tf_op | source)
XLA Modules:
  0.0 45.9 jit_solution(6386978806242741432)
XLA Ops:
  0.0 3.1 %shard_map.28 = (bf16[16,128,128]{2,1,0:T(8,128)(2,1)}, bf16[16,128,128]{2,1,0:T(8,128)(2,1)}, bf16[16,128,128]{2,1,0:T(8,128)(2,1)}, bf16[16,128,128]{2,1,0:T(8,128)(2,1)}, bf16[16,128,128]{2,1,0:T(8,128)(2,1)}) custom-call(bf16[16,7,128,128]{3,2,1,0:T(8,128)(2,1)} %blocks.7), custom_call_target="tpu_custom_call" | custom-call | bytes 1000 | tf_op jit(solution)/shard_map/pallas_call | solution.py:338
  3.1 0.7 %collective-permute-start = (bf16[16,128,128]{2,1,0:T(8,128)(2,1)}, bf16[16,128,128]{2,1,0:T(8,128)(2,1)S(1)}, u32[]{:S(2)}, u32[]{:S(2)}) collective-permute-start(bf16[16,128,128]{2,1,0:T(8,128)(2,1)} %get-tuple-element.24), channel_id=1, source_target_pairs={{0,1},{1,0},{2,3},{3,2},{4,5},{5,4},{6,7},{7,6},{8,9},{9,8},{10,11... | collective-permute-start | bytes 1572872 | tf_op jit(solution)/shard_map/ppermute | solution.py:28
  3.8 3.0 %collective-permute-start.1 = (bf16[16,128,128]{2,1,0:T(8,128)(2,1)}, bf16[16,128,128]{2,1,0:T(8,128)(2,1)S(1)}, u32[]{:S(2)}, u32[]{:S(2)}) collective-permute-start(bf16[16,128,128]{2,1,0:T(8,128)(2,1)} %get-tuple-element.25), channel_id=1, source_target_pairs={{1,2},{2,1},{5,6},{6,5},{9,10},{10,9},{13,14},{14,13},{17,18},{18,... | collective-permute-start | bytes 1572872 | tf_op jit(solution)/shard_map/ppermute | solution.py:28
  6.9 0.2 collective-permute-start.2
  7.1 4.3 %collective-permute-start.3 = (bf16[16,128,128]{2,1,0:T(8,128)(2,1)}, bf16[16,128,128]{2,1,0:T(8,128)(2,1)S(1)}, u32[]{:S(2)}, u32[]{:S(2)}) collective-permute-start(bf16[16,128,128]{2,1,0:T(8,128)(2,1)} %get-tuple-element.30), channel_id=1, source_target_pairs={{4,8},{5,9},{6,10},{7,11},{8,4},{9,5},{10,6},{11,7},{20,24},{21,25... | collective-permute-start | bytes 1572872 | tf_op jit(solution)/shard_map/ppermute | solution.py:28
  11.4 0.1 collective-permute-start.4
  11.5 0.0 collective-permute-done.near_a
  11.5 1.9 %collective-permute-start.5 = (bf16[16,128,128]{2,1,0:T(8,128)(2,1)}, bf16[16,128,128]{2,1,0:T(8,128)(2,1)S(1)}, u32[]{:S(2)}, u32[]{:S(2)}) collective-permute-start(bf16[16,128,128]{2,1,0:T(8,128)(2,1)} %get-tuple-element.23.diag_t), channel_id=1, source_target_pairs={{4,8},{5,9},{6,10},{7,11},{8,4},{9,5},{10,6},{11,7},{20,24},{21,25... | collective-permute-start | bytes 1572872 | tf_op jit(solution)/shard_map/ppermute | solution.py:28
  13.5 0.0 copy-done.3
  13.5 0.1 copy.8.cols
  13.5 1.3 %collective-permute-done.1.near_b = bf16[16,128,128]{2,1,0:T(8,128)(2,1)S(1)} collective-permute-done((bf16[16,128,128]{2,1,0:T(8,128)(2,1)}, bf16[16,128,128]{2,1,0:T(8,128)(2,1)S(1)}, u32[]{:S(2)}, u32[]{:S(2)}) %collective-permute-start.1) | collective-permute-done | bytes 524320 | tf_op jit(solution)/shard_map/ppermute | solution.py:28
  14.8 2.0 %copy-done = bf16[16,7,128,128]{3,2,1,0:T(8,128)(2,1)S(1)} copy-done((bf16[16,7,128,128]{3,2,1,0:T(8,128)(2,1)S(1)}, bf16[16,7,128,128]{3,2,1,0:T(8,128)(2,1)}, u32[]{:S(2)}) %copy-start) | copy-done | bytes 3670040
  16.9 1.0 %copy-done.1 = bf16[16,128,128]{2,1,0:T(8,128)(2,1)S(1)} copy-done((bf16[16,128,128]{2,1,0:T(8,128)(2,1)S(1)}, bf16[16,128,128]{2,1,0:T(8,128)(2,1)}, u32[]{:S(2)}) %copy-start.1) | copy-done | bytes 524312
  17.9 3.5 %shard_map.29 = (bf16[4,16,128,128]{3,2,1,0:T(8,128)(2,1)S(1)}, bf16[4,16,128,128]{3,2,1,0:T(8,128)(2,1)S(1)}, f32[16,128,128]{2,1,0:T(8,128)S(1)}, bf16[2,8,128...) custom-call(s32[16,7]{1,0:T(8,128)S(1)} %copy.8.cols, ...), custom_call_target="tpu_custom_call" | custom-call | bytes 1000 | tf_op jit(solution)/shard_map/pallas_call | solution.py:338
  21.4 0.0 copy-start.2
  21.4 0.0 collective-permute-done.2.far_a.off_a
  21.4 2.8 %collective-permute-done.3.far_b.off_b = bf16[16,128,128]{2,1,0:T(8,128)(2,1)S(1)} collective-permute-done((bf16[16,128,128]{2,1,0:T(8,128)(2,1)}, bf16[16,128,128]{2,1,0:T(8,128)(2,1)S(1)}, u32[]{:S(2)}, u32[]{:S(2)}) %collective-permute-start.3) | collective-permute-done | bytes 524320 | tf_op jit(solution)/shard_map/ppermute | solution.py:28
  24.2 1.2 %shard_map.30.diag_square_t = bf16[16,128,128]{2,1,0:T(8,128)(2,1)S(1)} custom-call(s32[16,7]{1,0:T(8,128)S(1)} %copy.8.cols, bf16[16,7,128,128]{3,2,1,0:T(8,128)(2,1)S(1)} %copy-done, f32[16,128,128]{2,1,0:T(8,128)S(1)} %get-tuple-element.28.total, bf16[16,128,128]{2,1,0:T(8,128)(2,1)S(1)} %collective-permute-done.2.far_a.off_a, ...), custom_call_target="tpu_custom_call" | custom-call | bytes 1000 | tf_op jit(solution)/shard_map/pallas_call | solution.py:338
  25.4 0.1 collective-permute-start.6
  25.4 3.4 %collective-permute-start.7 = (bf16[16,128,128]{2,1,0:T(8,128)(2,1)S(1)}, bf16[16,128,128]{2,1,0:T(8,128)(2,1)S(1)}, u32[]{:S(2)}, u32[]{:S(2)}) collective-permute-start(bf16[16,128,128]{2,1,0:T(8,128)(2,1)S(1)} %shard_map.30.diag_square_t), channel_id=1, source_target_pairs={{4,8},{5,9},{6,10},{7,11},{8,4},{9,5},{10,6},{11,7},{20,24},{21,25... | collective-permute-start | bytes 1572872 | tf_op jit(solution)/shard_map/ppermute | solution.py:28
  28.8 2.6 %shard_map.31 = (bf16[16,7,128,128]{3,2,1,0:T(8,128)(2,1)}, bf16[8,128,128]{2,1,0:T(8,128)(2,1)S(1)}, bf16[8,128,128]{2,1,0:T(8,128)(2,1)S(1)}, bf16[2,16,128,12...) custom-call(s32[16,7]{1,0:T(8,128)S(1)} %copy.8.cols, bf16[16,7,128,128]{3,2,1,0:T(8,128)(2,1)S(1)} %copy-done, ...), custom_call_target="tpu_custom_call" | custom-call | bytes 1000 | tf_op jit(solution)/shard_map/pallas_call | solution.py:338
  31.4 0.1 collective-permute-start.8
  31.5 0.9 %collective-permute-done.4.diag_a = bf16[16,128,128]{2,1,0:T(8,128)(2,1)S(1)} collective-permute-done((bf16[16,128,128]{2,1,0:T(8,128)(2,1)}, bf16[16,128,128]{2,1,0:T(8,128)(2,1)S(1)}, u32[]{:S(2)}, u32[]{:S(2)}) %collective-permute-start.4) | collective-permute-done | bytes 524320 | tf_op jit(solution)/shard_map/ppermute | solution.py:28
  32.4 3.3 %collective-permute-start.9 = (bf16[8,128,128]{2,1,0:T(8,128)(2,1)S(1)}, bf16[8,128,128]{2,1,0:T(8,128)(2,1)S(1)}, u32[]{:S(2)}, u32[]{:S(2)}) collective-permute-start(bf16[8,128,128]{2,1,0:T(8,128)(2,1)S(1)} %get-tuple-element.39), channel_id=1, source_target_pairs={{1,2},{2,1},{5,6},{6,5},{9,10},{10,9},{13,14},{14,13},{17,18},{18,... | collective-permute-start | bytes 786440 | tf_op jit(solution)/shard_map/ppermute | solution.py:28
  35.8 0.0 collective-permute-done.5.diag_b
  35.8 2.5 %shard_map.32 = (bf16[16,7,128,128]{3,2,1,0:T(8,128)(2,1)}, bf16[2,16,128,128]{3,2,1,0:T(8,128)(2,1)S(1)}) custom-call(bf16[16,128,128]{2,1,0:T(8,128)(2,1)S(1)} %copy-done.2, f32[16,128,128]{2,1,0:T(8,128)S(1)} %get-tuple-element.32.cube_t, bf16[16,128,128]{2,1,0:T(8,128)(2,1)S(1)} %shard_map.30.diag_square_t, ...), custom_call_target="tpu_custom_call", output_to_operand_aliasing={{0}: (7, {})} | custom-call | bytes 1000 | tf_op jit(solution)/shard_map/pallas_call | solution.py:338
  38.3 0.0 collective-permute-done.8.near_a
  38.3 2.1 %collective-permute-done.9.near_b = bf16[8,128,128]{2,1,0:T(8,128)(2,1)S(1)} collective-permute-done((bf16[8,128,128]{2,1,0:T(8,128)(2,1)S(1)}, bf16[8,128,128]{2,1,0:T(8,128)(2,1)S(1)}, u32[]{:S(2)}, u32[]{:S(2)}) %collective-permute-start.9) | collective-permute-done | bytes 262176 | tf_op jit(solution)/shard_map/ppermute | solution.py:28
  40.4 1.1 %shard_map.33.old = bf16[16,7,128,128]{3,2,1,0:T(8,128)(2,1)} custom-call(bf16[16,128,128]{2,1,0:T(8,128)(2,1)S(1)} %copy-done.2, bf16[2,8,128,128]{3,2,1,0:T(8,128)(2,1)S(1)} %get-tuple-element.36.near_left, bf16[2,8,128,128]{3,2,1,0:T(8,128)(2,1)S(1)} %get-tuple-element.37.near_square, ...), custom_call_target="tpu_custom_call", output_to_operand_aliasing={{}: (5, {})} | custom-call | bytes 1000 | tf_op jit(solution)/shard_map/pallas_call | solution.py:338
  41.5 0.2 collective-permute-done.6.far_a
  41.7 2.7 %collective-permute-done.7.far_b = bf16[16,128,128]{2,1,0:T(8,128)(2,1)S(1)} collective-permute-done((bf16[16,128,128]{2,1,0:T(8,128)(2,1)S(1)}, bf16[16,128,128]{2,1,0:T(8,128)(2,1)S(1)}, u32[]{:S(2)}, u32[]{:S(2)}) %collective-permute-start.7) | collective-permute-done | bytes 524320 | tf_op jit(solution)/shard_map/ppermute | solution.py:28
  44.4 1.5 %shard_map.34 = bf16[16,7,128,128]{3,2,1,0:T(8,128)(2,1)} custom-call(bf16[16,128,128]{2,1,0:T(8,128)(2,1)S(1)} %copy-done.2, bf16[2,16,128,128]{3,2,1,0:T(8,128)(2,1)S(1)} %get-tuple-element.31.far_left, bf16[2,16,128,128]{3,2,1,0:T(8,128)(2,1)S(1)} %get-tuple-element.35.far_square, ...), custom_call_target="tpu_custom_call", output_to_operand_aliasing={{}: (5, {})} | custom-call | bytes 1000 | tf_op jit(solution)/shard_map/pallas_call | solution.py:338
  (4 shorter events, 0.0 us)
Async XLA Ops:
  0.0 13.5 %copy-start.3 = (s32[16,7]{0,1:T(8,128)S(1)}, s32[16,7]{0,1:T(8,128)}, u32[]{:S(2)}) copy-start(s32[16,7]{0,1:T(8,128)} %param.3) | copy-start | bytes 1348
  3.1 8.4 %collective-permute-start = (bf16[16,128,128]{2,1,0:T(8,128)(2,1)}, bf16[16,128,128]{2,1,0:T(8,128)(2,1)S(1)}, u32[]{:S(2)}, u32[]{:S(2)}) collective-permute-start(bf16[16,128,128]{2,1,0:T(8,128)(2,1)} %get-tuple-element.24), channel_id=1, source_target_pairs={{0,1},{1,0},{2,3},{3,2},{4,5},{5,4},{6,7},{7,6},{8,9},{9,8},{10,11... | collective-permute-start | bytes 1572872 | tf_op jit(solution)/shard_map/ppermute | solution.py:28
  3.8 11.0 %collective-permute-start.1 = (bf16[16,128,128]{2,1,0:T(8,128)(2,1)}, bf16[16,128,128]{2,1,0:T(8,128)(2,1)S(1)}, u32[]{:S(2)}, u32[]{:S(2)}) collective-permute-start(bf16[16,128,128]{2,1,0:T(8,128)(2,1)} %get-tuple-element.25), channel_id=1, source_target_pairs={{1,2},{2,1},{5,6},{6,5},{9,10},{10,9},{13,14},{14,13},{17,18},{18,... | collective-permute-start | bytes 1572872 | tf_op jit(solution)/shard_map/ppermute | solution.py:28
  6.9 14.5 %collective-permute-start.2 = (bf16[16,128,128]{2,1,0:T(8,128)(2,1)}, bf16[16,128,128]{2,1,0:T(8,128)(2,1)S(1)}, u32[]{:S(2)}, u32[]{:S(2)}) collective-permute-start(bf16[16,128,128]{2,1,0:T(8,128)(2,1)} %get-tuple-element.29), channel_id=1, source_target_pairs={{0,4},{1,5},{2,6},{3,7},{4,0},{5,1},{6,2},{7,3},{8,12},{9,13},{10,... | collective-permute-start | bytes 1572872 | tf_op jit(solution)/shard_map/ppermute | solution.py:28
  7.1 17.1 %collective-permute-start.3 = (bf16[16,128,128]{2,1,0:T(8,128)(2,1)}, bf16[16,128,128]{2,1,0:T(8,128)(2,1)S(1)}, u32[]{:S(2)}, u32[]{:S(2)}) collective-permute-start(bf16[16,128,128]{2,1,0:T(8,128)(2,1)} %get-tuple-element.30), channel_id=1, source_target_pairs={{4,8},{5,9},{6,10},{7,11},{8,4},{9,5},{10,6},{11,7},{20,24},{21,25... | collective-permute-start | bytes 1572872 | tf_op jit(solution)/shard_map/ppermute | solution.py:28
  11.4 21.0 %collective-permute-start.4 = (bf16[16,128,128]{2,1,0:T(8,128)(2,1)}, bf16[16,128,128]{2,1,0:T(8,128)(2,1)S(1)}, u32[]{:S(2)}, u32[]{:S(2)}) collective-permute-start(bf16[16,128,128]{2,1,0:T(8,128)(2,1)} %get-tuple-element.23.diag_t), channel_id=1, source_target_pairs={{0,4},{1,5},{2,6},{3,7},{4,0},{5,1},{6,2},{7,3},{8,12},{9,13},{10,... | collective-permute-start | bytes 1572872 | tf_op jit(solution)/shard_map/ppermute | solution.py:28
  11.5 24.2 %collective-permute-start.5 = (bf16[16,128,128]{2,1,0:T(8,128)(2,1)}, bf16[16,128,128]{2,1,0:T(8,128)(2,1)S(1)}, u32[]{:S(2)}, u32[]{:S(2)}) collective-permute-start(bf16[16,128,128]{2,1,0:T(8,128)(2,1)} %get-tuple-element.23.diag_t), channel_id=1, source_target_pairs={{4,8},{5,9},{6,10},{7,11},{8,4},{9,5},{10,6},{11,7},{20,24},{21,25... | collective-permute-start | bytes 1572872 | tf_op jit(solution)/shard_map/ppermute | solution.py:28
  14.8 2.0 %copy-start = (bf16[16,7,128,128]{3,2,1,0:T(8,128)(2,1)S(1)}, bf16[16,7,128,128]{3,2,1,0:T(8,128)(2,1)}, u32[]{:S(2)}) copy-start(bf16[16,7,128,128]{3,2,1,0:T(8,128)(2,1)} %blocks.7) | copy-start | bytes 11010052
  16.9 1.0 %copy-start.1 = (bf16[16,128,128]{2,1,0:T(8,128)(2,1)S(1)}, bf16[16,128,128]{2,1,0:T(8,128)(2,1)}, u32[]{:S(2)}) copy-start(bf16[16,128,128]{2,1,0:T(8,128)(2,1)} %get-tuple-element.23.diag_t) | copy-start | bytes 1572868
  21.4 7.4 %copy-start.2 = (bf16[16,128,128]{2,1,0:T(8,128)(2,1)S(1)}, bf16[16,128,128]{2,1,0:T(8,128)(2,1)}, u32[]{:S(2)}) copy-start(bf16[16,128,128]{2,1,0:T(8,128)(2,1)} %get-tuple-element.23.diag_t) | copy-start | bytes 1572868
  25.4 16.3 %collective-permute-start.6 = (bf16[16,128,128]{2,1,0:T(8,128)(2,1)S(1)}, bf16[16,128,128]{2,1,0:T(8,128)(2,1)S(1)}, u32[]{:S(2)}, u32[]{:S(2)}) collective-permute-start(bf16[16,128,128]{2,1,0:T(8,128)(2,1)S(1)} %shard_map.30.diag_square_t), channel_id=1, source_target_pairs={{0,4},{1,5},{2,6},{3,7},{4,0},{5,1},{6,2},{7,3},{8,12},{9,13},{10,... | collective-permute-start | bytes 1572872 | tf_op jit(solution)/shard_map/ppermute | solution.py:28
  25.4 19.0 %collective-permute-start.7 = (bf16[16,128,128]{2,1,0:T(8,128)(2,1)S(1)}, bf16[16,128,128]{2,1,0:T(8,128)(2,1)S(1)}, u32[]{:S(2)}, u32[]{:S(2)}) collective-permute-start(bf16[16,128,128]{2,1,0:T(8,128)(2,1)S(1)} %shard_map.30.diag_square_t), channel_id=1, source_target_pairs={{4,8},{5,9},{6,10},{7,11},{8,4},{9,5},{10,6},{11,7},{20,24},{21,25... | collective-permute-start | bytes 1572872 | tf_op jit(solution)/shard_map/ppermute | solution.py:28
  31.4 6.8 %collective-permute-start.8 = (bf16[8,128,128]{2,1,0:T(8,128)(2,1)S(1)}, bf16[8,128,128]{2,1,0:T(8,128)(2,1)S(1)}, u32[]{:S(2)}, u32[]{:S(2)}) collective-permute-start(bf16[8,128,128]{2,1,0:T(8,128)(2,1)S(1)} %get-tuple-element.38), channel_id=1, source_target_pairs={{0,1},{1,0},{2,3},{3,2},{4,5},{5,4},{6,7},{7,6},{8,9},{9,8},{10,11... | collective-permute-start | bytes 786440 | tf_op jit(solution)/shard_map/ppermute | solution.py:28
  32.4 8.0 %collective-permute-start.9 = (bf16[8,128,128]{2,1,0:T(8,128)(2,1)S(1)}, bf16[8,128,128]{2,1,0:T(8,128)(2,1)S(1)}, u32[]{:S(2)}, u32[]{:S(2)}) collective-permute-start(bf16[8,128,128]{2,1,0:T(8,128)(2,1)S(1)} %get-tuple-element.39), channel_id=1, source_target_pairs={{1,2},{2,1},{5,6},{6,5},{9,10},{10,9},{13,14},{14,13},{17,18},{18,... | collective-permute-start | bytes 786440 | tf_op jit(solution)/shard_map/ppermute | solution.py:28

commit v3 on v2

--- a/solution.py
+++ b/solution.py
@@ -1,3 +1,5 @@
+import functools
+
 import jax
 import jax.numpy as jnp
 from jax import lax
@@ -12,20 +14,26 @@
 BF16 = jnp.bfloat16
 F32 = jnp.float32
 VMEM_LIMIT = 12 * 1024 * 1024
+STAGE_LIMIT = 50 * 1024 * 1024
 KERNEL_COST = 1000
-STAGE_LIMIT = 58 * 1024 * 1024
-
-
-def matching(value, parity, distance, period):
-    count = lax.axis_size("row")
+
+
+def far_pairs(pairing, layer_dist, count):
     pairs = []
     for source in range(count):
-        place = source % period // distance
-        step = distance if place % 2 == parity else -distance
-        target = source + step
-        if 0 <= target < count and target // period == source // period:
-            pairs.append((source, target))
-    return lax.ppermute(value, "row", pairs)
+        step = layer_dist if (source // layer_dist + pairing) % 2 == 0 else -layer_dist
+        if 0 <= source + step < count:
+            pairs.append((source, source + step))
+    return pairs
+
+
+def near_pairs(pairing, layer_dist, count):
+    pairs = []
+    for source in range(count):
+        step = 1 if (source % layer_dist + pairing) % 2 == 0 else -1
+        if (source + step) // layer_dist == source // layer_dist:
+            pairs.append((source, source + step))
+    return pairs
 
 
 def dot(a, b):
@@ -58,45 +66,44 @@
 def places(rows):
     row_id = lax.axis_index("row")
     layer_dist = PLANE // rows
+    strip = row_id % layer_dist
     far_slot = jnp.where(row_id // layer_dist % 2 == 0, K - 1, 0)
-    even = row_id % layer_dist % 2 == 0
+    even = strip % 2 == 0
     near_slot = jnp.where(even, CENTER + 2, CENTER - 2)
     near_base = jnp.where(even, rows - GX, 0)
     return (far_slot, K - 1 - far_slot), (near_slot, K - 1 - near_slot), (near_base, rows - GX - near_base)
 
 
-def stage_kernel(blocks, diag_t, send_a, send_b, strip_a, strip_b, diag, sem):
+def stage_kernel(blocks, send_a, send_b, strip_a, strip_b, sem):
     rows = blocks.shape[0]
     far_slots, near_slots, bases = places(rows)
-    copies = [pltpu.make_async_copy(blocks.at[:, CENTER], diag, sem.at[0])]
-    for at, send in ((1, send_b), (0, send_a)):
-        copies.append(pltpu.make_async_copy(blocks.at[:, far_slots[at]], send, sem.at[1 + at]))
-    for at, strip in ((1, strip_b), (0, strip_a)):
-        source = blocks.at[pl.ds(bases[at], GX), near_slots[at]]
-        copies.append(pltpu.make_async_copy(source, strip.at[pl.ds(0, GX)], sem.at[3 + at]))
+    copies = []
+    for at, send in ((0, send_a), (1, send_b)):
+        copies.append(pltpu.make_async_copy(blocks.at[:, far_slots[at]], send, sem.at[at]))
+    for at, strip in ((0, strip_a), (1, strip_b)):
+        at_rows = pl.ds(bases[at], GX)
+        for half, slot in enumerate((near_slots[at], CENTER)):
+            part = strip.at[pl.ds(half * GX, GX)]
+            copies.append(pltpu.make_async_copy(blocks.at[at_rows, slot], part, sem.at[2 + 2 * at + half]))
     for copy in copies:
         copy.start()
-    copies[0].wait()
-    in_groups(list(range(rows)), lambda j: (diag[j],), lambda x: x.T, diag_t.__setitem__)
-    for at, strip in ((1, strip_b), (0, strip_a)):
-        for e in range(GX):
-            strip[GX + e] = diag_t[bases[at] + e]
-    for copy in copies[1:]:
+    for copy in copies:
         copy.wait()
 
 
 def local_kernel(
-    cols, blocks, diag_t, near_a, near_b,
-    left_t, square_t, cube_t, near_left, near_square, total, near_right, near_other,
+    cols, blocks, near_a, near_b, strip_a, strip_b,
+    diag_t, left_t, square_t, cube_t, near_left, near_square, total, near_diag, near_right, near_other,
 ):
-    rows = blocks.shape[0]
+    rows = diag_t.shape[0]
+    in_groups(list(range(rows)), lambda j: (blocks[j, CENTER],), lambda x: x.T, diag_t.__setitem__)
     edges = local_edges(rows)
     _, near_slots, bases = places(rows)
     strip = list(range(GX))
 
     def load(edge):
         j, slot, place, k = edge
-        return cols[j, slot] >= 0, blocks[k, K - 1 - slot], diag_t[j], diag_t[k]
+        return cols[slot, j] >= 0, blocks[k, K - 1 - slot], diag_t[j], diag_t[k]
 
     def compute(flag, x, diag_own, diag_other):
         x_t = flipped(flag, x)
@@ -106,30 +113,32 @@
         j, slot, place, k = edge
         left_t[place, j], square_t[place, j] = result
 
-    in_groups(edges, load, compute, store)
     if rows != 2 * GX:
         total[...] = jnp.zeros_like(total)
         cube_t[...] = jnp.zeros_like(cube_t)
-    for side, near in enumerate((near_a, near_b)):
+    for side, (near, own) in enumerate(((near_a, strip_a), (near_b, strip_b))):
         slot, base = near_slots[side], bases[side]
 
         def load_left(e):
-            return cols[base + e, slot] >= 0, near[e]
+            return cols[slot, base + e] >= 0, near[e]
 
         def load_right(e):
-            return cols[base + e, slot] >= 0, blocks[base + e, slot]
-
+            return cols[slot, base + e] >= 0, own[e]
+
+        in_groups(
+            strip, lambda e: (near[GX + e],), lambda x: x.T, lambda e, value: near_diag.__setitem__((side, e), value)
+        )
         in_groups(strip, load_left, flipped, lambda e, value: near_left.__setitem__((side, e), value))
         in_groups(strip, load_right, flipped, lambda e, value: near_right.__setitem__((side, e), value))
         in_groups(
             strip,
-            lambda e: (diag_t[base + e], near_left[side, e], near[GX + e]),
+            lambda e: (diag_t[base + e], near_left[side, e], near_diag[side, e]),
             one_square,
             lambda e, value: near_square.__setitem__((side, e), value),
         )
         in_groups(
             strip,
-            lambda e: (near[GX + e], near_right[side, e], diag_t[base + e]),
+            lambda e: (near_diag[side, e], near_right[side, e], diag_t[base + e]),
             one_square,
             lambda e, value: near_other.__setitem__((side, e), value),
         )
@@ -147,6 +156,8 @@
                 ref[j] = value if rows == 2 * GX else ref[j] + value
 
         in_groups(strip, load_near, near_terms, store_near)
+
+    in_groups(edges, load, compute, store)
 
     def load_row(j):
         own = [edge for edge in edges if edge[0] == j]
@@ -171,12 +182,12 @@
     in_groups(list(range(rows)), load_row, row_terms, store_row)
 
 
-def diag_square_kernel(cols, blocks, total, far_a, far_b, square_t):
-    rows = blocks.shape[0]
+def diag_square_kernel(cols, own_a, own_b, total, far_a, far_b, square_t):
+    rows = total.shape[0]
     far_slots, _, _ = places(rows)
 
     def load(j):
-        own = [masked(cols[j, slot] >= 0, blocks[j, slot]) for slot in far_slots]
+        own = [masked(cols[slot, j] >= 0, own[j]) for slot, own in zip(far_slots, (own_a, own_b))]
         return jnp.concatenate(own, axis=1), jnp.concatenate([far_a[j], far_b[j]], axis=0), total[j]
 
     in_groups(
@@ -203,10 +214,10 @@
 
 
 def inside_kernel(
-    cols, blocks, diag_t, left_t, square_t, diag_square_t, off_a, off_b,
+    cols, own_a, own_b, diag_t, left_t, square_t, diag_square_t, off_a, off_b,
     out, send_a, send_b, far_left, far_right, local_out, sem,
 ):
-    rows = blocks.shape[0]
+    rows = diag_t.shape[0]
     edges = local_edges(rows)
     far_slots, _, bases = places(rows)
     for at, send in ((1, send_b), (0, send_a)):
@@ -229,17 +240,17 @@
         at = pl.ds(first, last + 1 - first)
         copies.append(pltpu.make_async_copy(local_out.at[place, at], out.at[at, slot], sem.at[place]))
         copies[-1].start()
-    for at, off in enumerate((off_a, off_b)):
+    for at, (off, own) in enumerate(((off_a, own_a), (off_b, own_b))):
         slot = far_slots[at]
         in_groups(
             list(range(rows)),
-            lambda j: (cols[j, slot] >= 0, off[j]),
+            lambda j: (cols[slot, j] >= 0, off[j]),
             flipped,
             lambda j, value: far_left.__setitem__((at, j), value),
         )
         in_groups(
             list(range(rows)),
-            lambda j: (cols[j, slot] >= 0, blocks[j, slot]),
+            lambda j: (cols[slot, j] >= 0, own[j]),
             flipped,
             lambda j, value: far_right.__setitem__((at, j), value),
         )
@@ -298,18 +309,20 @@
         copy.wait()
 
 
-def far_last_kernel(diag_t, far_left, far_square, far_a, far_b, old, out, far_out, sem):
+def far_last_kernel(side, diag_t, far_left, far_square, far, old, out, far_out, sem):
     rows = diag_t.shape[0]
-    far_slots, _, _ = places(rows)
+    slot = places(rows)[0][side]
     copies = []
-    for side, far in enumerate((far_a, far_b)):
-        in_groups(
-            list(range(rows)),
+    for part in range(rows // GX):
+        first = part * GX
+        in_groups(
+            list(range(first, first + GX)),
             lambda j: (diag_t[j], far_left[side, j], far_square[side, j], far[j]),
             finish,
-            lambda j, value: far_out.__setitem__((side, j), value),
-        )
-        copies.append(pltpu.make_async_copy(far_out.at[side], out.at[:, far_slots[side]], sem.at[side]))
+            far_out.__setitem__,
+        )
+        at = pl.ds(first, GX)
+        copies.append(pltpu.make_async_copy(far_out.at[at], out.at[at, slot], sem.at[part]))
         copies[-1].start()
     for copy in copies:
         copy.wait()
@@ -329,6 +342,7 @@
     def scratch(*dims):
         return pltpu.VMEM((*dims, size, size), BF16)
 
+    cols = block_cols.T
     dma = pltpu.SemaphoreType.DMA
     smem = pl.BlockSpec(memory_space=pltpu.SMEM)
     vmem = pl.BlockSpec(memory_space=pltpu.VMEM)
@@ -347,38 +361,38 @@
         )(*args)
 
     def far(value, pairing):
-        return matching(value, pairing, layer_dist, count)
+        return lax.ppermute(value, "row", far_pairs(pairing, layer_dist, count))
 
     def near(value, pairing):
-        return matching(value, pairing, 1, layer_dist)
-
-    diag_t, send_a, send_b, strip_a, strip_b = call(
+        return lax.ppermute(value, "row", near_pairs(pairing, layer_dist, count))
+
+    send_a, send_b, strip_a, strip_b = call(
         stage_kernel,
         [hbm],
         [density],
-        [block(rows), block(rows), block(rows), block(2 * GX), block(2 * GX)],
-        [vmem] * 5,
-        [scratch(rows), dma((5,))],
+        [block(rows), block(rows), block(2 * GX), block(2 * GX)],
+        [vmem] * 4,
+        [dma((6,))],
         vmem_limit=STAGE_LIMIT,
     )
     off_b = far(send_b, 1)
     off_a = far(send_a, 0)
+    near_b = near(strip_b, 1)
+    near_a = near(strip_a, 0)
+    diag_t, left_t, square_t, cube_t, near_left, near_square, total = call(
+        local_kernel,
+        [smem] + [vmem] * 5,
+        [cols, density, near_a, near_b, strip_a, strip_b],
+        [block(rows), block(4, rows), block(4, rows), wide(rows), block(2, GX), block(2, GX), wide(rows)],
+        [vmem] * 7,
+        [scratch(2, GX)] * 3,
+    )
     diag_b = far(diag_t, 1)
     diag_a = far(diag_t, 0)
-    near_b = near(strip_b, 1)
-    near_a = near(strip_a, 0)
-    left_t, square_t, cube_t, near_left, near_square, total = call(
-        local_kernel,
-        [smem] + [vmem] * 4,
-        [block_cols, density, diag_t, near_a, near_b],
-        [block(4, rows), block(4, rows), wide(rows), block(2, GX), block(2, GX), wide(rows)],
-        [vmem] * 6,
-        [scratch(2, GX), scratch(2, GX)],
-    )
     diag_square_t = call(
         diag_square_kernel,
-        [smem] + [vmem] * 4,
-        [block_cols, density, total, off_a, off_b],
+        [smem] + [vmem] * 5,
+        [cols, send_a, send_b, total, off_a, off_b],
         block(rows),
         vmem,
         [],
@@ -387,8 +401,8 @@
     far_square_a = far(diag_square_t, 0)
     out, square_a, square_b, far_left, far_right = call(
         inside_kernel,
-        [smem] + [vmem] * 7,
-        [block_cols, density, diag_t, left_t, square_t, diag_square_t, off_a, off_b],
+        [smem] + [vmem] * 8,
+        [cols, send_a, send_b, diag_t, left_t, square_t, diag_square_t, off_a, off_b],
         [block(rows, K), block(GX), block(GX), block(2, rows), block(2, rows)],
         [hbm] + [vmem] * 4,
         [scratch(4, rows), dma((4,))],
@@ -413,15 +427,17 @@
         [scratch(2, GX), dma((2,))],
         alias=5,
     )
-    return call(
-        far_last_kernel,
-        [vmem] * 5 + [hbm],
-        [diag_t, far_left, far_square, far_square_a, far_square_b, out],
-        block(rows, K),
-        hbm,
-        [scratch(2, rows), dma((2,))],
-        alias=5,
-    )
+    for side, far_diag_square in ((0, far_square_a), (1, far_square_b)):
+        out = call(
+            functools.partial(far_last_kernel, side),
+            [vmem] * 4 + [hbm],
+            [diag_t, far_left, far_square, far_diag_square, out],
+            block(rows, K),
+            hbm,
+            [scratch(rows), dma((rows // GX,))],
+            alias=4,
+        )
+    return out
 
 
 def solution(mesh):

time: 46.7 us -> 44.6 us (0.955)
  local copies, waits for them, and re-layouts: 3.17 us -> 0.01 us
  starting transfers between devices: 17.2 us -> 20 us
  waiting for transfers between devices: 9.91 us -> 8.79 us
  Pallas kernels: 15.5 us -> 15 us
    unnamed x9 -> x4, local copies, waits for them, and re-layouts: 3.17 us -> 0.01 us
    ppermute x10, starting transfers between devices: 17.2 us -> 20 us  [the longest x6 12.5 us: far(): return lax.ppermute(value, 'row', far_pairs(pairing, layer_dist, count))]
    ppermute x10, waiting for transfers between devices: 9.91 us -> 8.79 us  [the longest x4 4.99 us: near(): return lax.ppermute(value, 'row', near_pairs(pairing, layer_dist, count))]
    pallas_call x7 -> x8, Pallas kernels: 15.5 us -> 15 us  [call(): pl.pallas_call(kernel, in_specs=in_specs, out_specs=out_specs, out_shape=...]
  transfers between devices with their start and end apart: 10 -> 10, of which waited for: 6 -> 5; matrix products, arithmetic and copies ran while one was open for 0% -> 0% of each run, Pallas kernels for 24% -> 28%
where the time goes in v3:
time: 44.6 us; the launch traced here: 44 us
  starting transfers between devices  20 us (45%)
  Pallas kernels  15 us (34%)
  waiting for transfers between devices  8.79 us (20%)
    pallas_call x8, Pallas kernels, call(): pl.pallas_call(kernel, in_specs=in_specs, out_specs=out_specs, out_shape=...  15 us
    ppermute x6, starting transfers between devices, far(): return lax.ppermute(value, 'row', far_pairs(pairing, layer_dist, count))  12.5 us
    ppermute x4, starting transfers between devices, near(): return lax.ppermute(value, 'row', near_pairs(pairing, layer_dist, count))  7.46 us
    ppermute x4, waiting for transfers between devices, near(): return lax.ppermute(value, 'row', near_pairs(pairing, layer_dist, count))  4.99 us
    ppermute x6, waiting for transfers between devices, far(): return lax.ppermute(value, 'row', far_pairs(pairing, layer_dist, count))  3.81 us
  transfers between devices with their start and end apart: 10, of which 5 were waited for; matrix products, arithmetic and copies ran while one was open for 0% of the time, Pallas kernels for 28%

profile of v3, /device:TPU:11, one launch (start us, length us, event | category | flops | bytes accessed | tf_op | source)
XLA Modules:
  0.0 44.0 jit_solution(16708050607608224481)
XLA Ops:
  0.0 0.0 copy-start
  0.0 0.0 copy-start.1
  0.0 1.7 %shard_map.28 = (bf16[16,128,128]{2,1,0:T(8,128)(2,1)S(1)}, bf16[16,128,128]{2,1,0:T(8,128)(2,1)S(1)}, bf16[16,128,128]{2,1,0:T(8,128)(2,1)S(1)}, bf16[16,128,128]{2,1,0:T(8,128)(2,1)S(1)}) custom-call(bf16[16,7,128,128]{3,2,1,0:T(8,128)(2,1)} %blocks.3), custom_call_target="tpu_custom_call" | custom-call | bytes 1000 | tf_op jit(solution)/shard_map/pallas_call | solution.py:352
  1.7 0.7 %collective-permute-start = (bf16[16,128,128]{2,1,0:T(8,128)(2,1)S(1)}, bf16[16,128,128]{2,1,0:T(8,128)(2,1)S(1)}, u32[]{:S(2)}, u32[]{:S(2)}) collective-permute-start(bf16[16,128,128]{2,1,0:T(8,128)(2,1)S(1)} %get-tuple-element.23.strip_a), channel_id=1, source_target_pairs={{0,1},{1,0},{2,3},{3,2},{4,5},{5,4},{6,7},{7,6},{8,9},{9,8},{10,11... | collective-permute-start | bytes 1572872 | tf_op jit(solution)/shard_map/ppermute | solution.py:367
  2.5 3.0 %collective-permute-start.1 = (bf16[16,128,128]{2,1,0:T(8,128)(2,1)S(1)}, bf16[16,128,128]{2,1,0:T(8,128)(2,1)S(1)}, u32[]{:S(2)}, u32[]{:S(2)}) collective-permute-start(bf16[16,128,128]{2,1,0:T(8,128)(2,1)S(1)} %get-tuple-element.24.strip_b), channel_id=1, source_target_pairs={{1,2},{2,1},{5,6},{6,5},{9,10},{10,9},{13,14},{14,13},{17,18},{18,... | collective-permute-start | bytes 1572872 | tf_op jit(solution)/shard_map/ppermute | solution.py:367
  5.5 0.2 collective-permute-start.2
  5.7 4.3 %collective-permute-start.3 = (bf16[16,128,128]{2,1,0:T(8,128)(2,1)S(1)}, bf16[16,128,128]{2,1,0:T(8,128)(2,1)S(1)}, u32[]{:S(2)}, u32[]{:S(2)}) collective-permute-start(bf16[16,128,128]{2,1,0:T(8,128)(2,1)S(1)} %get-tuple-element.27.own_b), channel_id=1, source_target_pairs={{4,8},{5,9},{6,10},{7,11},{8,4},{9,5},{10,6},{11,7},{20,24},{21,25... | collective-permute-start | bytes 1572872 | tf_op jit(solution)/shard_map/ppermute | solution.py:364
  10.1 0.0 collective-permute-done.near_a
  10.1 3.2 %collective-permute-done.1.near_b = bf16[16,128,128]{2,1,0:T(8,128)(2,1)S(1)} collective-permute-done((bf16[16,128,128]{2,1,0:T(8,128)(2,1)S(1)}, bf16[16,128,128]{2,1,0:T(8,128)(2,1)S(1)}, u32[]{:S(2)}, u32[]{:S(2)}) %collective-permute-start.1) | collective-permute-done | bytes 524320 | tf_op jit(solution)/shard_map/ppermute | solution.py:367
  13.2 0.0 copy-done
  13.2 0.0 copy-done.1
  13.2 3.7 %shard_map.29 = (bf16[16,128,128]{2,1,0:T(8,128)(2,1)S(1)}, bf16[4,16,128,128]{3,2,1,0:T(8,128)(2,1)S(1)}, bf16[4,16,128,128]{3,2,1,0:T(8,128)(2,1)S(1)}, f32[16...) custom-call(s32[7,16]{1,0:T(8,128)S(1)} %bitcast.1, ...), custom_call_target="tpu_custom_call" | custom-call | bytes 1000 | tf_op jit(solution)/shard_map/pallas_call | solution.py:352
  17.0 0.2 collective-permute-start.4
  17.2 4.3 %collective-permute-start.5 = (bf16[16,128,128]{2,1,0:T(8,128)(2,1)S(1)}, bf16[16,128,128]{2,1,0:T(8,128)(2,1)S(1)}, u32[]{:S(2)}, u32[]{:S(2)}) collective-permute-start(bf16[16,128,128]{2,1,0:T(8,128)(2,1)S(1)} %get-tuple-element.25.diag_t), channel_id=1, source_target_pairs={{4,8},{5,9},{6,10},{7,11},{8,4},{9,5},{10,6},{11,7},{20,24},{21,25... | collective-permute-start | bytes 1572872 | tf_op jit(solution)/shard_map/ppermute | solution.py:364
  21.5 0.0 collective-permute-done.2.far_a.off_a
  21.5 1.1 %collective-permute-done.3.far_b.off_b = bf16[16,128,128]{2,1,0:T(8,128)(2,1)S(1)} collective-permute-done((bf16[16,128,128]{2,1,0:T(8,128)(2,1)S(1)}, bf16[16,128,128]{2,1,0:T(8,128)(2,1)S(1)}, u32[]{:S(2)}, u32[]{:S(2)}) %collective-permute-start.3) | collective-permute-done | bytes 524320 | tf_op jit(solution)/shard_map/ppermute | solution.py:364
  22.6 1.1 %shard_map.30.diag_square_t = bf16[16,128,128]{2,1,0:T(8,128)(2,1)S(1)} custom-call(s32[7,16]{1,0:T(8,128)S(1)} %bitcast.2, bf16[16,128,128]{2,1,0:T(8,128)(2,1)S(1)} %get-tuple-element.26.own_a, bf16[16,128,128]{2,1,0:T(8,128)(2,1)S(1)} %get-tuple-element.27.own_b, f32[16,128,128]{2,1,0:T(8,128)S(1)} %get-tuple-element.30.total, ...), custom_call_target="tpu_custom_call" | custom-call | bytes 1000 | tf_op jit(solution)/shard_map/pallas_call | solution.py:352
  23.7 0.1 collective-permute-start.7
  23.8 3.4 %collective-permute-start.6 = (bf16[16,128,128]{2,1,0:T(8,128)(2,1)S(1)}, bf16[16,128,128]{2,1,0:T(8,128)(2,1)S(1)}, u32[]{:S(2)}, u32[]{:S(2)}) collective-permute-start(bf16[16,128,128]{2,1,0:T(8,128)(2,1)S(1)} %shard_map.30.diag_square_t), channel_id=1, source_target_pairs={{4,8},{5,9},{6,10},{7,11},{8,4},{9,5},{10,6},{11,7},{20,24},{21,25... | collective-permute-start | bytes 1572872 | tf_op jit(solution)/shard_map/ppermute | solution.py:364
  27.2 2.5 %shard_map.31 = (bf16[16,7,128,128]{3,2,1,0:T(8,128)(2,1)}, bf16[8,128,128]{2,1,0:T(8,128)(2,1)S(1)}, bf16[8,128,128]{2,1,0:T(8,128)(2,1)S(1)}, bf16[2,16,128,12...) custom-call(s32[7,16]{1,0:T(8,128)S(1)} %bitcast.3, bf16[16,128,128]{2,1,0:T(8,128)(2,1)S(1)} %get-tuple-element.26.own_a, ...), custom_call_target="tpu_custom_call" | custom-call | bytes 1000 | tf_op jit(solution)/shard_map/pallas_call | solution.py:352
  29.7 0.1 collective-permute-start.8
  29.8 1.2 %collective-permute-done.4.diag_a = bf16[16,128,128]{2,1,0:T(8,128)(2,1)S(1)} collective-permute-done((bf16[16,128,128]{2,1,0:T(8,128)(2,1)S(1)}, bf16[16,128,128]{2,1,0:T(8,128)(2,1)S(1)}, u32[]{:S(2)}, u32[]{:S(2)}) %collective-permute-start.4) | collective-permute-done | bytes 524320 | tf_op jit(solution)/shard_map/ppermute | solution.py:364
  31.0 3.6 %collective-permute-start.9 = (bf16[8,128,128]{2,1,0:T(8,128)(2,1)S(1)}, bf16[8,128,128]{2,1,0:T(8,128)(2,1)S(1)}, u32[]{:S(2)}, u32[]{:S(2)}) collective-permute-start(bf16[8,128,128]{2,1,0:T(8,128)(2,1)S(1)} %get-tuple-element.39), channel_id=1, source_target_pairs={{1,2},{2,1},{5,6},{6,5},{9,10},{10,9},{13,14},{14,13},{17,18},{18,... | collective-permute-start | bytes 786440 | tf_op jit(solution)/shard_map/ppermute | solution.py:367
  34.7 0.0 collective-permute-done.5.diag_b
  34.7 2.5 %shard_map.32 = (bf16[16,7,128,128]{3,2,1,0:T(8,128)(2,1)}, bf16[2,16,128,128]{3,2,1,0:T(8,128)(2,1)S(1)}) custom-call(bf16[16,128,128]{2,1,0:T(8,128)(2,1)S(1)} %get-tuple-element.25.diag_t, f32[16,128,128]{2,1,0:T(8,128)S(1)} %get-tuple-element.32.cube_t, bf16[16,128,128]{2,1,0:T(8,128)(2,1)S(1)} %shard_map.30.diag_square_t, ...), custom_call_target="tpu_custom_call", output_to_operand_aliasing={{0}: (7, {})} | custom-call | bytes 1000 | tf_op jit(solution)/shard_map/pallas_call | solution.py:352
  37.2 0.0 collective-permute-done.8.near_a
  37.2 1.8 %collective-permute-done.9.near_b = bf16[8,128,128]{2,1,0:T(8,128)(2,1)S(1)} collective-permute-done((bf16[8,128,128]{2,1,0:T(8,128)(2,1)S(1)}, bf16[8,128,128]{2,1,0:T(8,128)(2,1)S(1)}, u32[]{:S(2)}, u32[]{:S(2)}) %collective-permute-start.9) | collective-permute-done | bytes 262176 | tf_op jit(solution)/shard_map/ppermute | solution.py:367
  39.0 1.1 %shard_map.33.old = bf16[16,7,128,128]{3,2,1,0:T(8,128)(2,1)} custom-call(bf16[16,128,128]{2,1,0:T(8,128)(2,1)S(1)} %get-tuple-element.25.diag_t, bf16[2,8,128,128]{3,2,1,0:T(8,128)(2,1)S(1)} %get-tuple-element.36.near_left, bf16[2,8,128,128]{3,2,1,0:T(8,128)(2,1)S(1)} %get-tuple-element.37.near_square, ...), custom_call_target="tpu_custom_call", output_to_operand_aliasing={{}: (5, {})} | custom-call | bytes 1000 | tf_op jit(solution)/shard_map/pallas_call | solution.py:352
  40.2 0.0 collective-permute-done.7.far
  40.2 1.2 %shard_map.34.old = bf16[16,7,128,128]{3,2,1,0:T(8,128)(2,1)} custom-call(bf16[16,128,128]{2,1,0:T(8,128)(2,1)S(1)} %get-tuple-element.25.diag_t, bf16[2,16,128,128]{3,2,1,0:T(8,128)(2,1)S(1)} %get-tuple-element.31.far_left, bf16[2,16,128,128]{3,2,1,0:T(8,128)(2,1)S(1)} %get-tuple-element.35.far_square, ...), custom_call_target="tpu_custom_call", output_to_operand_aliasing={{}: (4, {})} | custom-call | bytes 1000 | tf_op jit(solution)/shard_map/pallas_call | solution.py:352
  41.4 1.5 %collective-permute-done.6.far = bf16[16,128,128]{2,1,0:T(8,128)(2,1)S(1)} collective-permute-done((bf16[16,128,128]{2,1,0:T(8,128)(2,1)S(1)}, bf16[16,128,128]{2,1,0:T(8,128)(2,1)S(1)}, u32[]{:S(2)}, u32[]{:S(2)}) %collective-permute-start.6) | collective-permute-done | bytes 524320 | tf_op jit(solution)/shard_map/ppermute | solution.py:364
  42.8 1.1 %shard_map.35 = bf16[16,7,128,128]{3,2,1,0:T(8,128)(2,1)} custom-call(bf16[16,128,128]{2,1,0:T(8,128)(2,1)S(1)} %get-tuple-element.25.diag_t, bf16[2,16,128,128]{3,2,1,0:T(8,128)(2,1)S(1)} %get-tuple-element.31.far_left, bf16[2,16,128,128]{3,2,1,0:T(8,128)(2,1)S(1)} %get-tuple-element.35.far_square, ...), custom_call_target="tpu_custom_call", output_to_operand_aliasing={{}: (4, {})} | custom-call | bytes 1000 | tf_op jit(solution)/shard_map/pallas_call | solution.py:352
Async XLA Ops:
  0.0 13.2 %copy-start = (bf16[16,7,128,128]{3,2,1,0:T(8,128)(2,1)S(1)}, bf16[16,7,128,128]{3,2,1,0:T(8,128)(2,1)}, u32[]{:S(2)}) copy-start(bf16[16,7,128,128]{3,2,1,0:T(8,128)(2,1)} %blocks.3) | copy-start | bytes 11010052
  0.0 13.2 %copy-start.1 = (s32[16,7]{0,1:T(8,128)S(1)}, s32[16,7]{0,1:T(8,128)}, u32[]{:S(2)}) copy-start(s32[16,7]{0,1:T(8,128)} %param.3) | copy-start | bytes 1348
  1.7 8.4 %collective-permute-start = (bf16[16,128,128]{2,1,0:T(8,128)(2,1)S(1)}, bf16[16,128,128]{2,1,0:T(8,128)(2,1)S(1)}, u32[]{:S(2)}, u32[]{:S(2)}) collective-permute-start(bf16[16,128,128]{2,1,0:T(8,128)(2,1)S(1)} %get-tuple-element.23.strip_a), channel_id=1, source_target_pairs={{0,1},{1,0},{2,3},{3,2},{4,5},{5,4},{6,7},{7,6},{8,9},{9,8},{10,11... | collective-permute-start | bytes 1572872 | tf_op jit(solution)/shard_map/ppermute | solution.py:367
  2.5 10.8 %collective-permute-start.1 = (bf16[16,128,128]{2,1,0:T(8,128)(2,1)S(1)}, bf16[16,128,128]{2,1,0:T(8,128)(2,1)S(1)}, u32[]{:S(2)}, u32[]{:S(2)}) collective-permute-start(bf16[16,128,128]{2,1,0:T(8,128)(2,1)S(1)} %get-tuple-element.24.strip_b), channel_id=1, source_target_pairs={{1,2},{2,1},{5,6},{6,5},{9,10},{10,9},{13,14},{14,13},{17,18},{18,... | collective-permute-start | bytes 1572872 | tf_op jit(solution)/shard_map/ppermute | solution.py:367
  5.5 16.0 %collective-permute-start.2 = (bf16[16,128,128]{2,1,0:T(8,128)(2,1)S(1)}, bf16[16,128,128]{2,1,0:T(8,128)(2,1)S(1)}, u32[]{:S(2)}, u32[]{:S(2)}) collective-permute-start(bf16[16,128,128]{2,1,0:T(8,128)(2,1)S(1)} %get-tuple-element.26.own_a), channel_id=1, source_target_pairs={{0,4},{1,5},{2,6},{3,7},{4,0},{5,1},{6,2},{7,3},{8,12},{9,13},{10,... | collective-permute-start | bytes 1572872 | tf_op jit(solution)/shard_map/ppermute | solution.py:364
  5.7 16.9 %collective-permute-start.3 = (bf16[16,128,128]{2,1,0:T(8,128)(2,1)S(1)}, bf16[16,128,128]{2,1,0:T(8,128)(2,1)S(1)}, u32[]{:S(2)}, u32[]{:S(2)}) collective-permute-start(bf16[16,128,128]{2,1,0:T(8,128)(2,1)S(1)} %get-tuple-element.27.own_b), channel_id=1, source_target_pairs={{4,8},{5,9},{6,10},{7,11},{8,4},{9,5},{10,6},{11,7},{20,24},{21,25... | collective-permute-start | bytes 1572872 | tf_op jit(solution)/shard_map/ppermute | solution.py:364
  17.0 14.1 %collective-permute-start.4 = (bf16[16,128,128]{2,1,0:T(8,128)(2,1)S(1)}, bf16[16,128,128]{2,1,0:T(8,128)(2,1)S(1)}, u32[]{:S(2)}, u32[]{:S(2)}) collective-permute-start(bf16[16,128,128]{2,1,0:T(8,128)(2,1)S(1)} %get-tuple-element.25.diag_t), channel_id=1, source_target_pairs={{0,4},{1,5},{2,6},{3,7},{4,0},{5,1},{6,2},{7,3},{8,12},{9,13},{10,... | collective-permute-start | bytes 1572872 | tf_op jit(solution)/shard_map/ppermute | solution.py:364
  17.2 17.5 %collective-permute-start.5 = (bf16[16,128,128]{2,1,0:T(8,128)(2,1)S(1)}, bf16[16,128,128]{2,1,0:T(8,128)(2,1)S(1)}, u32[]{:S(2)}, u32[]{:S(2)}) collective-permute-start(bf16[16,128,128]{2,1,0:T(8,128)(2,1)S(1)} %get-tuple-element.25.diag_t), channel_id=1, source_target_pairs={{4,8},{5,9},{6,10},{7,11},{8,4},{9,5},{10,6},{11,7},{20,24},{21,25... | collective-permute-start | bytes 1572872 | tf_op jit(solution)/shard_map/ppermute | solution.py:364
  23.7 16.4 %collective-permute-start.7 = (bf16[16,128,128]{2,1,0:T(8,128)(2,1)S(1)}, bf16[16,128,128]{2,1,0:T(8,128)(2,1)S(1)}, u32[]{:S(2)}, u32[]{:S(2)}) collective-permute-start(bf16[16,128,128]{2,1,0:T(8,128)(2,1)S(1)} %shard_map.30.diag_square_t), channel_id=1, source_target_pairs={{0,4},{1,5},{2,6},{3,7},{4,0},{5,1},{6,2},{7,3},{8,12},{9,13},{10,... | collective-permute-start | bytes 1572872 | tf_op jit(solution)/shard_map/ppermute | solution.py:364
  23.8 19.0 %collective-permute-start.6 = (bf16[16,128,128]{2,1,0:T(8,128)(2,1)S(1)}, bf16[16,128,128]{2,1,0:T(8,128)(2,1)S(1)}, u32[]{:S(2)}, u32[]{:S(2)}) collective-permute-start(bf16[16,128,128]{2,1,0:T(8,128)(2,1)S(1)} %shard_map.30.diag_square_t), channel_id=1, source_target_pairs={{4,8},{5,9},{6,10},{7,11},{8,4},{9,5},{10,6},{11,7},{20,24},{21,25... | collective-permute-start | bytes 1572872 | tf_op jit(solution)/shard_map/ppermute | solution.py:364
  29.7 7.5 %collective-permute-start.8 = (bf16[8,128,128]{2,1,0:T(8,128)(2,1)S(1)}, bf16[8,128,128]{2,1,0:T(8,128)(2,1)S(1)}, u32[]{:S(2)}, u32[]{:S(2)}) collective-permute-start(bf16[8,128,128]{2,1,0:T(8,128)(2,1)S(1)} %get-tuple-element.38), channel_id=1, source_target_pairs={{0,1},{1,0},{2,3},{3,2},{4,5},{5,4},{6,7},{7,6},{8,9},{9,8},{10,11... | collective-permute-start | bytes 786440 | tf_op jit(solution)/shard_map/ppermute | solution.py:367
  31.0 8.0 %collective-permute-start.9 = (bf16[8,128,128]{2,1,0:T(8,128)(2,1)S(1)}, bf16[8,128,128]{2,1,0:T(8,128)(2,1)S(1)}, u32[]{:S(2)}, u32[]{:S(2)}) collective-permute-start(bf16[8,128,128]{2,1,0:T(8,128)(2,1)S(1)} %get-tuple-element.39), channel_id=1, source_target_pairs={{1,2},{2,1},{5,6},{6,5},{9,10},{10,9},{13,14},{14,13},{17,18},{18,... | collective-permute-start | bytes 786440 | tf_op jit(solution)/shard_map/ppermute | solution.py:367

commit v4 on v3

--- a/solution.py
+++ b/solution.py
@@ -74,32 +74,25 @@
     return (far_slot, K - 1 - far_slot), (near_slot, K - 1 - near_slot), (near_base, rows - GX - near_base)
 
 
-def stage_kernel(blocks, send_a, send_b, strip_a, strip_b, sem):
-    rows = blocks.shape[0]
-    far_slots, near_slots, bases = places(rows)
+def pack_kernel(blocks, send_a, send_b, sem):
+    far_slots, _, _ = places(blocks.shape[0])
     copies = []
-    for at, send in ((0, send_a), (1, send_b)):
+    for at, send in enumerate((send_a, send_b)):
         copies.append(pltpu.make_async_copy(blocks.at[:, far_slots[at]], send, sem.at[at]))
-    for at, strip in ((0, strip_a), (1, strip_b)):
-        at_rows = pl.ds(bases[at], GX)
-        for half, slot in enumerate((near_slots[at], CENTER)):
-            part = strip.at[pl.ds(half * GX, GX)]
-            copies.append(pltpu.make_async_copy(blocks.at[at_rows, slot], part, sem.at[2 + 2 * at + half]))
-    for copy in copies:
-        copy.start()
+        copies[-1].start()
     for copy in copies:
         copy.wait()
 
 
-def local_kernel(
-    cols, blocks, near_a, near_b, strip_a, strip_b,
-    diag_t, left_t, square_t, cube_t, near_left, near_square, total, near_diag, near_right, near_other,
-):
+def local_kernel(cols, blocks, diag_t, left_t, square_t, cube_t, total, strip_a, strip_b):
     rows = diag_t.shape[0]
+    _, near_slots, bases = places(rows)
     in_groups(list(range(rows)), lambda j: (blocks[j, CENTER],), lambda x: x.T, diag_t.__setitem__)
+    for at, strip in enumerate((strip_a, strip_b)):
+        for e in range(GX):
+            strip[e] = blocks[bases[at] + e, near_slots[at]]
+            strip[GX + e] = diag_t[bases[at] + e]
     edges = local_edges(rows)
-    _, near_slots, bases = places(rows)
-    strip = list(range(GX))
 
     def load(edge):
         j, slot, place, k = edge
@@ -112,50 +105,6 @@
     def store(edge, result):
         j, slot, place, k = edge
         left_t[place, j], square_t[place, j] = result
-
-    if rows != 2 * GX:
-        total[...] = jnp.zeros_like(total)
-        cube_t[...] = jnp.zeros_like(cube_t)
-    for side, (near, own) in enumerate(((near_a, strip_a), (near_b, strip_b))):
-        slot, base = near_slots[side], bases[side]
-
-        def load_left(e):
-            return cols[slot, base + e] >= 0, near[e]
-
-        def load_right(e):
-            return cols[slot, base + e] >= 0, own[e]
-
-        in_groups(
-            strip, lambda e: (near[GX + e],), lambda x: x.T, lambda e, value: near_diag.__setitem__((side, e), value)
-        )
-        in_groups(strip, load_left, flipped, lambda e, value: near_left.__setitem__((side, e), value))
-        in_groups(strip, load_right, flipped, lambda e, value: near_right.__setitem__((side, e), value))
-        in_groups(
-            strip,
-            lambda e: (diag_t[base + e], near_left[side, e], near_diag[side, e]),
-            one_square,
-            lambda e, value: near_square.__setitem__((side, e), value),
-        )
-        in_groups(
-            strip,
-            lambda e: (near_diag[side, e], near_right[side, e], diag_t[base + e]),
-            one_square,
-            lambda e, value: near_other.__setitem__((side, e), value),
-        )
-
-        def load_near(e):
-            j = base + e
-            return near_left[side, e], near_other[side, e], near_right[side, e]
-
-        def near_terms(x_t, square, y_t):
-            return dot(x_t, square), dot(x_t, y_t)
-
-        def store_near(e, result):
-            j = base + e
-            for ref, value in zip((cube_t, total), result):
-                ref[j] = value if rows == 2 * GX else ref[j] + value
-
-        in_groups(strip, load_near, near_terms, store_near)
 
     in_groups(edges, load, compute, store)
 
@@ -169,20 +118,20 @@
             jnp.concatenate(squares, axis=0),
             jnp.concatenate(lhs + [diag_t[j]], axis=1),
             jnp.concatenate(others + [diag_t[j]], axis=0),
-            cube_t[j],
-            total[j],
-        )
-
-    def row_terms(lhs, squares, lhs_all, others, cube, square):
-        return dot(lhs, squares) + cube, dot(lhs_all, others) + square
+        )
 
     def store_row(j, result):
         cube_t[j], total[j] = result
 
-    in_groups(list(range(rows)), load_row, row_terms, store_row)
-
-
-def diag_square_kernel(cols, own_a, own_b, total, far_a, far_b, square_t):
+    in_groups(
+        list(range(rows)),
+        load_row,
+        lambda lhs, squares, lhs_all, others: (dot(lhs, squares), dot(lhs_all, others)),
+        store_row,
+    )
+
+
+def far_terms_kernel(cols, own_a, own_b, total, far_a, far_b, more):
     rows = total.shape[0]
     far_slots, _, _ = places(rows)
 
@@ -190,12 +139,35 @@
         own = [masked(cols[slot, j] >= 0, own[j]) for slot, own in zip(far_slots, (own_a, own_b))]
         return jnp.concatenate(own, axis=1), jnp.concatenate([far_a[j], far_b[j]], axis=0), total[j]
 
-    in_groups(
-        list(range(rows)),
-        load,
-        lambda lhs, rhs, extra_t: (dot(lhs, rhs).T + extra_t).astype(BF16),
-        square_t.__setitem__,
-    )
+    in_groups(list(range(rows)), load, lambda lhs, rhs, extra_t: dot(lhs, rhs).T + extra_t, more.__setitem__)
+
+
+def near_terms_kernel(cols, strip_a, strip_b, more, near_a, near_b, square_t, near_left, near_right, total):
+    rows = more.shape[0]
+    _, near_slots, bases = places(rows)
+    if rows != 2 * GX:
+        total[...] = more[...]
+    for side, (near, own) in enumerate(((near_a, strip_a), (near_b, strip_b))):
+        slot, base = near_slots[side], bases[side]
+        so_far = more if rows == 2 * GX else total
+
+        def load(e):
+            return cols[slot, base + e] >= 0, own[e], near[e], so_far[base + e]
+
+        def compute(flag, y, x, extra_t):
+            x_t, y_t = flipped(flag, x), flipped(flag, y)
+            return x_t, y_t, dot(x_t, y_t) + extra_t
+
+        def store(e, result):
+            near_left[side, e], near_right[side, e], square = result
+            if rows == 2 * GX:
+                square_t[base + e] = square.astype(BF16)
+            else:
+                total[base + e] = square
+
+        in_groups(list(range(GX)), load, compute, store)
+    if rows != 2 * GX:
+        square_t[...] = total[...].astype(BF16)
 
 
 def one_square(diag_own, x_t, diag_other):
@@ -214,8 +186,9 @@
 
 
 def inside_kernel(
-    cols, own_a, own_b, diag_t, left_t, square_t, diag_square_t, off_a, off_b,
-    out, send_a, send_b, far_left, far_right, local_out, sem,
+    cols, own_a, own_b, diag_t, left_t, square_t, cube_in, diag_square_t, off_a, off_b,
+    near_a, near_b, near_left, near_right,
+    out, send_a, send_b, far_left, far_right, near_square, cube_t, local_out, near_other, sem,
 ):
     rows = diag_t.shape[0]
     edges = local_edges(rows)
@@ -240,6 +213,30 @@
         at = pl.ds(first, last + 1 - first)
         copies.append(pltpu.make_async_copy(local_out.at[place, at], out.at[at, slot], sem.at[place]))
         copies[-1].start()
+    if rows != 2 * GX:
+        cube_t[...] = cube_in[...]
+    strip = list(range(GX))
+    for side, near in enumerate((near_a, near_b)):
+        base = bases[side]
+        so_far = cube_in if rows == 2 * GX else cube_t
+        in_groups(
+            strip,
+            lambda e: (diag_t[base + e], near_left[side, e], near[GX + e]),
+            one_square,
+            lambda e, value: near_square.__setitem__((side, e), value),
+        )
+        in_groups(
+            strip,
+            lambda e: (near[GX + e], near_right[side, e], diag_t[base + e]),
+            one_square,
+            lambda e, value: near_other.__setitem__((side, e), value),
+        )
+        in_groups(
+            strip,
+            lambda e: (near_left[side, e], near_other[side, e], so_far[base + e]),
+            lambda x_t, square, extra: dot(x_t, square) + extra,
+            lambda e, value: cube_t.__setitem__(base + e, value),
+        )
     for at, (off, own) in enumerate(((off_a, own_a), (off_b, own_b))):
         slot = far_slots[at]
         in_groups(
@@ -366,46 +363,61 @@
     def near(value, pairing):
         return lax.ppermute(value, "row", near_pairs(pairing, layer_dist, count))
 
-    send_a, send_b, strip_a, strip_b = call(
-        stage_kernel,
+    send_a, send_b = call(
+        pack_kernel,
         [hbm],
         [density],
-        [block(rows), block(rows), block(2 * GX), block(2 * GX)],
-        [vmem] * 4,
-        [dma((6,))],
+        [block(rows), block(rows)],
+        [vmem] * 2,
+        [dma((2,))],
         vmem_limit=STAGE_LIMIT,
     )
     off_b = far(send_b, 1)
     off_a = far(send_a, 0)
+    diag_t, left_t, square_t, cube_t, total, strip_a, strip_b = call(
+        local_kernel,
+        [smem, vmem],
+        [cols, density],
+        [
+            block(rows), block(4, rows), block(4, rows), wide(rows), wide(rows), block(2 * GX), block(2 * GX),
+        ],
+        [vmem] * 7,
+        [],
+    )
+    diag_b = far(diag_t, 1)
+    diag_a = far(diag_t, 0)
     near_b = near(strip_b, 1)
     near_a = near(strip_a, 0)
-    diag_t, left_t, square_t, cube_t, near_left, near_square, total = call(
-        local_kernel,
-        [smem] + [vmem] * 5,
-        [cols, density, near_a, near_b, strip_a, strip_b],
-        [block(rows), block(4, rows), block(4, rows), wide(rows), block(2, GX), block(2, GX), wide(rows)],
-        [vmem] * 7,
-        [scratch(2, GX)] * 3,
-    )
-    diag_b = far(diag_t, 1)
-    diag_a = far(diag_t, 0)
-    diag_square_t = call(
-        diag_square_kernel,
+    total = call(
+        far_terms_kernel,
         [smem] + [vmem] * 5,
         [cols, send_a, send_b, total, off_a, off_b],
-        block(rows),
+        wide(rows),
         vmem,
         [],
     )
+    diag_square_t, near_left, near_right = call(
+        near_terms_kernel,
+        [smem] + [vmem] * 5,
+        [cols, strip_a, strip_b, total, near_a, near_b],
+        [block(rows), block(2, GX), block(2, GX)],
+        [vmem] * 3,
+        [pltpu.VMEM((rows, size, size), F32)],
+    )
     far_square_b = far(diag_square_t, 1)
     far_square_a = far(diag_square_t, 0)
-    out, square_a, square_b, far_left, far_right = call(
+    out, square_a, square_b, far_left, far_right, near_square, cube_t = call(
         inside_kernel,
-        [smem] + [vmem] * 8,
-        [cols, send_a, send_b, diag_t, left_t, square_t, diag_square_t, off_a, off_b],
-        [block(rows, K), block(GX), block(GX), block(2, rows), block(2, rows)],
-        [hbm] + [vmem] * 4,
-        [scratch(4, rows), dma((4,))],
+        [smem] + [vmem] * 13,
+        [
+            cols, send_a, send_b, diag_t, left_t, square_t, cube_t, diag_square_t, off_a, off_b,
+            near_a, near_b, near_left, near_right,
+        ],
+        [
+            block(rows, K), block(GX), block(GX), block(2, rows), block(2, rows), block(2, GX), wide(rows),
+        ],
+        [hbm] + [vmem] * 6,
+        [scratch(4, rows), scratch(2, GX), dma((4,))],
     )
     near_square_b = near(square_b, 1)
     near_square_a = near(square_a, 0)

time: 44.6 us -> 42.4 us (0.951)
  the two profiles are of different devices: /device:TPU:11 before, /device:TPU:10 now
where the time goes in v4:
time: 42.4 us; the launch traced here: 42.2 us
  Pallas kernels  15.6 us (37%)
  starting transfers between devices  13.6 us (32%)
  waiting for transfers between devices  12.7 us (30%)
    pallas_call x9, Pallas kernels, call(): pl.pallas_call(kernel, in_specs=in_specs, out_specs=out_specs, out_shape=...  15.6 us
    ppermute x6, waiting for transfers between devices, far(): return lax.ppermute(value, 'row', far_pairs(pairing, layer_dist, count))  12.7 us
    ppermute x6, starting transfers between devices, far(): return lax.ppermute(value, 'row', far_pairs(pairing, layer_dist, count))  12.1 us
    ppermute x4, starting transfers between devices, near(): return lax.ppermute(value, 'row', near_pairs(pairing, layer_dist, count))  1.51 us
  transfers between devices with their start and end apart: 10, of which 4 were waited for; matrix products, arithmetic and copies ran while one was open for 0% of the time, Pallas kernels for 31%

profile of v4, /device:TPU:10, one launch (start us, length us, event | category | flops | bytes accessed | tf_op | source)
XLA Modules:
  0.0 42.2 jit_solution(12722314549680765250)
XLA Ops:
  0.0 0.0 copy-start
  0.0 1.4 %shard_map.29 = (bf16[16,128,128]{2,1,0:T(8,128)(2,1)S(1)}, bf16[16,128,128]{2,1,0:T(8,128)(2,1)S(1)}) custom-call(bf16[16,7,128,128]{3,2,1,0:T(8,128)(2,1)} %blocks.3), custom_call_target="tpu_custom_call" | custom-call | bytes 1000 | tf_op jit(solution)/shard_map/pallas_call | solution.py:349
  1.4 0.5 %collective-permute-start = (bf16[16,128,128]{2,1,0:T(8,128)(2,1)S(1)}, bf16[16,128,128]{2,1,0:T(8,128)(2,1)S(1)}, u32[]{:S(2)}, u32[]{:S(2)}) collective-permute-start(bf16[16,128,128]{2,1,0:T(8,128)(2,1)S(1)} %get-tuple-element.27.own_a), channel_id=1, source_target_pairs={{0,4},{1,5},{2,6},{3,7},{4,0},{5,1},{6,2},{7,3},{8,12},{9,13},{10,... | collective-permute-start | bytes 1572872 | tf_op jit(solution)/shard_map/ppermute | solution.py:361
  1.9 4.6 %collective-permute-start.1 = (bf16[16,128,128]{2,1,0:T(8,128)(2,1)S(1)}, bf16[16,128,128]{2,1,0:T(8,128)(2,1)S(1)}, u32[]{:S(2)}, u32[]{:S(2)}) collective-permute-start(bf16[16,128,128]{2,1,0:T(8,128)(2,1)S(1)} %get-tuple-element.28.own_b), channel_id=1, source_target_pairs={{4,8},{5,9},{6,10},{7,11},{8,4},{9,5},{10,6},{11,7},{20,24},{21,25... | collective-permute-start | bytes 1572872 | tf_op jit(solution)/shard_map/ppermute | solution.py:361
  6.5 0.0 copy-done
  6.5 0.0 copy-done.1
  6.5 2.7 %shard_map.28 = (bf16[16,128,128]{2,1,0:T(8,128)(2,1)S(1)}, bf16[4,16,128,128]{3,2,1,0:T(8,128)(2,1)S(1)}, bf16[4,16,128,128]{3,2,1,0:T(8,128)(2,1)S(1)}, f32[16...) custom-call(s32[7,16]{1,0:T(8,128)S(1)} %bitcast.1, ...), custom_call_target="tpu_custom_call" | custom-call | bytes 1000 | tf_op jit(solution)/shard_map/pallas_call | solution.py:349
  9.3 0.1 collective-permute-start.2
  9.4 0.7 %collective-permute-start.3 = (bf16[16,128,128]{2,1,0:T(8,128)(2,1)S(1)}, bf16[16,128,128]{2,1,0:T(8,128)(2,1)S(1)}, u32[]{:S(2)}, u32[]{:S(2)}) collective-permute-start(bf16[16,128,128]{2,1,0:T(8,128)(2,1)S(1)} %get-tuple-element.33.strip_b), channel_id=1, source_target_pairs={{1,2},{2,1},{5,6},{6,5},{9,10},{10,9},{13,14},{14,13},{17,18},{18,... | collective-permute-start | bytes 1572872 | tf_op jit(solution)/shard_map/ppermute | solution.py:364
  10.1 0.1 collective-permute-start.4
  10.1 5.0 %collective-permute-done.far_a.off_a = bf16[16,128,128]{2,1,0:T(8,128)(2,1)S(1)} collective-permute-done((bf16[16,128,128]{2,1,0:T(8,128)(2,1)S(1)}, bf16[16,128,128]{2,1,0:T(8,128)(2,1)S(1)}, u32[]{:S(2)}, u32[]{:S(2)}) %collective-permute-start) | collective-permute-done | bytes 524320 | tf_op jit(solution)/shard_map/ppermute | solution.py:361
  15.1 4.5 %collective-permute-start.5 = (bf16[16,128,128]{2,1,0:T(8,128)(2,1)S(1)}, bf16[16,128,128]{2,1,0:T(8,128)(2,1)S(1)}, u32[]{:S(2)}, u32[]{:S(2)}) collective-permute-start(bf16[16,128,128]{2,1,0:T(8,128)(2,1)S(1)} %get-tuple-element.26.diag_t), channel_id=1, source_target_pairs={{4,8},{5,9},{6,10},{7,11},{8,4},{9,5},{10,6},{11,7},{20,24},{21,25... | collective-permute-start | bytes 1572872 | tf_op jit(solution)/shard_map/ppermute | solution.py:361
  19.6 0.0 collective-permute-done.1.far_b.off_b
  19.6 1.1 %shard_map.30.more = f32[16,128,128]{2,1,0:T(8,128)S(1)} custom-call(s32[7,16]{1,0:T(8,128)S(1)} %bitcast.2, bf16[16,128,128]{2,1,0:T(8,128)(2,1)S(1)} %get-tuple-element.27.own_a, bf16[16,128,128]{2,1,0:T(8,128)(2,1)S(1)} %get-tuple-element.28.own_b, f32[16,128,128]{2,1,0:T(8,128)S(1)} %get-tuple-element.34.total, ...), custom_call_target="tpu_custom_call" | custom-call | bytes 1000 | tf_op jit(solution)/shard_map/pallas_call | solution.py:349
  20.8 0.0 collective-permute-done.2.near_a
  20.8 0.0 collective-permute-done.3.near_b
  20.8 1.2 %shard_map.31 = (bf16[16,128,128]{2,1,0:T(8,128)(2,1)S(1)}, bf16[2,8,128,128]{3,2,1,0:T(8,128)(2,1)S(1)}, bf16[2,8,128,128]{3,2,1,0:T(8,128)(2,1)S(1)}) custom-call(s32[7,16]{1,0:T(8,128)S(1)} %bitcast.3, bf16[16,128,128]{2,1,0:T(8,128)(2,1)S(1)} %get-tuple-element.32.strip_a, bf16[16,128,128]{2,1,0:T(8,128)(2,1)S(1)} %get-tuple-element.33.strip_b, ...), custom_call_target="tpu_custom_call" | custom-call | bytes 1000 | tf_op jit(solution)/shard_map/pallas_call | solution.py:349
  22.0 0.1 collective-permute-start.7
  22.0 2.4 %collective-permute-start.6 = (bf16[16,128,128]{2,1,0:T(8,128)(2,1)S(1)}, bf16[16,128,128]{2,1,0:T(8,128)(2,1)S(1)}, u32[]{:S(2)}, u32[]{:S(2)}) collective-permute-start(bf16[16,128,128]{2,1,0:T(8,128)(2,1)S(1)} %get-tuple-element.35.diag_square_t), channel_id=1, source_target_pairs={{4,8},{5,9},{6,10},{7,11},{8,4},{9,5},{10,6},{11,7},{20,24},{21,25... | collective-permute-start | bytes 1572872 | tf_op jit(solution)/shard_map/ppermute | solution.py:361
  24.4 3.2 %shard_map.32 = (bf16[16,7,128,128]{3,2,1,0:T(8,128)(2,1)}, bf16[8,128,128]{2,1,0:T(8,128)(2,1)S(1)}, bf16[8,128,128]{2,1,0:T(8,128)(2,1)S(1)}, bf16[2,16,128,12...) custom-call(s32[7,16]{1,0:T(8,128)S(1)} %bitcast.4, ...), custom_call_target="tpu_custom_call" | custom-call | bytes 1000 | tf_op jit(solution)/shard_map/pallas_call | solution.py:349
  27.6 0.1 collective-permute-start.8
  27.7 0.0 collective-permute-done.4.diag_a
  27.7 0.7 %collective-permute-start.9 = (bf16[8,128,128]{2,1,0:T(8,128)(2,1)S(1)}, bf16[8,128,128]{2,1,0:T(8,128)(2,1)S(1)}, u32[]{:S(2)}, u32[]{:S(2)}) collective-permute-start(bf16[8,128,128]{2,1,0:T(8,128)(2,1)S(1)} %get-tuple-element.45), channel_id=1, source_target_pairs={{1,2},{2,1},{5,6},{6,5},{9,10},{10,9},{13,14},{14,13},{17,18},{18,... | collective-permute-start | bytes 786440 | tf_op jit(solution)/shard_map/ppermute | solution.py:364
  28.4 4.0 %collective-permute-done.5.diag_b = bf16[16,128,128]{2,1,0:T(8,128)(2,1)S(1)} collective-permute-done((bf16[16,128,128]{2,1,0:T(8,128)(2,1)S(1)}, bf16[16,128,128]{2,1,0:T(8,128)(2,1)S(1)}, u32[]{:S(2)}, u32[]{:S(2)}) %collective-permute-start.5) | collective-permute-done | bytes 524320 | tf_op jit(solution)/shard_map/ppermute | solution.py:361
  32.5 2.5 %shard_map.33 = (bf16[16,7,128,128]{3,2,1,0:T(8,128)(2,1)}, bf16[2,16,128,128]{3,2,1,0:T(8,128)(2,1)S(1)}) custom-call(bf16[16,128,128]{2,1,0:T(8,128)(2,1)S(1)} %get-tuple-element.26.diag_t, f32[16,128,128]{2,1,0:T(8,128)S(1)} %get-tuple-element.39.cube_t, ...), custom_call_target="tpu_custom_call", output_to_operand_aliasing={{0}: (7, {})} | custom-call | bytes 1000 | tf_op jit(solution)/shard_map/pallas_call | solution.py:349
  34.9 0.0 collective-permute-done.8.near_a
  35.0 0.0 collective-permute-done.9.near_b
  35.0 1.1 %shard_map.34.old = bf16[16,7,128,128]{3,2,1,0:T(8,128)(2,1)} custom-call(bf16[16,128,128]{2,1,0:T(8,128)(2,1)S(1)} %get-tuple-element.26.diag_t, bf16[2,8,128,128]{3,2,1,0:T(8,128)(2,1)S(1)} %get-tuple-element.36.near_left, bf16[2,8,128,128]{3,2,1,0:T(8,128)(2,1)S(1)} %get-tuple-element.43.near_square, ...), custom_call_target="tpu_custom_call", output_to_operand_aliasing={{}: (5, {})} | custom-call | bytes 1000 | tf_op jit(solution)/shard_map/pallas_call | solution.py:349
  36.1 0.9 %collective-permute-done.7.far = bf16[16,128,128]{2,1,0:T(8,128)(2,1)S(1)} collective-permute-done((bf16[16,128,128]{2,1,0:T(8,128)(2,1)S(1)}, bf16[16,128,128]{2,1,0:T(8,128)(2,1)S(1)}, u32[]{:S(2)}, u32[]{:S(2)}) %collective-permute-start.7) | collective-permute-done | bytes 524320 | tf_op jit(solution)/shard_map/ppermute | solution.py:361
  37.1 1.2 %shard_map.35.old = bf16[16,7,128,128]{3,2,1,0:T(8,128)(2,1)} custom-call(bf16[16,128,128]{2,1,0:T(8,128)(2,1)S(1)} %get-tuple-element.26.diag_t, bf16[2,16,128,128]{3,2,1,0:T(8,128)(2,1)S(1)} %get-tuple-element.38.far_left, bf16[2,16,128,128]{3,2,1,0:T(8,128)(2,1)S(1)} %get-tuple-element.42.far_square, ...), custom_call_target="tpu_custom_call", output_to_operand_aliasing={{}: (4, {})} | custom-call | bytes 1000 | tf_op jit(solution)/shard_map/pallas_call | solution.py:349
  38.2 2.8 %collective-permute-done.6.far = bf16[16,128,128]{2,1,0:T(8,128)(2,1)S(1)} collective-permute-done((bf16[16,128,128]{2,1,0:T(8,128)(2,1)S(1)}, bf16[16,128,128]{2,1,0:T(8,128)(2,1)S(1)}, u32[]{:S(2)}, u32[]{:S(2)}) %collective-permute-start.6) | collective-permute-done | bytes 524320 | tf_op jit(solution)/shard_map/ppermute | solution.py:361
  41.0 1.1 %shard_map.36 = bf16[16,7,128,128]{3,2,1,0:T(8,128)(2,1)} custom-call(bf16[16,128,128]{2,1,0:T(8,128)(2,1)S(1)} %get-tuple-element.26.diag_t, bf16[2,16,128,128]{3,2,1,0:T(8,128)(2,1)S(1)} %get-tuple-element.38.far_left, bf16[2,16,128,128]{3,2,1,0:T(8,128)(2,1)S(1)} %get-tuple-element.42.far_square, ...), custom_call_target="tpu_custom_call", output_to_operand_aliasing={{}: (4, {})} | custom-call | bytes 1000 | tf_op jit(solution)/shard_map/pallas_call | solution.py:349
  (1 shorter events, 0.0 us)
Async XLA Ops:
  0.0 6.5 %copy-start = (bf16[16,7,128,128]{3,2,1,0:T(8,128)(2,1)S(1)}, bf16[16,7,128,128]{3,2,1,0:T(8,128)(2,1)}, u32[]{:S(2)}) copy-start(bf16[16,7,128,128]{3,2,1,0:T(8,128)(2,1)} %blocks.3) | copy-start | bytes 11010052
  0.0 6.5 %copy-start.1 = (s32[16,7]{0,1:T(8,128)S(1)}, s32[16,7]{0,1:T(8,128)}, u32[]{:S(2)}) copy-start(s32[16,7]{0,1:T(8,128)} %param.3) | copy-start | bytes 1348
  1.4 13.7 %collective-permute-start = (bf16[16,128,128]{2,1,0:T(8,128)(2,1)S(1)}, bf16[16,128,128]{2,1,0:T(8,128)(2,1)S(1)}, u32[]{:S(2)}, u32[]{:S(2)}) collective-permute-start(bf16[16,128,128]{2,1,0:T(8,128)(2,1)S(1)} %get-tuple-element.27.own_a), channel_id=1, source_target_pairs={{0,4},{1,5},{2,6},{3,7},{4,0},{5,1},{6,2},{7,3},{8,12},{9,13},{10,... | collective-permute-start | bytes 1572872 | tf_op jit(solution)/shard_map/ppermute | solution.py:361
  1.9 17.7 %collective-permute-start.1 = (bf16[16,128,128]{2,1,0:T(8,128)(2,1)S(1)}, bf16[16,128,128]{2,1,0:T(8,128)(2,1)S(1)}, u32[]{:S(2)}, u32[]{:S(2)}) collective-permute-start(bf16[16,128,128]{2,1,0:T(8,128)(2,1)S(1)} %get-tuple-element.28.own_b), channel_id=1, source_target_pairs={{4,8},{5,9},{6,10},{7,11},{8,4},{9,5},{10,6},{11,7},{20,24},{21,25... | collective-permute-start | bytes 1572872 | tf_op jit(solution)/shard_map/ppermute | solution.py:361
  9.3 11.5 %collective-permute-start.2 = (bf16[16,128,128]{2,1,0:T(8,128)(2,1)S(1)}, bf16[16,128,128]{2,1,0:T(8,128)(2,1)S(1)}, u32[]{:S(2)}, u32[]{:S(2)}) collective-permute-start(bf16[16,128,128]{2,1,0:T(8,128)(2,1)S(1)} %get-tuple-element.32.strip_a), channel_id=1, source_target_pairs={{0,1},{1,0},{2,3},{3,2},{4,5},{5,4},{6,7},{7,6},{8,9},{9,8},{10,11... | collective-permute-start | bytes 1572872 | tf_op jit(solution)/shard_map/ppermute | solution.py:364
  9.4 11.4 %collective-permute-start.3 = (bf16[16,128,128]{2,1,0:T(8,128)(2,1)S(1)}, bf16[16,128,128]{2,1,0:T(8,128)(2,1)S(1)}, u32[]{:S(2)}, u32[]{:S(2)}) collective-permute-start(bf16[16,128,128]{2,1,0:T(8,128)(2,1)S(1)} %get-tuple-element.33.strip_b), channel_id=1, source_target_pairs={{1,2},{2,1},{5,6},{6,5},{9,10},{10,9},{13,14},{14,13},{17,18},{18,... | collective-permute-start | bytes 1572872 | tf_op jit(solution)/shard_map/ppermute | solution.py:364
  10.1 17.7 %collective-permute-start.4 = (bf16[16,128,128]{2,1,0:T(8,128)(2,1)S(1)}, bf16[16,128,128]{2,1,0:T(8,128)(2,1)S(1)}, u32[]{:S(2)}, u32[]{:S(2)}) collective-permute-start(bf16[16,128,128]{2,1,0:T(8,128)(2,1)S(1)} %get-tuple-element.26.diag_t), channel_id=1, source_target_pairs={{0,4},{1,5},{2,6},{3,7},{4,0},{5,1},{6,2},{7,3},{8,12},{9,13},{10,... | collective-permute-start | bytes 1572872 | tf_op jit(solution)/shard_map/ppermute | solution.py:361
  15.1 17.3 %collective-permute-start.5 = (bf16[16,128,128]{2,1,0:T(8,128)(2,1)S(1)}, bf16[16,128,128]{2,1,0:T(8,128)(2,1)S(1)}, u32[]{:S(2)}, u32[]{:S(2)}) collective-permute-start(bf16[16,128,128]{2,1,0:T(8,128)(2,1)S(1)} %get-tuple-element.26.diag_t), channel_id=1, source_target_pairs={{4,8},{5,9},{6,10},{7,11},{8,4},{9,5},{10,6},{11,7},{20,24},{21,25... | collective-permute-start | bytes 1572872 | tf_op jit(solution)/shard_map/ppermute | solution.py:361
  22.0 15.1 %collective-permute-start.7 = (bf16[16,128,128]{2,1,0:T(8,128)(2,1)S(1)}, bf16[16,128,128]{2,1,0:T(8,128)(2,1)S(1)}, u32[]{:S(2)}, u32[]{:S(2)}) collective-permute-start(bf16[16,128,128]{2,1,0:T(8,128)(2,1)S(1)} %get-tuple-element.35.diag_square_t), channel_id=1, source_target_pairs={{0,4},{1,5},{2,6},{3,7},{4,0},{5,1},{6,2},{7,3},{8,12},{9,13},{10,... | collective-permute-start | bytes 1572872 | tf_op jit(solution)/shard_map/ppermute | solution.py:361
  22.0 19.0 %collective-permute-start.6 = (bf16[16,128,128]{2,1,0:T(8,128)(2,1)S(1)}, bf16[16,128,128]{2,1,0:T(8,128)(2,1)S(1)}, u32[]{:S(2)}, u32[]{:S(2)}) collective-permute-start(bf16[16,128,128]{2,1,0:T(8,128)(2,1)S(1)} %get-tuple-element.35.diag_square_t), channel_id=1, source_target_pairs={{4,8},{5,9},{6,10},{7,11},{8,4},{9,5},{10,6},{11,7},{20,24},{21,25... | collective-permute-start | bytes 1572872 | tf_op jit(solution)/shard_map/ppermute | solution.py:361
  27.6 7.3 %collective-permute-start.8 = (bf16[8,128,128]{2,1,0:T(8,128)(2,1)S(1)}, bf16[8,128,128]{2,1,0:T(8,128)(2,1)S(1)}, u32[]{:S(2)}, u32[]{:S(2)}) collective-permute-start(bf16[8,128,128]{2,1,0:T(8,128)(2,1)S(1)} %get-tuple-element.44), channel_id=1, source_target_pairs={{0,1},{1,0},{2,3},{3,2},{4,5},{5,4},{6,7},{7,6},{8,9},{9,8},{10,11... | collective-permute-start | bytes 786440 | tf_op jit(solution)/shard_map/ppermute | solution.py:364
  27.7 7.2 %collective-permute-start.9 = (bf16[8,128,128]{2,1,0:T(8,128)(2,1)S(1)}, bf16[8,128,128]{2,1,0:T(8,128)(2,1)S(1)}, u32[]{:S(2)}, u32[]{:S(2)}) collective-permute-start(bf16[8,128,128]{2,1,0:T(8,128)(2,1)S(1)} %get-tuple-element.45), channel_id=1, source_target_pairs={{1,2},{2,1},{5,6},{6,5},{9,10},{10,9},{13,14},{14,13},{17,18},{18,... | collective-permute-start | bytes 786440 | tf_op jit(solution)/shard_map/ppermute | solution.py:364

commit v5 on v4

--- a/solution.py
+++ b/solution.py
@@ -16,6 +16,7 @@
 VMEM_LIMIT = 12 * 1024 * 1024
 STAGE_LIMIT = 50 * 1024 * 1024
 KERNEL_COST = 1000
+SPARE = 16
 
 
 def far_pairs(pairing, layer_dist, count):
@@ -74,20 +75,34 @@
     return (far_slot, K - 1 - far_slot), (near_slot, K - 1 - near_slot), (near_base, rows - GX - near_base)
 
 
+def packed(ref, j):
+    size = ref.shape[1]
+    return ref.at[pl.ds(j * size, size)]
+
+
 def pack_kernel(blocks, send_a, send_b, sem):
-    far_slots, _, _ = places(blocks.shape[0])
+    rows = blocks.shape[0]
+    far_slots, _, _ = places(rows)
     copies = []
     for at, send in enumerate((send_a, send_b)):
-        copies.append(pltpu.make_async_copy(blocks.at[:, far_slots[at]], send, sem.at[at]))
+        size = send.shape[1]
+        target = send.at[pl.ds(0, rows * size)].reshape(rows, size, size)
+        copies.append(pltpu.make_async_copy(blocks.at[:, far_slots[at]], target, sem.at[at]))
         copies[-1].start()
+        spare = pl.ds(rows * send.shape[1], SPARE)
+        send[spare] = jnp.zeros((SPARE, send.shape[1]), BF16)
     for copy in copies:
         copy.wait()
 
 
-def local_kernel(cols, blocks, diag_t, left_t, square_t, cube_t, total, strip_a, strip_b):
+def local_kernel(cols, blocks, diag_t, diag_send, left_t, square_t, cube_t, total, strip_a, strip_b):
     rows = diag_t.shape[0]
     _, near_slots, bases = places(rows)
     in_groups(list(range(rows)), lambda j: (blocks[j, CENTER],), lambda x: x.T, diag_t.__setitem__)
+    size = diag_send.shape[1]
+    for j in range(rows):
+        diag_send[pl.ds(j * size, size)] = diag_t[j]
+    diag_send[pl.ds(rows * size, SPARE)] = jnp.zeros((SPARE, size), BF16)
     for at, strip in enumerate((strip_a, strip_b)):
         for e in range(GX):
             strip[e] = blocks[bases[at] + e, near_slots[at]]
@@ -131,25 +146,17 @@
     )
 
 
-def far_terms_kernel(cols, own_a, own_b, total, far_a, far_b, more):
-    rows = total.shape[0]
-    far_slots, _, _ = places(rows)
-
-    def load(j):
-        own = [masked(cols[slot, j] >= 0, own[j]) for slot, own in zip(far_slots, (own_a, own_b))]
-        return jnp.concatenate(own, axis=1), jnp.concatenate([far_a[j], far_b[j]], axis=0), total[j]
-
-    in_groups(list(range(rows)), load, lambda lhs, rhs, extra_t: dot(lhs, rhs).T + extra_t, more.__setitem__)
-
-
-def near_terms_kernel(cols, strip_a, strip_b, more, near_a, near_b, square_t, near_left, near_right, total):
-    rows = more.shape[0]
-    _, near_slots, bases = places(rows)
+def diag_square_kernel(
+    cols, strip_a, strip_b, own_a, own_b, local, near_a, near_b, far_a, far_b,
+    square_t, near_left, near_right, square_a, square_b, total,
+):
+    rows = local.shape[0]
+    far_slots, near_slots, bases = places(rows)
     if rows != 2 * GX:
-        total[...] = more[...]
+        total[...] = local[...]
     for side, (near, own) in enumerate(((near_a, strip_a), (near_b, strip_b))):
         slot, base = near_slots[side], bases[side]
-        so_far = more if rows == 2 * GX else total
+        so_far = local if rows == 2 * GX else total
 
         def load(e):
             return cols[slot, base + e] >= 0, own[e], near[e], so_far[base + e]
@@ -159,15 +166,23 @@
             return x_t, y_t, dot(x_t, y_t) + extra_t
 
         def store(e, result):
-            near_left[side, e], near_right[side, e], square = result
-            if rows == 2 * GX:
-                square_t[base + e] = square.astype(BF16)
-            else:
-                total[base + e] = square
+            near_left[side, e], near_right[side, e], total[base + e] = result
 
         in_groups(list(range(GX)), load, compute, store)
-    if rows != 2 * GX:
-        square_t[...] = total[...].astype(BF16)
+
+    def load_far(j):
+        own = [masked(cols[slot, j] >= 0, packed(own, j)[...]) for slot, own in zip(far_slots, (own_a, own_b))]
+        return jnp.concatenate(own, axis=1), jnp.concatenate([packed(far_a, j)[...], packed(far_b, j)[...]], axis=0), total[j]
+
+    in_groups(
+        list(range(rows)),
+        load_far,
+        lambda lhs, rhs, extra_t: (dot(lhs, rhs).T + extra_t).astype(BF16),
+        square_t.__setitem__,
+    )
+    for at, send in enumerate((square_a, square_b)):
+        for e in range(GX):
+            send[e] = square_t[bases[at] + e]
 
 
 def one_square(diag_own, x_t, diag_other):
@@ -188,14 +203,11 @@
 def inside_kernel(
     cols, own_a, own_b, diag_t, left_t, square_t, cube_in, diag_square_t, off_a, off_b,
     near_a, near_b, near_left, near_right,
-    out, send_a, send_b, far_left, far_right, near_square, cube_t, local_out, near_other, sem,
+    out, far_left, far_right, near_square, cube_t, local_out, near_other, sem,
 ):
     rows = diag_t.shape[0]
     edges = local_edges(rows)
     far_slots, _, bases = places(rows)
-    for at, send in ((1, send_b), (0, send_a)):
-        for e in range(GX):
-            send[e] = diag_square_t[bases[at] + e]
     copies = []
     for slot, place in ((2, 1), (4, 2), (1, 0), (5, 3)):
         own = [edge for edge in edges if edge[2] == place]
@@ -241,13 +253,13 @@
         slot = far_slots[at]
         in_groups(
             list(range(rows)),
-            lambda j: (cols[slot, j] >= 0, off[j]),
+            lambda j: (cols[slot, j] >= 0, packed(off, j)[...]),
             flipped,
             lambda j, value: far_left.__setitem__((at, j), value),
         )
         in_groups(
             list(range(rows)),
-            lambda j: (cols[slot, j] >= 0, own[j]),
+            lambda j: (cols[slot, j] >= 0, packed(own, j)[...]),
             flipped,
             lambda j, value: far_right.__setitem__((at, j), value),
         )
@@ -260,16 +272,16 @@
     out, far_square, far_other, diag_out, sem,
 ):
     rows = diag_t.shape[0]
-    for diag, at in ((diag_a, 0), (diag_b, 1)):
+    for at, diag in enumerate((diag_a, diag_b)):
         in_groups(
             list(range(rows)),
-            lambda j: (diag_t[j], far_left[at, j], diag[j]),
+            lambda j: (diag_t[j], far_left[at, j], packed(diag, j)[...]),
             one_square,
             lambda j, value: far_square.__setitem__((at, j), value),
         )
         in_groups(
             list(range(rows)),
-            lambda j: (diag[j], far_right[at, j], diag_t[j]),
+            lambda j: (packed(diag, j)[...], far_right[at, j], diag_t[j]),
             one_square,
             lambda j, value: far_other.__setitem__((at, j), value),
         )
@@ -363,50 +375,46 @@
     def near(value, pairing):
         return lax.ppermute(value, "row", near_pairs(pairing, layer_dist, count))
 
+    rows_and_spare = jax.ShapeDtypeStruct((rows * size + SPARE, size), BF16)
     send_a, send_b = call(
         pack_kernel,
         [hbm],
         [density],
-        [block(rows), block(rows)],
+        [rows_and_spare] * 2,
         [vmem] * 2,
         [dma((2,))],
         vmem_limit=STAGE_LIMIT,
     )
     off_b = far(send_b, 1)
     off_a = far(send_a, 0)
-    diag_t, left_t, square_t, cube_t, total, strip_a, strip_b = call(
+    diag_t, diag_send, left_t, square_t, cube_t, total, strip_a, strip_b = call(
         local_kernel,
         [smem, vmem],
         [cols, density],
         [
-            block(rows), block(4, rows), block(4, rows), wide(rows), wide(rows), block(2 * GX), block(2 * GX),
+            block(rows), rows_and_spare, block(4, rows), block(4, rows), wide(rows), wide(rows),
+            block(2 * GX), block(2 * GX),
         ],
-        [vmem] * 7,
+        [vmem] * 8,
         [],
     )
-    diag_b = far(diag_t, 1)
-    diag_a = far(diag_t, 0)
+    diag_b = far(diag_send, 1)
+    diag_a = far(diag_send, 0)
     near_b = near(strip_b, 1)
     near_a = near(strip_a, 0)
-    total = call(
-        far_terms_kernel,
-        [smem] + [vmem] * 5,
-        [cols, send_a, send_b, total, off_a, off_b],
-        wide(rows),
-        vmem,
-        [],
-    )
-    diag_square_t, near_left, near_right = call(
-        near_terms_kernel,
-        [smem] + [vmem] * 5,
-        [cols, strip_a, strip_b, total, near_a, near_b],
-        [block(rows), block(2, GX), block(2, GX)],
-        [vmem] * 3,
+    diag_square_t, near_left, near_right, square_a, square_b = call(
+        diag_square_kernel,
+        [smem] + [vmem] * 9,
+        [cols, strip_a, strip_b, send_a, send_b, total, near_a, near_b, off_a, off_b],
+        [block(rows), block(2, GX), block(2, GX), block(GX), block(GX)],
+        [vmem] * 5,
         [pltpu.VMEM((rows, size, size), F32)],
     )
     far_square_b = far(diag_square_t, 1)
     far_square_a = far(diag_square_t, 0)
-    out, square_a, square_b, far_left, far_right, near_square, cube_t = call(
+    near_square_b = near(square_b, 1)
+    near_square_a = near(square_a, 0)
+    out, far_left, far_right, near_square, cube_t = call(
         inside_kernel,
         [smem] + [vmem] * 13,
         [
@@ -414,13 +422,20 @@
             near_a, near_b, near_left, near_right,
         ],
         [
-            block(rows, K), block(GX), block(GX), block(2, rows), block(2, rows), block(2, GX), wide(rows),
+            block(rows, K), block(2, rows), block(2, rows), block(2, GX), wide(rows),
         ],
-        [hbm] + [vmem] * 6,
+        [hbm] + [vmem] * 4,
         [scratch(4, rows), scratch(2, GX), dma((4,))],
     )
-    near_square_b = near(square_b, 1)
-    near_square_a = near(square_a, 0)
+    out = call(
+        near_last_kernel,
+        [vmem] * 5 + [hbm],
+        [diag_t, near_left, near_square, near_square_a, near_square_b, out],
+        block(rows, K),
+        hbm,
+        [scratch(2, GX), dma((2,))],
+        alias=5,
+    )
     out, far_square = call(
         far_kernel,
         [vmem] * 7 + [hbm],
@@ -429,15 +444,6 @@
         [hbm, vmem],
         [scratch(2, rows), scratch(rows), dma],
         alias=7,
-    )
-    out = call(
-        near_last_kernel,
-        [vmem] * 5 + [hbm],
-        [diag_t, near_left, near_square, near_square_a, near_square_b, out],
-        block(rows, K),
-        hbm,
-        [scratch(2, GX), dma((2,))],
-        alias=5,
     )
     for side, far_diag_square in ((0, far_square_a), (1, far_square_b)):
         out = call(

time: 42.4 us -> 42.3 us (level)
  the two profiles are of different devices: /device:TPU:10 before, /device:TPU:11 now
where the time goes in v5:
time: 42.3 us; the launch traced here: 41.5 us
  starting transfers between devices  17.2 us (41%)
  Pallas kernels  15.1 us (36%)
  waiting for transfers between devices  9 us (21%)
    pallas_call x8, Pallas kernels, call(): pl.pallas_call(kernel, in_specs=in_specs, out_specs=out_specs, out_shape=...  15.1 us
    ppermute x6, starting transfers between devices, far(): return lax.ppermute(value, 'row', far_pairs(pairing, layer_dist, count))  9.42 us
    ppermute x4, starting transfers between devices, near(): return lax.ppermute(value, 'row', near_pairs(pairing, layer_dist, count))  7.81 us
    ppermute x4, waiting for transfers between devices, near(): return lax.ppermute(value, 'row', near_pairs(pairing, layer_dist, count))  6.96 us
    ppermute x6, waiting for transfers between devices, far(): return lax.ppermute(value, 'row', far_pairs(pairing, layer_dist, count))  2.04 us
  transfers between devices with their start and end apart: 10, of which 4 were waited for; matrix products, arithmetic and copies ran while one was open for 0% of the time, Pallas kernels for 30%

profile of v5, /device:TPU:11, one launch (start us, length us, event | category | flops | bytes accessed | tf_op | source)
XLA Modules:
  0.0 41.5 jit_solution(5428546796341923450)
XLA Ops:
  0.0 0.0 copy-start
  0.0 0.0 copy-start.1
  0.0 1.4 %shard_map.29 = (bf16[2064,128]{1,0:T(8,128)(2,1)S(1)}, bf16[2064,128]{1,0:T(8,128)(2,1)S(1)}) custom-call(bf16[16,7,128,128]{3,2,1,0:T(8,128)(2,1)} %blocks.3), custom_call_target="tpu_custom_call" | custom-call | bytes 1000 | tf_op jit(solution)/shard_map/pallas_call | solution.py:361
  1.4 0.2 collective-permute-start.2
  1.6 4.3 %collective-permute-start.3 = (bf16[2064,128]{1,0:T(8,128)(2,1)S(1)}, bf16[2064,128]{1,0:T(8,128)(2,1)S(1)}, u32[]{:S(2)}, u32[]{:S(2)}) collective-permute-start(bf16[2064,128]{1,0:T(8,128)(2,1)S(1)} %get-tuple-element.29.own_b), channel_id=1, source_target_pairs={{4,8},{5,9},{6,10},{7,11},{8,4},{9,5},{10,6},{11,7},{20,24},{21,25... | collective-permute-start | bytes 1585160 | tf_op jit(solution)/shard_map/ppermute | solution.py:373
  5.9 0.0 copy-done
  6.0 0.0 copy-done.1
  6.0 2.8 %shard_map.28 = (bf16[16,128,128]{2,1,0:T(8,128)(2,1)S(1)}, bf16[2064,128]{1,0:T(8,128)(2,1)S(1)}, bf16[4,16,128,128]{3,2,1,0:T(8,128)(2,1)S(1)}, bf16[4,16,128,...) custom-call(s32[7,16]{1,0:T(8,128)S(1)} %bitcast.1, ...), custom_call_target="tpu_custom_call" | custom-call | bytes 1000 | tf_op jit(solution)/shard_map/pallas_call | solution.py:361
  8.8 1.3 %collective-permute-start = (bf16[16,128,128]{2,1,0:T(8,128)(2,1)S(1)}, bf16[16,128,128]{2,1,0:T(8,128)(2,1)S(1)}, u32[]{:S(2)}, u32[]{:S(2)}) collective-permute-start(bf16[16,128,128]{2,1,0:T(8,128)(2,1)S(1)} %get-tuple-element.33.strip_a), channel_id=1, source_target_pairs={{0,1},{1,0},{2,3},{3,2},{4,5},{5,4},{6,7},{7,6},{8,9},{9,8},{10,11... | collective-permute-start | bytes 1572872 | tf_op jit(solution)/shard_map/ppermute | solution.py:376
  10.1 3.0 %collective-permute-start.1 = (bf16[16,128,128]{2,1,0:T(8,128)(2,1)S(1)}, bf16[16,128,128]{2,1,0:T(8,128)(2,1)S(1)}, u32[]{:S(2)}, u32[]{:S(2)}) collective-permute-start(bf16[16,128,128]{2,1,0:T(8,128)(2,1)S(1)} %get-tuple-element.34.strip_b), channel_id=1, source_target_pairs={{1,2},{2,1},{5,6},{6,5},{9,10},{10,9},{13,14},{14,13},{17,18},{18,... | collective-permute-start | bytes 1572872 | tf_op jit(solution)/shard_map/ppermute | solution.py:376
  13.1 1.9 %collective-permute-start.5 = (bf16[2064,128]{1,0:T(8,128)(2,1)S(1)}, bf16[2064,128]{1,0:T(8,128)(2,1)S(1)}, u32[]{:S(2)}, u32[]{:S(2)}) collective-permute-start(bf16[2064,128]{1,0:T(8,128)(2,1)S(1)} %get-tuple-element.42), channel_id=1, source_target_pairs={{4,8},{5,9},{6,10},{7,11},{8,4},{9,5},{10,6},{11,7},{20,24},{21,25... | collective-permute-start | bytes 1585160 | tf_op jit(solution)/shard_map/ppermute | solution.py:373
  15.0 0.0 collective-permute-done.near_a
  15.1 0.1 collective-permute-start.4
  15.1 5.7 %collective-permute-done.1.near_b = bf16[16,128,128]{2,1,0:T(8,128)(2,1)S(1)} collective-permute-done((bf16[16,128,128]{2,1,0:T(8,128)(2,1)S(1)}, bf16[16,128,128]{2,1,0:T(8,128)(2,1)S(1)}, u32[]{:S(2)}, u32[]{:S(2)}) %collective-permute-start.1) | collective-permute-done | bytes 524320 | tf_op jit(solution)/shard_map/ppermute | solution.py:376
  20.8 0.0 collective-permute-done.2.far_a.off_a
  20.8 0.0 collective-permute-done.3.far_b.off_b
  20.8 1.6 %shard_map.30 = (bf16[16,128,128]{2,1,0:T(8,128)(2,1)S(1)}, bf16[2,8,128,128]{3,2,1,0:T(8,128)(2,1)S(1)}, bf16[2,8,128,128]{3,2,1,0:T(8,128)(2,1)S(1)}, bf16[8,1...) custom-call(s32[7,16]{1,0:T(8,128)S(1)} %bitcast.2, bf16[16,128,128]{2,1,0:T(8,128)(2,1)S(1)} %get-tuple-element.33.strip_a, ...), custom_call_target="tpu_custom_call" | custom-call | bytes 1000 | tf_op jit(solution)/shard_map/pallas_call | solution.py:361
  22.5 0.1 collective-permute-start.6
  22.6 0.1 collective-permute-start.9
  22.6 2.8 %collective-permute-start.8 = (bf16[16,128,128]{2,1,0:T(8,128)(2,1)S(1)}, bf16[16,128,128]{2,1,0:T(8,128)(2,1)S(1)}, u32[]{:S(2)}, u32[]{:S(2)}) collective-permute-start(bf16[16,128,128]{2,1,0:T(8,128)(2,1)S(1)} %get-tuple-element.36.diag_square_t), channel_id=1, source_target_pairs={{4,8},{5,9},{6,10},{7,11},{8,4},{9,5},{10,6},{11,7},{20,24},{21,25... | collective-permute-start | bytes 1572872 | tf_op jit(solution)/shard_map/ppermute | solution.py:373
  25.5 0.0 collective-permute-done.6.near_a
  25.5 3.4 %collective-permute-start.7 = (bf16[8,128,128]{2,1,0:T(8,128)(2,1)S(1)}, bf16[8,128,128]{2,1,0:T(8,128)(2,1)S(1)}, u32[]{:S(2)}, u32[]{:S(2)}) collective-permute-start(bf16[8,128,128]{2,1,0:T(8,128)(2,1)S(1)} %get-tuple-element.45), channel_id=1, source_target_pairs={{1,2},{2,1},{5,6},{6,5},{9,10},{10,9},{13,14},{14,13},{17,18},{18,... | collective-permute-start | bytes 786440 | tf_op jit(solution)/shard_map/ppermute | solution.py:376
  28.9 3.3 %shard_map.31 = (bf16[16,7,128,128]{3,2,1,0:T(8,128)(2,1)}, bf16[2,16,128,128]{3,2,1,0:T(8,128)(2,1)S(1)}, bf16[2,16,128,128]{3,2,1,0:T(8,128)(2,1)S(1)}, bf16[2...) custom-call(s32[7,16]{1,0:T(8,128)S(1)} %bitcast.3, bf16[2064,128]{1,0:T(8,128)(2,1)S(1)} %get-tuple-element.28.own_a, ...), custom_call_target="tpu_custom_call" | custom-call | bytes 1000 | tf_op jit(solution)/shard_map/pallas_call | solution.py:361
  32.2 1.2 %collective-permute-done.7.near_b = bf16[8,128,128]{2,1,0:T(8,128)(2,1)S(1)} collective-permute-done((bf16[8,128,128]{2,1,0:T(8,128)(2,1)S(1)}, bf16[8,128,128]{2,1,0:T(8,128)(2,1)S(1)}, u32[]{:S(2)}, u32[]{:S(2)}) %collective-permute-start.7) | collective-permute-done | bytes 262176 | tf_op jit(solution)/shard_map/ppermute | solution.py:376
  33.5 1.2 %shard_map.32.old = bf16[16,7,128,128]{3,2,1,0:T(8,128)(2,1)} custom-call(bf16[16,128,128]{2,1,0:T(8,128)(2,1)S(1)} %get-tuple-element.27.diag_t, bf16[2,8,128,128]{3,2,1,0:T(8,128)(2,1)S(1)} %get-tuple-element.37.near_left, bf16[2,8,128,128]{3,2,1,0:T(8,128)(2,1)S(1)} %get-tuple-element.43.near_square, ...), custom_call_target="tpu_custom_call", output_to_operand_aliasing={{}: (5, {})} | custom-call | bytes 1000 | tf_op jit(solution)/shard_map/pallas_call | solution.py:361
  34.6 0.0 collective-permute-done.5.diag_b
  34.6 0.0 collective-permute-done.4.diag_a
  34.6 2.5 %shard_map.33 = (bf16[16,7,128,128]{3,2,1,0:T(8,128)(2,1)}, bf16[2,16,128,128]{3,2,1,0:T(8,128)(2,1)S(1)}) custom-call(bf16[16,128,128]{2,1,0:T(8,128)(2,1)S(1)} %get-tuple-element.27.diag_t, f32[16,128,128]{2,1,0:T(8,128)S(1)} %get-tuple-element.40.cube_t, ...), custom_call_target="tpu_custom_call", output_to_operand_aliasing={{0}: (7, {})} | custom-call | bytes 1000 | tf_op jit(solution)/shard_map/pallas_call | solution.py:361
  37.2 1.3 %collective-permute-done.9.far = bf16[16,128,128]{2,1,0:T(8,128)(2,1)S(1)} collective-permute-done((bf16[16,128,128]{2,1,0:T(8,128)(2,1)S(1)}, bf16[16,128,128]{2,1,0:T(8,128)(2,1)S(1)}, u32[]{:S(2)}, u32[]{:S(2)}) %collective-permute-start.9) | collective-permute-done | bytes 524320 | tf_op jit(solution)/shard_map/ppermute | solution.py:373
  38.5 1.1 %shard_map.34.old = bf16[16,7,128,128]{3,2,1,0:T(8,128)(2,1)} custom-call(bf16[16,128,128]{2,1,0:T(8,128)(2,1)S(1)} %get-tuple-element.27.diag_t, bf16[2,16,128,128]{3,2,1,0:T(8,128)(2,1)S(1)} %get-tuple-element.39.far_left, bf16[2,16,128,128]{3,2,1,0:T(8,128)(2,1)S(1)} %get-tuple-element.47.far_square, ...), custom_call_target="tpu_custom_call", output_to_operand_aliasing={{}: (4, {})} | custom-call | bytes 1000 | tf_op jit(solution)/shard_map/pallas_call | solution.py:361
  39.7 0.7 %collective-permute-done.8.far = bf16[16,128,128]{2,1,0:T(8,128)(2,1)S(1)} collective-permute-done((bf16[16,128,128]{2,1,0:T(8,128)(2,1)S(1)}, bf16[16,128,128]{2,1,0:T(8,128)(2,1)S(1)}, u32[]{:S(2)}, u32[]{:S(2)}) %collective-permute-start.8) | collective-permute-done | bytes 524320 | tf_op jit(solution)/shard_map/ppermute | solution.py:373
  40.3 1.1 %shard_map.35 = bf16[16,7,128,128]{3,2,1,0:T(8,128)(2,1)} custom-call(bf16[16,128,128]{2,1,0:T(8,128)(2,1)S(1)} %get-tuple-element.27.diag_t, bf16[2,16,128,128]{3,2,1,0:T(8,128)(2,1)S(1)} %get-tuple-element.39.far_left, bf16[2,16,128,128]{3,2,1,0:T(8,128)(2,1)S(1)} %get-tuple-element.47.far_square, ...), custom_call_target="tpu_custom_call", output_to_operand_aliasing={{}: (4, {})} | custom-call | bytes 1000 | tf_op jit(solution)/shard_map/pallas_call | solution.py:361
Async XLA Ops:
  0.0 5.9 %copy-start = (bf16[16,7,128,128]{3,2,1,0:T(8,128)(2,1)S(1)}, bf16[16,7,128,128]{3,2,1,0:T(8,128)(2,1)}, u32[]{:S(2)}) copy-start(bf16[16,7,128,128]{3,2,1,0:T(8,128)(2,1)} %blocks.3) | copy-start | bytes 11010052
  0.0 6.0 %copy-start.1 = (s32[16,7]{0,1:T(8,128)S(1)}, s32[16,7]{0,1:T(8,128)}, u32[]{:S(2)}) copy-start(s32[16,7]{0,1:T(8,128)} %param.3) | copy-start | bytes 1348
  1.4 19.5 %collective-permute-start.2 = (bf16[2064,128]{1,0:T(8,128)(2,1)S(1)}, bf16[2064,128]{1,0:T(8,128)(2,1)S(1)}, u32[]{:S(2)}, u32[]{:S(2)}) collective-permute-start(bf16[2064,128]{1,0:T(8,128)(2,1)S(1)} %get-tuple-element.28.own_a), channel_id=1, source_target_pairs={{0,4},{1,5},{2,6},{3,7},{4,0},{5,1},{6,2},{7,3},{8,12},{9,13},{10,... | collective-permute-start | bytes 1585160 | tf_op jit(solution)/shard_map/ppermute | solution.py:373
  1.6 19.2 %collective-permute-start.3 = (bf16[2064,128]{1,0:T(8,128)(2,1)S(1)}, bf16[2064,128]{1,0:T(8,128)(2,1)S(1)}, u32[]{:S(2)}, u32[]{:S(2)}) collective-permute-start(bf16[2064,128]{1,0:T(8,128)(2,1)S(1)} %get-tuple-element.29.own_b), channel_id=1, source_target_pairs={{4,8},{5,9},{6,10},{7,11},{8,4},{9,5},{10,6},{11,7},{20,24},{21,25... | collective-permute-start | bytes 1585160 | tf_op jit(solution)/shard_map/ppermute | solution.py:373
  8.8 6.3 %collective-permute-start = (bf16[16,128,128]{2,1,0:T(8,128)(2,1)S(1)}, bf16[16,128,128]{2,1,0:T(8,128)(2,1)S(1)}, u32[]{:S(2)}, u32[]{:S(2)}) collective-permute-start(bf16[16,128,128]{2,1,0:T(8,128)(2,1)S(1)} %get-tuple-element.33.strip_a), channel_id=1, source_target_pairs={{0,1},{1,0},{2,3},{3,2},{4,5},{5,4},{6,7},{7,6},{8,9},{9,8},{10,11... | collective-permute-start | bytes 1572872 | tf_op jit(solution)/shard_map/ppermute | solution.py:376
  10.1 10.8 %collective-permute-start.1 = (bf16[16,128,128]{2,1,0:T(8,128)(2,1)S(1)}, bf16[16,128,128]{2,1,0:T(8,128)(2,1)S(1)}, u32[]{:S(2)}, u32[]{:S(2)}) collective-permute-start(bf16[16,128,128]{2,1,0:T(8,128)(2,1)S(1)} %get-tuple-element.34.strip_b), channel_id=1, source_target_pairs={{1,2},{2,1},{5,6},{6,5},{9,10},{10,9},{13,14},{14,13},{17,18},{18,... | collective-permute-start | bytes 1572872 | tf_op jit(solution)/shard_map/ppermute | solution.py:376
  13.1 21.5 %collective-permute-start.5 = (bf16[2064,128]{1,0:T(8,128)(2,1)S(1)}, bf16[2064,128]{1,0:T(8,128)(2,1)S(1)}, u32[]{:S(2)}, u32[]{:S(2)}) collective-permute-start(bf16[2064,128]{1,0:T(8,128)(2,1)S(1)} %get-tuple-element.42), channel_id=1, source_target_pairs={{4,8},{5,9},{6,10},{7,11},{8,4},{9,5},{10,6},{11,7},{20,24},{21,25... | collective-permute-start | bytes 1585160 | tf_op jit(solution)/shard_map/ppermute | solution.py:373
  15.1 19.6 %collective-permute-start.4 = (bf16[2064,128]{1,0:T(8,128)(2,1)S(1)}, bf16[2064,128]{1,0:T(8,128)(2,1)S(1)}, u32[]{:S(2)}, u32[]{:S(2)}) collective-permute-start(bf16[2064,128]{1,0:T(8,128)(2,1)S(1)} %get-tuple-element.42), channel_id=1, source_target_pairs={{0,4},{1,5},{2,6},{3,7},{4,0},{5,1},{6,2},{7,3},{8,12},{9,13},{10,... | collective-permute-start | bytes 1585160 | tf_op jit(solution)/shard_map/ppermute | solution.py:373
  22.5 3.0 %collective-permute-start.6 = (bf16[8,128,128]{2,1,0:T(8,128)(2,1)S(1)}, bf16[8,128,128]{2,1,0:T(8,128)(2,1)S(1)}, u32[]{:S(2)}, u32[]{:S(2)}) collective-permute-start(bf16[8,128,128]{2,1,0:T(8,128)(2,1)S(1)} %get-tuple-element.44), channel_id=1, source_target_pairs={{0,1},{1,0},{2,3},{3,2},{4,5},{5,4},{6,7},{7,6},{8,9},{9,8},{10,11... | collective-permute-start | bytes 786440 | tf_op jit(solution)/shard_map/ppermute | solution.py:376
  22.6 15.9 %collective-permute-start.9 = (bf16[16,128,128]{2,1,0:T(8,128)(2,1)S(1)}, bf16[16,128,128]{2,1,0:T(8,128)(2,1)S(1)}, u32[]{:S(2)}, u32[]{:S(2)}) collective-permute-start(bf16[16,128,128]{2,1,0:T(8,128)(2,1)S(1)} %get-tuple-element.36.diag_square_t), channel_id=1, source_target_pairs={{0,4},{1,5},{2,6},{3,7},{4,0},{5,1},{6,2},{7,3},{8,12},{9,13},{10,... | collective-permute-start | bytes 1572872 | tf_op jit(solution)/shard_map/ppermute | solution.py:373
  22.6 17.7 %collective-permute-start.8 = (bf16[16,128,128]{2,1,0:T(8,128)(2,1)S(1)}, bf16[16,128,128]{2,1,0:T(8,128)(2,1)S(1)}, u32[]{:S(2)}, u32[]{:S(2)}) collective-permute-start(bf16[16,128,128]{2,1,0:T(8,128)(2,1)S(1)} %get-tuple-element.36.diag_square_t), channel_id=1, source_target_pairs={{4,8},{5,9},{6,10},{7,11},{8,4},{9,5},{10,6},{11,7},{20,24},{21,25... | collective-permute-start | bytes 1572872 | tf_op jit(solution)/shard_map/ppermute | solution.py:373
  25.5 8.0 %collective-permute-start.7 = (bf16[8,128,128]{2,1,0:T(8,128)(2,1)S(1)}, bf16[8,128,128]{2,1,0:T(8,128)(2,1)S(1)}, u32[]{:S(2)}, u32[]{:S(2)}) collective-permute-start(bf16[8,128,128]{2,1,0:T(8,128)(2,1)S(1)} %get-tuple-element.45), channel_id=1, source_target_pairs={{1,2},{2,1},{5,6},{6,5},{9,10},{10,9},{13,14},{14,13},{17,18},{18,... | collective-permute-start | bytes 786440 | tf_op jit(solution)/shard_map/ppermute | solution.py:376

commit v6 on v5

--- a/solution.py
+++ b/solution.py
@@ -269,7 +269,7 @@
 
 def far_kernel(
     diag_t, cube_t, diag_square_t, far_left, far_right, diag_a, diag_b, old,
-    out, far_square, far_other, diag_out, sem,
+    out, far_part, far_square, far_other, diag_out, sem,
 ):
     rows = diag_t.shape[0]
     for at, diag in enumerate((diag_a, diag_b)):
@@ -278,6 +278,12 @@
             lambda j: (diag_t[j], far_left[at, j], packed(diag, j)[...]),
             one_square,
             lambda j, value: far_square.__setitem__((at, j), value),
+        )
+        in_groups(
+            list(range(rows)),
+            lambda j: (diag_t[j], far_square[at, j]),
+            lambda diag_own, square: 3.0 * square.astype(F32) - 2.0 * dot(diag_own, square),
+            lambda j, value: far_part.__setitem__((at, j), value),
         )
         in_groups(
             list(range(rows)),
@@ -318,16 +324,16 @@
         copy.wait()
 
 
-def far_last_kernel(side, diag_t, far_left, far_square, far, old, out, far_out, sem):
-    rows = diag_t.shape[0]
+def far_last_kernel(side, far_left, far_part, far, old, out, far_out, sem):
+    rows = far.shape[0]
     slot = places(rows)[0][side]
     copies = []
     for part in range(rows // GX):
         first = part * GX
         in_groups(
             list(range(first, first + GX)),
-            lambda j: (diag_t[j], far_left[side, j], far_square[side, j], far[j]),
-            finish,
+            lambda j: (far_left[side, j], far[j], far_part[side, j]),
+            lambda x_t, square, part: (part - 2.0 * dot(x_t, square)).astype(BF16),
             far_out.__setitem__,
         )
         at = pl.ds(first, GX)
@@ -436,24 +442,24 @@
         [scratch(2, GX), dma((2,))],
         alias=5,
     )
-    out, far_square = call(
+    out, far_part = call(
         far_kernel,
         [vmem] * 7 + [hbm],
         [diag_t, cube_t, diag_square_t, far_left, far_right, diag_a, diag_b, out],
-        [block(rows, K), block(2, rows)],
+        [block(rows, K), wide(2, rows)],
         [hbm, vmem],
-        [scratch(2, rows), scratch(rows), dma],
+        [scratch(2, rows), scratch(2, rows), scratch(rows), dma],
         alias=7,
     )
     for side, far_diag_square in ((0, far_square_a), (1, far_square_b)):
         out = call(
             functools.partial(far_last_kernel, side),
-            [vmem] * 4 + [hbm],
-            [diag_t, far_left, far_square, far_diag_square, out],
+            [vmem] * 3 + [hbm],
+            [far_left, far_part, far_diag_square, out],
             block(rows, K),
             hbm,
             [scratch(rows), dma((rows // GX,))],
-            alias=4,
+            alias=3,
         )
     return out
 

time: 42.3 us -> 42.2 us (level)
  transfers between devices with their start and end apart: 10 -> 10, of which waited for: 4 -> 4; matrix products, arithmetic and copies ran while one was open for 0% -> 0% of each run, Pallas kernels for 30% -> 31%
where the time goes in v6:
time: 42.2 us; the launch traced here: 41.4 us
  starting transfers between devices  17.2 us (41%)
  Pallas kernels  15.2 us (36%)
  waiting for transfers between devices  8.74 us (21%)
    pallas_call x8, Pallas kernels, call(): pl.pallas_call(kernel, in_specs=in_specs, out_specs=out_specs, out_shape=...  15.2 us
    ppermute x6, starting transfers between devices, far(): return lax.ppermute(value, 'row', far_pairs(pairing, layer_dist, count))  9.42 us
    ppermute x4, starting transfers between devices, near(): return lax.ppermute(value, 'row', near_pairs(pairing, layer_dist, count))  7.81 us
    ppermute x4, waiting for transfers between devices, near(): return lax.ppermute(value, 'row', near_pairs(pairing, layer_dist, count))  6.95 us
    ppermute x6, waiting for transfers between devices, far(): return lax.ppermute(value, 'row', far_pairs(pairing, layer_dist, count))  1.78 us
  transfers between devices with their start and end apart: 10, of which 4 were waited for; matrix products, arithmetic and copies ran while one was open for 0% of the time, Pallas kernels for 31%

profile of v6, /device:TPU:11, one launch (start us, length us, event | category | flops | bytes accessed | tf_op | source)
XLA Modules:
  0.0 41.4 jit_solution(10188881400370562788)
XLA Ops:
  0.0 0.0 copy-start
  0.0 0.0 copy-start.1
  0.0 1.4 %shard_map.28 = (bf16[2064,128]{1,0:T(8,128)(2,1)S(1)}, bf16[2064,128]{1,0:T(8,128)(2,1)S(1)}) custom-call(bf16[16,7,128,128]{3,2,1,0:T(8,128)(2,1)} %blocks.3), custom_call_target="tpu_custom_call" | custom-call | bytes 1000 | tf_op jit(solution)/shard_map/pallas_call | solution.py:367
  1.4 0.2 collective-permute-start.2
  1.6 4.3 %collective-permute-start.3 = (bf16[2064,128]{1,0:T(8,128)(2,1)S(1)}, bf16[2064,128]{1,0:T(8,128)(2,1)S(1)}, u32[]{:S(2)}, u32[]{:S(2)}) collective-permute-start(bf16[2064,128]{1,0:T(8,128)(2,1)S(1)} %get-tuple-element.28.own_b), channel_id=1, source_target_pairs={{4,8},{5,9},{6,10},{7,11},{8,4},{9,5},{10,6},{11,7},{20,24},{21,25... | collective-permute-start | bytes 1585160 | tf_op jit(solution)/shard_map/ppermute | solution.py:379
  5.9 0.0 copy-done
  6.0 0.0 copy-done.1
  6.0 2.8 %shard_map.29 = (bf16[16,128,128]{2,1,0:T(8,128)(2,1)S(1)}, bf16[2064,128]{1,0:T(8,128)(2,1)S(1)}, bf16[4,16,128,128]{3,2,1,0:T(8,128)(2,1)S(1)}, bf16[4,16,128,...) custom-call(s32[7,16]{1,0:T(8,128)S(1)} %bitcast.1, ...), custom_call_target="tpu_custom_call" | custom-call | bytes 1000 | tf_op jit(solution)/shard_map/pallas_call | solution.py:367
  8.8 1.3 %collective-permute-start = (bf16[16,128,128]{2,1,0:T(8,128)(2,1)S(1)}, bf16[16,128,128]{2,1,0:T(8,128)(2,1)S(1)}, u32[]{:S(2)}, u32[]{:S(2)}) collective-permute-start(bf16[16,128,128]{2,1,0:T(8,128)(2,1)S(1)} %get-tuple-element.33.strip_a), channel_id=1, source_target_pairs={{0,1},{1,0},{2,3},{3,2},{4,5},{5,4},{6,7},{7,6},{8,9},{9,8},{10,11... | collective-permute-start | bytes 1572872 | tf_op jit(solution)/shard_map/ppermute | solution.py:382
  10.1 3.0 %collective-permute-start.1 = (bf16[16,128,128]{2,1,0:T(8,128)(2,1)S(1)}, bf16[16,128,128]{2,1,0:T(8,128)(2,1)S(1)}, u32[]{:S(2)}, u32[]{:S(2)}) collective-permute-start(bf16[16,128,128]{2,1,0:T(8,128)(2,1)S(1)} %get-tuple-element.34.strip_b), channel_id=1, source_target_pairs={{1,2},{2,1},{5,6},{6,5},{9,10},{10,9},{13,14},{14,13},{17,18},{18,... | collective-permute-start | bytes 1572872 | tf_op jit(solution)/shard_map/ppermute | solution.py:382
  13.1 1.9 %collective-permute-start.5 = (bf16[2064,128]{1,0:T(8,128)(2,1)S(1)}, bf16[2064,128]{1,0:T(8,128)(2,1)S(1)}, u32[]{:S(2)}, u32[]{:S(2)}) collective-permute-start(bf16[2064,128]{1,0:T(8,128)(2,1)S(1)} %get-tuple-element.42), channel_id=1, source_target_pairs={{4,8},{5,9},{6,10},{7,11},{8,4},{9,5},{10,6},{11,7},{20,24},{21,25... | collective-permute-start | bytes 1585160 | tf_op jit(solution)/shard_map/ppermute | solution.py:379
  15.0 0.0 collective-permute-done.near_a
  15.1 0.1 collective-permute-start.4
  15.1 5.7 %collective-permute-done.1.near_b = bf16[16,128,128]{2,1,0:T(8,128)(2,1)S(1)} collective-permute-done((bf16[16,128,128]{2,1,0:T(8,128)(2,1)S(1)}, bf16[16,128,128]{2,1,0:T(8,128)(2,1)S(1)}, u32[]{:S(2)}, u32[]{:S(2)}) %collective-permute-start.1) | collective-permute-done | bytes 524320 | tf_op jit(solution)/shard_map/ppermute | solution.py:382
  20.8 0.0 collective-permute-done.2.far_a.off_a
  20.8 0.0 collective-permute-done.3.far_b.off_b
  20.9 1.6 %shard_map.30 = (bf16[16,128,128]{2,1,0:T(8,128)(2,1)S(1)}, bf16[2,8,128,128]{3,2,1,0:T(8,128)(2,1)S(1)}, bf16[2,8,128,128]{3,2,1,0:T(8,128)(2,1)S(1)}, bf16[8,1...) custom-call(s32[7,16]{1,0:T(8,128)S(1)} %bitcast.2, bf16[16,128,128]{2,1,0:T(8,128)(2,1)S(1)} %get-tuple-element.33.strip_a, ...), custom_call_target="tpu_custom_call" | custom-call | bytes 1000 | tf_op jit(solution)/shard_map/pallas_call | solution.py:367
  22.5 0.1 collective-permute-start.6
  22.6 0.1 collective-permute-start.9
  22.6 2.8 %collective-permute-start.8 = (bf16[16,128,128]{2,1,0:T(8,128)(2,1)S(1)}, bf16[16,128,128]{2,1,0:T(8,128)(2,1)S(1)}, u32[]{:S(2)}, u32[]{:S(2)}) collective-permute-start(bf16[16,128,128]{2,1,0:T(8,128)(2,1)S(1)} %get-tuple-element.36.diag_square_t), channel_id=1, source_target_pairs={{4,8},{5,9},{6,10},{7,11},{8,4},{9,5},{10,6},{11,7},{20,24},{21,25... | collective-permute-start | bytes 1572872 | tf_op jit(solution)/shard_map/ppermute | solution.py:379
  25.5 0.0 collective-permute-done.6.near_a
  25.5 3.4 %collective-permute-start.7 = (bf16[8,128,128]{2,1,0:T(8,128)(2,1)S(1)}, bf16[8,128,128]{2,1,0:T(8,128)(2,1)S(1)}, u32[]{:S(2)}, u32[]{:S(2)}) collective-permute-start(bf16[8,128,128]{2,1,0:T(8,128)(2,1)S(1)} %get-tuple-element.45), channel_id=1, source_target_pairs={{1,2},{2,1},{5,6},{6,5},{9,10},{10,9},{13,14},{14,13},{17,18},{18,... | collective-permute-start | bytes 786440 | tf_op jit(solution)/shard_map/ppermute | solution.py:382
  28.9 3.3 %shard_map.31 = (bf16[16,7,128,128]{3,2,1,0:T(8,128)(2,1)}, bf16[2,16,128,128]{3,2,1,0:T(8,128)(2,1)S(1)}, bf16[2,16,128,128]{3,2,1,0:T(8,128)(2,1)S(1)}, bf16[2...) custom-call(s32[7,16]{1,0:T(8,128)S(1)} %bitcast.3, bf16[2064,128]{1,0:T(8,128)(2,1)S(1)} %get-tuple-element.27.own_a, ...), custom_call_target="tpu_custom_call" | custom-call | bytes 1000 | tf_op jit(solution)/shard_map/pallas_call | solution.py:367
  32.2 1.2 %collective-permute-done.7.near_b = bf16[8,128,128]{2,1,0:T(8,128)(2,1)S(1)} collective-permute-done((bf16[8,128,128]{2,1,0:T(8,128)(2,1)S(1)}, bf16[8,128,128]{2,1,0:T(8,128)(2,1)S(1)}, u32[]{:S(2)}, u32[]{:S(2)}) %collective-permute-start.7) | collective-permute-done | bytes 262176 | tf_op jit(solution)/shard_map/ppermute | solution.py:382
  33.5 1.2 %shard_map.32.old = bf16[16,7,128,128]{3,2,1,0:T(8,128)(2,1)} custom-call(bf16[16,128,128]{2,1,0:T(8,128)(2,1)S(1)} %get-tuple-element.29.diag_t, bf16[2,8,128,128]{3,2,1,0:T(8,128)(2,1)S(1)} %get-tuple-element.37.near_left, bf16[2,8,128,128]{3,2,1,0:T(8,128)(2,1)S(1)} %get-tuple-element.43.near_square, ...), custom_call_target="tpu_custom_call", output_to_operand_aliasing={{}: (5, {})} | custom-call | bytes 1000 | tf_op jit(solution)/shard_map/pallas_call | solution.py:367
  34.6 0.0 collective-permute-done.5.diag_b
  34.6 0.0 collective-permute-done.4.diag_a
  34.6 2.9 %shard_map.33 = (bf16[16,7,128,128]{3,2,1,0:T(8,128)(2,1)}, f32[2,16,128,128]{3,2,1,0:T(8,128)S(1)}) custom-call(bf16[16,128,128]{2,1,0:T(8,128)(2,1)S(1)} %get-tuple-element.29.diag_t, f32[16,128,128]{2,1,0:T(8,128)S(1)} %get-tuple-element.40.cube_t, bf16[16,128,128]{2,1,0:T(8,128)(2,1)S(1)} %get-tuple-element.36.diag_square_t, ...), custom_call_target="tpu_custom_call", output_to_operand_aliasing={{0}: (7, {})} | custom-call | bytes 1000 | tf_op jit(solution)/shard_map/pallas_call | solution.py:367
  37.5 1.0 %collective-permute-done.9.far = bf16[16,128,128]{2,1,0:T(8,128)(2,1)S(1)} collective-permute-done((bf16[16,128,128]{2,1,0:T(8,128)(2,1)S(1)}, bf16[16,128,128]{2,1,0:T(8,128)(2,1)S(1)}, u32[]{:S(2)}, u32[]{:S(2)}) %collective-permute-start.9) | collective-permute-done | bytes 524320 | tf_op jit(solution)/shard_map/ppermute | solution.py:379
  38.5 1.0 %shard_map.34.old = bf16[16,7,128,128]{3,2,1,0:T(8,128)(2,1)} custom-call(bf16[2,16,128,128]{3,2,1,0:T(8,128)(2,1)S(1)} %get-tuple-element.39.far_left, f32[2,16,128,128]{3,2,1,0:T(8,128)S(1)} %get-tuple-element.47.far_part, bf16[16,128,128]{2,1,0:T(8,128)(2,1)S(1)} %collective-permute-done.9.far, ...), custom_call_target="tpu_custom_call", output_to_operand_aliasing={{}: (3, {})} | custom-call | bytes 1000 | tf_op jit(solution)/shard_map/pallas_call | solution.py:367
  39.6 0.8 %collective-permute-done.8.far = bf16[16,128,128]{2,1,0:T(8,128)(2,1)S(1)} collective-permute-done((bf16[16,128,128]{2,1,0:T(8,128)(2,1)S(1)}, bf16[16,128,128]{2,1,0:T(8,128)(2,1)S(1)}, u32[]{:S(2)}, u32[]{:S(2)}) %collective-permute-start.8) | collective-permute-done | bytes 524320 | tf_op jit(solution)/shard_map/ppermute | solution.py:379
  40.3 1.0 %shard_map.35 = bf16[16,7,128,128]{3,2,1,0:T(8,128)(2,1)} custom-call(bf16[2,16,128,128]{3,2,1,0:T(8,128)(2,1)S(1)} %get-tuple-element.39.far_left, f32[2,16,128,128]{3,2,1,0:T(8,128)S(1)} %get-tuple-element.47.far_part, bf16[16,128,128]{2,1,0:T(8,128)(2,1)S(1)} %collective-permute-done.8.far, ...), custom_call_target="tpu_custom_call", output_to_operand_aliasing={{}: (3, {})} | custom-call | bytes 1000 | tf_op jit(solution)/shard_map/pallas_call | solution.py:367
Async XLA Ops:
  0.0 5.9 %copy-start = (bf16[16,7,128,128]{3,2,1,0:T(8,128)(2,1)S(1)}, bf16[16,7,128,128]{3,2,1,0:T(8,128)(2,1)}, u32[]{:S(2)}) copy-start(bf16[16,7,128,128]{3,2,1,0:T(8,128)(2,1)} %blocks.3) | copy-start | bytes 11010052
  0.0 6.0 %copy-start.1 = (s32[16,7]{0,1:T(8,128)S(1)}, s32[16,7]{0,1:T(8,128)}, u32[]{:S(2)}) copy-start(s32[16,7]{0,1:T(8,128)} %param.3) | copy-start | bytes 1348
  1.4 19.5 %collective-permute-start.2 = (bf16[2064,128]{1,0:T(8,128)(2,1)S(1)}, bf16[2064,128]{1,0:T(8,128)(2,1)S(1)}, u32[]{:S(2)}, u32[]{:S(2)}) collective-permute-start(bf16[2064,128]{1,0:T(8,128)(2,1)S(1)} %get-tuple-element.27.own_a), channel_id=1, source_target_pairs={{0,4},{1,5},{2,6},{3,7},{4,0},{5,1},{6,2},{7,3},{8,12},{9,13},{10,... | collective-permute-start | bytes 1585160 | tf_op jit(solution)/shard_map/ppermute | solution.py:379
  1.6 19.2 %collective-permute-start.3 = (bf16[2064,128]{1,0:T(8,128)(2,1)S(1)}, bf16[2064,128]{1,0:T(8,128)(2,1)S(1)}, u32[]{:S(2)}, u32[]{:S(2)}) collective-permute-start(bf16[2064,128]{1,0:T(8,128)(2,1)S(1)} %get-tuple-element.28.own_b), channel_id=1, source_target_pairs={{4,8},{5,9},{6,10},{7,11},{8,4},{9,5},{10,6},{11,7},{20,24},{21,25... | collective-permute-start | bytes 1585160 | tf_op jit(solution)/shard_map/ppermute | solution.py:379
  8.8 6.3 %collective-permute-start = (bf16[16,128,128]{2,1,0:T(8,128)(2,1)S(1)}, bf16[16,128,128]{2,1,0:T(8,128)(2,1)S(1)}, u32[]{:S(2)}, u32[]{:S(2)}) collective-permute-start(bf16[16,128,128]{2,1,0:T(8,128)(2,1)S(1)} %get-tuple-element.33.strip_a), channel_id=1, source_target_pairs={{0,1},{1,0},{2,3},{3,2},{4,5},{5,4},{6,7},{7,6},{8,9},{9,8},{10,11... | collective-permute-start | bytes 1572872 | tf_op jit(solution)/shard_map/ppermute | solution.py:382
  10.1 10.8 %collective-permute-start.1 = (bf16[16,128,128]{2,1,0:T(8,128)(2,1)S(1)}, bf16[16,128,128]{2,1,0:T(8,128)(2,1)S(1)}, u32[]{:S(2)}, u32[]{:S(2)}) collective-permute-start(bf16[16,128,128]{2,1,0:T(8,128)(2,1)S(1)} %get-tuple-element.34.strip_b), channel_id=1, source_target_pairs={{1,2},{2,1},{5,6},{6,5},{9,10},{10,9},{13,14},{14,13},{17,18},{18,... | collective-permute-start | bytes 1572872 | tf_op jit(solution)/shard_map/ppermute | solution.py:382
  13.1 21.5 %collective-permute-start.5 = (bf16[2064,128]{1,0:T(8,128)(2,1)S(1)}, bf16[2064,128]{1,0:T(8,128)(2,1)S(1)}, u32[]{:S(2)}, u32[]{:S(2)}) collective-permute-start(bf16[2064,128]{1,0:T(8,128)(2,1)S(1)} %get-tuple-element.42), channel_id=1, source_target_pairs={{4,8},{5,9},{6,10},{7,11},{8,4},{9,5},{10,6},{11,7},{20,24},{21,25... | collective-permute-start | bytes 1585160 | tf_op jit(solution)/shard_map/ppermute | solution.py:379
  15.1 19.6 %collective-permute-start.4 = (bf16[2064,128]{1,0:T(8,128)(2,1)S(1)}, bf16[2064,128]{1,0:T(8,128)(2,1)S(1)}, u32[]{:S(2)}, u32[]{:S(2)}) collective-permute-start(bf16[2064,128]{1,0:T(8,128)(2,1)S(1)} %get-tuple-element.42), channel_id=1, source_target_pairs={{0,4},{1,5},{2,6},{3,7},{4,0},{5,1},{6,2},{7,3},{8,12},{9,13},{10,... | collective-permute-start | bytes 1585160 | tf_op jit(solution)/shard_map/ppermute | solution.py:379
  22.5 3.0 %collective-permute-start.6 = (bf16[8,128,128]{2,1,0:T(8,128)(2,1)S(1)}, bf16[8,128,128]{2,1,0:T(8,128)(2,1)S(1)}, u32[]{:S(2)}, u32[]{:S(2)}) collective-permute-start(bf16[8,128,128]{2,1,0:T(8,128)(2,1)S(1)} %get-tuple-element.44), channel_id=1, source_target_pairs={{0,1},{1,0},{2,3},{3,2},{4,5},{5,4},{6,7},{7,6},{8,9},{9,8},{10,11... | collective-permute-start | bytes 786440 | tf_op jit(solution)/shard_map/ppermute | solution.py:382
  22.6 15.9 %collective-permute-start.9 = (bf16[16,128,128]{2,1,0:T(8,128)(2,1)S(1)}, bf16[16,128,128]{2,1,0:T(8,128)(2,1)S(1)}, u32[]{:S(2)}, u32[]{:S(2)}) collective-permute-start(bf16[16,128,128]{2,1,0:T(8,128)(2,1)S(1)} %get-tuple-element.36.diag_square_t), channel_id=1, source_target_pairs={{0,4},{1,5},{2,6},{3,7},{4,0},{5,1},{6,2},{7,3},{8,12},{9,13},{10,... | collective-permute-start | bytes 1572872 | tf_op jit(solution)/shard_map/ppermute | solution.py:379
  22.6 17.7 %collective-permute-start.8 = (bf16[16,128,128]{2,1,0:T(8,128)(2,1)S(1)}, bf16[16,128,128]{2,1,0:T(8,128)(2,1)S(1)}, u32[]{:S(2)}, u32[]{:S(2)}) collective-permute-start(bf16[16,128,128]{2,1,0:T(8,128)(2,1)S(1)} %get-tuple-element.36.diag_square_t), channel_id=1, source_target_pairs={{4,8},{5,9},{6,10},{7,11},{8,4},{9,5},{10,6},{11,7},{20,24},{21,25... | collective-permute-start | bytes 1572872 | tf_op jit(solution)/shard_map/ppermute | solution.py:379
  25.5 8.0 %collective-permute-start.7 = (bf16[8,128,128]{2,1,0:T(8,128)(2,1)S(1)}, bf16[8,128,128]{2,1,0:T(8,128)(2,1)S(1)}, u32[]{:S(2)}, u32[]{:S(2)}) collective-permute-start(bf16[8,128,128]{2,1,0:T(8,128)(2,1)S(1)} %get-tuple-element.45), channel_id=1, source_target_pairs={{1,2},{2,1},{5,6},{6,5},{9,10},{10,9},{13,14},{14,13},{17,18},{18,... | collective-permute-start | bytes 786440 | tf_op jit(solution)/shard_map/ppermute | solution.py:382
